TPU v7x, 128 devices: a whole 4x4x4 slice. The times are simulated.
128 devices in a mesh: clus: 8 (over x, core), fold: 16 (over y, z).
Axes of the slice: x: 4, y: 4, z: 4, core: 2. Of those that a mesh axis runs over, the one named last changes fastest.
Arguments:
- embeddings: bfloat16 [98304, 1024], P(('clus', 'fold'))
- labels: int32 [98304], P(('clus', 'fold')), may hold values from 0 to 8, as said below
- ordinals: int32 [98304], P(('clus', 'fold')), may hold values from 0 to 12287, as said below
Outputs:
- best_match: float32 [98304], P(('clus', 'fold'))
Inputs may be any that keep to these rules, and one draw needn't show every extreme that they name: `labels`: A label of 8 marks a document outside the scored clusters, whose ordinal is 0; live documents with one label have distinct ordinals. Among the 768 documents of one loader device, at most 3 live ones fall in any aligned run of 384 ordinals of one cluster, and in every cluster one loader device has exactly that many in every such run.
All inputs are finite; a program needn't handle non-finite values.
Results may differ from a plain program's by a relative error of at most 0.0003.
Values may be sent and summed in bfloat16 or wider, within the bound.
No kernel may reach another device: no remote copies, remote signals or barrier semaphores. Data moves between devices by JAX's collectives and lax.ppermute only.
A program may use at most 128 MiB of HBM per device.

v0:
```python
import jax
import jax.numpy as jnp
from jax import lax
from jax.sharding import PartitionSpec as P


def per_device(embeddings, labels, ordinals):
    row_count, emb_width = embeddings.shape
    fold_count = lax.axis_size("fold")
    groups = lax.axis_size("clus")
    devices = fold_count * groups
    slot_count = row_count // devices
    half_rows = row_count // 2
    widened = embeddings.astype(jnp.float32)
    square_sum = jnp.sum(widened * widened, axis=1, keepdims=True) + 1e-06
    unit_rows = (widened * lax.rsqrt(square_sum)).astype(jnp.bfloat16)

    def half_base(owner_fold, which_half):
        return 2 * owner_fold + which_half

    is_live = labels < groups
    owner_fold = ordinals // row_count
    row_index = ordinals % row_count
    destination = jnp.where(is_live, labels * fold_count + owner_fold, devices)
    one_hot = (destination[:, None] == jnp.arange(devices, dtype=jnp.int32)[None, :]).astype(
        jnp.int32
    )
    earlier = jnp.cumsum(one_hot, axis=0) - one_hot
    send_rank = jnp.sum(earlier * one_hot, axis=1)
    send_place = jnp.where(is_live, destination * slot_count + send_rank, devices * slot_count)
    outgoing = (
        jnp.zeros((devices * slot_count, emb_width), jnp.bfloat16)
        .at[send_place]
        .set(unit_rows, mode="drop")
    )
    landing = (
        jnp.full((devices * slot_count,), row_count, jnp.int32)
        .at[send_place]
        .set(row_index, mode="drop")
    )
    arrived, arrived_rows = (
        lax.all_to_all(outgoing, ("clus", "fold"), split_axis=0, concat_axis=0, tiled=True),
        lax.all_to_all(landing, ("clus", "fold"), split_axis=0, concat_axis=0, tiled=True),
    )
    home_block = (
        jnp.zeros((row_count, emb_width), jnp.bfloat16).at[arrived_rows].set(arrived, mode="drop")
    )
    filled = (
        jnp.zeros((row_count,), jnp.bfloat16)
        .at[arrived_rows]
        .set(jnp.ones(arrived_rows.shape, jnp.bfloat16), mode="drop")
    )
    my_fold = lax.axis_index("fold")
    query_bases = (half_base(my_fold, 0), half_base(my_fold, 1))
    queries = (home_block[:half_rows], home_block[half_rows:])
    offsets = jnp.arange(half_rows, dtype=jnp.int32)
    start_best = (
        jnp.full((half_rows,), -1.0, jnp.float32),
        jnp.full((half_rows,), -1.0, jnp.float32),
    )
    best_sims = start_best
    key_table = lax.all_gather(home_block, "fold", axis=0, tiled=True)
    key_marks = lax.all_gather(filled, "fold", axis=0, tiled=True)
    sub_count = key_table.shape[0] // half_rows
    key_sub = key_table.reshape(sub_count, half_rows, emb_width)
    mark_sub = key_marks.reshape(sub_count, half_rows)

    def visit_tile(current_best, item):
        key_rows, key_used, sub_index = item
        first_row = sub_index * half_rows
        key_base = half_base(first_row // row_count, first_row % row_count // half_rows)
        key_pos = key_base * half_rows + offsets
        updated = []
        for which_half in range(2):
            query_rows = queries[which_half]
            query_pos = query_bases[which_half] * half_rows + offsets

            def score_tile(current, query_rows=query_rows, query_pos=query_pos):
                similarity = jnp.einsum(
                    "qe,ke->qk", query_rows, key_rows, preferred_element_type=jnp.float32
                )
                allowed = (key_pos[None, :] < query_pos[:, None]) & (key_used[None, :] > 0)
                return jnp.maximum(current, jnp.max(jnp.where(allowed, similarity, -1.0), axis=1))

            updated.append(
                lax.cond(
                    key_base <= query_bases[which_half],
                    score_tile,
                    lambda current: current,
                    current_best[which_half],
                )
            )
        return ((updated[0], updated[1]), None)

    best_sims, _ = lax.scan(
        visit_tile, best_sims, (key_sub, mark_sub, jnp.arange(sub_count, dtype=jnp.int32))
    )
    lower_best, upper_best = best_sims
    block_best = jnp.concatenate([lower_best, upper_best])
    results = jnp.where(
        arrived_rows < row_count, block_best[jnp.minimum(arrived_rows, row_count - 1)], -1.0
    )
    returned = lax.all_to_all(results, ("clus", "fold"), split_axis=0, concat_axis=0, tiled=True)
    picked = returned[jnp.minimum(send_place, devices * slot_count - 1)]
    return jnp.where(is_live, picked, -1.0)


def solution(mesh):
    return jax.shard_map(
        per_device,
        mesh=mesh,
        in_specs=(P(("clus", "fold"), None), P(("clus", "fold")), P(("clus", "fold"))),
        out_specs=P(("clus", "fold")),
        check_vma=False,
    )
```

profile of v0, /device:TPU:1, one launch (start us, length us, event | category | flops | bytes accessed | tf_op | source)
XLA Modules:
  0.0 388.5 jit_solution(12049898622817698061)
XLA Ops:
  8.1 3.4 scatter_custom_fusion
  12.2 11.5 %all-to-all-start = ((s32[128,6,1]{1,2,0:T(1,128)}), s32[128,6,1]{1,2,0:T(1,128)S(1)}, u32[]{:S(2)}, u32[]{:S(2)}) async-start(s32[128,6,1]{1,2,0:T(1,128)} %bitcast.4), calls=%async_computation | async-start | bytes 131072 | tf_op jit(solution)/shard_map/all_to_all | solution.py:43
  24.1 6.7 %scatter_custom_fusion.1 = bf16[768,1024]{1,0:T(8,128)(2,1)S(1)} fusion(s32[768]{0:T(1024)S(1)} %get-tuple-element.357, bf16[768,1024]{1,0:T(8,128)(2,1)S(1)} %copy-done.1, f32[768]{0:T(1024)S(1)} %add_rsqrt_fusion, bf16[]{:T(256)} %constant.130.clone.1), kind=kCustom, calls=%fused_computation.22 | custom fusion | flops 2359296 | bytes 3149826 | tf_op jit(solution)/shard_map/scatter | solution.py:34
  30.8 1.6 all_to_all.25
  33.3 9.0 %all-to-all-start.1 = ((bf16[128,6,1024]{2,1,0:T(8,128)(2,1)}), bf16[128,6,1024]{2,1,0:T(8,128)(2,1)S(1)}, u32[]{:S(2)}, u32[]{:S(2)}) async-start(bf16[128,6,1024]{2,1,0:T(8,128)(2,1)} %all_to_all.25), calls=%async_computation.1 | async-start | bytes 4194304 | tf_op jit(solution)/shard_map/all_to_all | solution.py:42
  43.8 27.9 %all-to-all-done.1 = bf16[128,6,1024]{2,1,0:T(8,128)(2,1)S(1)} async-done(((bf16[128,6,1024]{2,1,0:T(8,128)(2,1)}), bf16[128,6,1024]{2,1,0:T(8,128)(2,1)S(1)}, u32[]{:S(2)}, u32[]{:S(2)}) %all-to-all-start.1) | async-done | bytes 1572896 | tf_op jit(solution)/shard_map/all_to_all | solution.py:42
  71.7 1.4 reshape.138
  73.2 7.7 %scatter_custom_fusion.2 = bf16[768,1024]{1,0:T(8,128)(2,1)} fusion(s32[768]{0:T(1024)S(1)} %get-tuple-element.327, bf16[768,1024]{1,0:T(8,128)(2,1)} %reshape.138, bf16[]{:T(256)} %constant.130.clone.1), kind=kCustom, calls=%fused_computation.24 | custom fusion | bytes 1573376 | tf_op jit(solution)/shard_map/scatter | solution.py:46
  80.9 8.6 %scatter_custom_fusion.3 = bf16[768]{0:T(1024)(128)(2,1)S(1)} fusion(s32[768]{0:T(1024)S(1)} %get-tuple-element.327, bf16[768]{0:T(1024)(128)(2,1)S(1)} %broadcast.105, bf16[]{:T(256)} %constant.130.clone.1), kind=kCustom, calls=%fused_computation.60 | custom fusion | bytes 1538 | tf_op jit(solution)/shard_map/scatter | solution.py:51
  89.6 19.6 %all-gather = bf16[16,1,768]{2,1,0:T(2,128)(2,1)S(1)} all-gather(bf16[1,1,768]{2,1,0:T(2,128)(2,1)S(1)} %reshape.153), channel_id=1, replica_groups=mesh['clus'=8,'fold'=16] {'fold'}, dimensions={0}, use_global_device_ids=true | all-gather | bytes 26112 | tf_op jit(solution)/shard_map/all_gather | solution.py:63
  109.5 122.8 %all-gather.3.cloned.1.call-done = bf16[12288,1024]{1,0:T(8,128)(2,1)} async-done(((bf16[768,1024]{1,0:T(8,128)(2,1)}), bf16[12288,1024]{1,0:T(8,128)(2,1)}) %all-gather.3.cloned.1.call-update) | async-done | bytes 25165840 | tf_op jit(solution)/shard_map/all_gather | solution.py:62
  232.3 84.7 %while.23 = (s32[]{:T(128)}, f32[384]{0:T(512)S(1)}, f32[384]{0:T(512)S(1)}, s32[32]{0:T(128)S(1)}, s32[]{:T(128)}, /*index=5*/bf16[32,384,1024]{2,1,0:T(8,128)(...) while((s32[]{:T(128)}, f32[384]{0:T(512)S(1)}, ...), condition=%wide.region_15.16_spmd.clone.clone, body=%wide.region_8.15_spmd.clone.clone.sunk | while | flops 605161344 | bytes 4751466 | solution.py:95
  233.6 1.2 dynamic-slice_bitcast_fusion.2
  237.5 1.2 dynamic-slice_bitcast_fusion.2
  240.7 1.2 dynamic-slice_bitcast_fusion.2
  243.3 1.2 dynamic-slice_bitcast_fusion.2
  248.5 1.2 dynamic-slice_bitcast_fusion.2
  253.6 1.2 dynamic-slice_bitcast_fusion.2
  258.8 1.2 dynamic-slice_bitcast_fusion.2
  264.0 1.2 dynamic-slice_bitcast_fusion.2
  269.2 1.2 dynamic-slice_bitcast_fusion.2
  274.3 1.2 dynamic-slice_bitcast_fusion.2
  279.5 1.2 dynamic-slice_bitcast_fusion.2
  282.1 1.2 dynamic-slice_bitcast_fusion.2
  284.7 1.2 dynamic-slice_bitcast_fusion.2
  287.3 1.2 dynamic-slice_bitcast_fusion.2
  289.8 1.2 dynamic-slice_bitcast_fusion.2
  292.4 1.2 dynamic-slice_bitcast_fusion.2
  317.0 3.2 gather_fusion
  321.0 45.9 %all-to-all-start.2 = ((f32[128,6,1]{1,2,0:T(1,128)}), f32[128,6,1]{1,2,0:T(1,128)S(1)}, u32[]{:S(2)}, u32[]{:S(2)}) async-start(f32[128,6,1]{1,2,0:T(1,128)} %bitcast.7), calls=%async_computation.2 | async-start | bytes 131072 | tf_op jit(solution)/shard_map/all_to_all | solution.py:103
  366.9 9.6 %all-to-all-done.2 = f32[128,6,1]{1,2,0:T(1,128)S(1)} async-done(((f32[128,6,1]{1,2,0:T(1,128)}), f32[128,6,1]{1,2,0:T(1,128)S(1)}, u32[]{:S(2)}, u32[]{:S(2)}) %all-to-all-start.2) | async-done | bytes 3104 | tf_op jit(solution)/shard_map/all_to_all | solution.py:103
  377.9 3.2 gather_fusion.1
  (260 shorter events, 52.0 us)
Async XLA Ops:
  7.4 16.3 %copy-start.1 = (bf16[768,1024]{1,0:T(8,128)(2,1)S(1)}, bf16[768,1024]{1,0:T(8,128)(2,1)}, u32[]{:S(2)}) copy-start(bf16[768,1024]{1,0:T(8,128)(2,1)} %param.9) | copy-start | bytes 4718596
  12.2 21.1 %all-to-all-start = ((s32[128,6,1]{1,2,0:T(1,128)}), s32[128,6,1]{1,2,0:T(1,128)S(1)}, u32[]{:S(2)}, u32[]{:S(2)}) async-start(s32[128,6,1]{1,2,0:T(1,128)} %bitcast.4), calls=%async_computation | async-start | bytes 131072 | tf_op jit(solution)/shard_map/all_to_all | solution.py:43
  33.3 38.5 %all-to-all-start.1 = ((bf16[128,6,1024]{2,1,0:T(8,128)(2,1)}), bf16[128,6,1024]{2,1,0:T(8,128)(2,1)S(1)}, u32[]{:S(2)}, u32[]{:S(2)}) async-start(bf16[128,6,1024]{2,1,0:T(8,128)(2,1)} %all_to_all.25), calls=%async_computation.1 | async-start | bytes 4194304 | tf_op jit(solution)/shard_map/all_to_all | solution.py:42
  42.2 190.1 %all-gather.3.cloned.1.call-start = ((), (), s32[]{:S(2)}) async-start(), calls=%async_computation.3 | async-start | bytes 26738688 | tf_op jit(solution)/shard_map/all_gather | solution.py:62
  80.9 28.5 %copy-start = (bf16[768,1024]{1,0:T(8,128)(2,1)S(1)}, bf16[768,1024]{1,0:T(8,128)(2,1)}, u32[]{:S(2)}) copy-start(bf16[768,1024]{1,0:T(8,128)(2,1)} %scatter_custom_fusion.2) | copy-start | bytes 4718596
  321.0 55.5 %all-to-all-start.2 = ((f32[128,6,1]{1,2,0:T(1,128)}), f32[128,6,1]{1,2,0:T(1,128)S(1)}, u32[]{:S(2)}, u32[]{:S(2)}) async-start(f32[128,6,1]{1,2,0:T(1,128)} %bitcast.7), calls=%async_computation.2 | async-start | bytes 131072 | tf_op jit(solution)/shard_map/all_to_all | solution.py:103
Sparse Core Ops, SparseCore 0:
  81.0 151.2 all-gather.2
where the time goes:
time: 391 us; the launch traced here: 389 us
  waiting for transfers between devices  161 us (41%)
  local copies, waits for them, and re-layouts  89.9 us (23%)
  starting transfers between devices  66.4 us (17%)
  loops' own time  24.4 us (6%)
  blocking collectives  19.6 us (5%)
  between operations  13.6 us (3%)
  other arithmetic  11.6 us (3%)
    all_gather x1, waiting for transfers between devices, per_device(): key_table = lax.all_gather(home_block, 'fold', axis=0, tiled=True)  123 us
    all_to_all x1, starting transfers between devices, per_device(): lax.all_to_all(results, ('clus', 'fold'), split_axis=0, concat_axis=0, ti...  45.9 us
    squeeze x32, local copies, waits for them, and re-layouts, per_device(): lax.scan(visit_tile, best_sims, (key_sub, mark_sub, jnp.arange(sub_count,...  38.1 us
    all_to_all x1, waiting for transfers between devices, per_device(): lax.all_to_all(outgoing, ('clus', 'fold'), split_axis=0, concat_axis=0, t...  27.9 us
    another operation x1, loops' own time, per_device(): lax.scan(visit_tile, best_sims, (key_sub, mark_sub, jnp.arange(sub_count,...  23.6 us
    dynamic_slice x64, local copies, waits for them, and re-layouts, per_device(): lax.scan(visit_tile, best_sims, (key_sub, mark_sub, jnp.arange(sub_count,...  20 us
    all_gather x1, blocking collectives, per_device(): key_marks = lax.all_gather(filled, 'fold', axis=0, tiled=True)  19.6 us
    all_to_all x1, starting transfers between devices, per_device(): lax.all_to_all(landing, ('clus', 'fold'), split_axis=0, concat_axis=0, ti...  11.5 us
  transfers between devices with their start and end apart: 4, of which 4 were waited for; matrix products, arithmetic and copies ran while one was open for 4% of the time, Pallas kernels for 0%

commit v1 on v0

v1 whole, which is shorter than its diff:
```python
import functools

import jax
import jax.numpy as jnp
from jax import lax
from jax.experimental import pallas as pl
from jax.experimental.pallas import tpu as pltpu
from jax.sharding import PartitionSpec as P

AXES = ("clus", "fold")
RING = 4
EMB = 1024
ROWS = 768
PIECES = 8
PIECE = 96
PIECE_ROWS = 112
BLOCK_ROWS = 784
HALF = 384
LANES = 128
LO = 128
FAR = 1.0e6
TILE = 256
VMEM = 48 * 1024 * 1024


def place(x, core, y, z):
    return (x % RING * 2 + core) * 16 + y % RING * 4 + z % RING


def every_device():
    for x in range(RING):
        for core in range(2):
            for y in range(RING):
                for z in range(RING):
                    yield x, core, y, z


def packet_pairs(piece):
    offset, cross = divmod(piece, 2)
    pairs = []
    for x, core, y, z in every_device():
        kind = core ^ cross
        target = place(x + offset, 0, y, z) if kind == 0 else place(x, 1, y + offset, z)
        pairs.append((place(x, core, y, z), target))
    return pairs


def block_pairs(du, dv):
    pairs = []
    for x, core, y, z in every_device():
        source = place(x, 0, y + du, z + dv) if core == 0 else place(x + du, 1, y, z - dv)
        pairs.append((source, place(x, core, y, z)))
    return pairs


def turned(pairs):
    return [(b, a) for a, b in pairs]


def whole(count):
    return [pl.BlockSpec(memory_space=pltpu.VMEM)] * count


def pack_kernel(emb_ref, labels_ref, ordinals_ref, slot_ref, *piece_refs):
    clus, fold = lax.axis_index("clus"), lax.axis_index("fold")
    core, x, y = clus % 2, clus // 2, fold // RING
    labels, ordinals = labels_ref[...], ordinals_ref[...]
    kind = labels // RING
    coordinate = jnp.where(kind == 0, x, y)
    offset = (labels % RING - coordinate + RING) % RING
    piece = 2 * offset + jnp.where(kind == core, 0, 1)
    live = labels < PIECES
    ids = lax.broadcasted_iota(jnp.int32, (16, ROWS), 0)
    member = (ids == piece) & live
    before = lax.broadcasted_iota(jnp.int32, (ROWS, ROWS), 0) < lax.broadcasted_iota(
        jnp.int32, (ROWS, ROWS), 1
    )
    counts = jnp.dot(
        jnp.where(member, 1.0, 0.0).astype(jnp.bfloat16),
        jnp.where(before, 1.0, 0.0).astype(jnp.bfloat16),
        preferred_element_type=jnp.float32,
    )
    rank = jnp.sum(jnp.where(member, counts, 0.0), axis=0, keepdims=True).astype(jnp.int32)
    slot = jnp.where(live, piece * PIECE + rank, -1)
    slot_ref[...] = slot
    chosen = lax.broadcasted_iota(jnp.int32, (ROWS, ROWS), 0) == slot
    pick = jnp.where(chosen, 1.0, 0.0).astype(jnp.bfloat16)
    high, low = ordinals // LO + 1, ordinals % LO
    row_id = lax.broadcasted_iota(jnp.int32, (16, ROWS), 0)
    codes = jnp.where(row_id == 0, high, jnp.where(row_id == 1, low, 0)).astype(jnp.float32)
    packed_codes = lax.dot_general(
        codes.astype(jnp.bfloat16),
        pick,
        (((1,), (1,)), ((), ())),
        preferred_element_type=jnp.float32,
    )
    widened = emb_ref[...].astype(jnp.float32)
    square_sum = jnp.sum(widened * widened, axis=1, keepdims=True) + 1e-6
    unit_rows = (widened * lax.rsqrt(square_sum)).astype(jnp.bfloat16)
    lane_piece = lax.broadcasted_iota(jnp.int32, (16, ROWS), 1) // PIECE
    for s in range(PIECES):
        packed = jnp.dot(
            pick[s * PIECE : (s + 1) * PIECE], unit_rows, preferred_element_type=jnp.float32
        )
        piece_refs[s][:PIECE, :] = packed.astype(jnp.bfloat16)
        mine = jnp.where(lane_piece == s, packed_codes, 0.0).astype(jnp.bfloat16)
        piece_refs[s][PIECE:, :ROWS] = mine
        piece_refs[s][PIECE:, ROWS:] = jnp.zeros((16, EMB - ROWS), jnp.bfloat16)


def join_kernel(*refs):
    piece_refs, block_ref = refs[:PIECES], refs[PIECES]
    codes = jnp.zeros((16, EMB), jnp.float32)
    for s in range(PIECES):
        block_ref[s * PIECE : (s + 1) * PIECE, :] = piece_refs[s][:PIECE, :]
        codes = codes + piece_refs[s][PIECE:, :].astype(jnp.float32)
    block_ref[ROWS:, :] = codes.astype(jnp.bfloat16)


def meet_kernel(count, steps, has_before, *refs):
    blocks, refs = refs[:count], refs[count:]
    if has_before:
        before_ref, refs = refs[0], refs[1:]
    out_ref, rows_best, lanes_best, column_ord = refs
    clus, fold = lax.axis_index("clus"), lax.axis_index("fold")
    core, x, y, z = clus % 2, clus // 2, fold // RING, fold % RING
    role = {"u": jnp.where(core == 0, y, x) // 2, "v": z // 2}
    row_ord = []
    for b in range(count):
        codes = blocks[b][ROWS:, :ROWS].astype(jnp.float32)
        high, low = codes[0:1], codes[1:2]
        line = jnp.where(high == 0.0, FAR, (high - 1.0) * LO + low)
        row_ord.append(line)
        column_ord[b] = jnp.transpose(jnp.broadcast_to(line, (LANES, ROWS)))
    rows_best[...] = jnp.full_like(rows_best, -1.0)
    lanes_best[...] = jnp.full_like(lanes_best, -1.0)
    lane_ord = out_ref

    for b in range(count):
        lane_ord[b] = jnp.broadcast_to(row_ord[b], (8, ROWS))

    def tile(a, b, a_start, b_start, a_size, b_size, both):
        a_rows, b_rows = pl.ds(a_start, a_size), pl.ds(b_start, b_size)
        scores = lax.dot_general(
            blocks[a][a_rows, :],
            blocks[b][b_rows, :],
            (((1,), (1,)), ((), ())),
            preferred_element_type=jnp.float32,
        )
        mine = column_ord[a, a_rows, :]
        theirs = lane_ord[b, 0:1, b_rows]
        best = rows_best[a, a_rows, :]
        for k in range(b_size // LANES):
            cut = slice(k * LANES, (k + 1) * LANES)
            part = scores[:, cut]
            earlier = theirs[:, cut] < mine
            best = jnp.maximum(best, jnp.where(earlier, part, -1.0))
            if both:
                later = jnp.where(earlier, -1.0, part)
                later = jnp.max(later.reshape(a_size // 8, 8, LANES), axis=0)
                if isinstance(b_start, int):
                    lanes = pl.ds(b_start + k * LANES, LANES)
                else:
                    lanes = pl.ds(pl.multiple_of(b_start + k * LANES, LANES), LANES)
                lanes_best[b, :, lanes] = jnp.maximum(lanes_best[b, :, lanes], later)
        rows_best[a, a_rows, :] = best

    for a, b, kind in steps:
        if kind in ("u", "v"):
            start = pl.multiple_of(role[kind] * HALF, HALF)
            tile(a, b, 0, HALF, HALF, HALF, True)
            tile(a, b, start, start, HALF, HALF, True)
        else:
            for i in range(0, ROWS, TILE):
                tile(a, b, i, 0, TILE, ROWS, kind is None)
    for b in range(count):
        across = jnp.transpose(rows_best[b])
        best = jnp.maximum(
            jnp.max(across, axis=0, keepdims=True),
            jnp.max(lanes_best[b], axis=0, keepdims=True),
        )
        best = jnp.broadcast_to(best, (8, ROWS))
        if has_before:
            best = jnp.maximum(best, before_ref[b])
        out_ref[b] = best


def meet(blocks, steps, before):
    count = len(blocks)
    products = sum(0.5 if kind in ("u", "v") else 1.0 for _, _, kind in steps)
    given = list(blocks) + ([] if before is None else [before])
    return pl.pallas_call(
        functools.partial(meet_kernel, count, steps, before is not None),
        out_shape=jax.ShapeDtypeStruct((count, 8, ROWS), jnp.float32),
        in_specs=whole(len(given)),
        out_specs=whole(1)[0],
        scratch_shapes=[
            pltpu.VMEM((count, ROWS, LANES), jnp.float32),
            pltpu.VMEM((count, 8, ROWS), jnp.float32),
            pltpu.VMEM((count, ROWS, LANES), jnp.float32),
        ],
        compiler_params=pltpu.CompilerParams(vmem_limit_bytes=VMEM),
        cost_estimate=pl.CostEstimate(
            flops=int(2 * products * ROWS * ROWS * EMB),
            bytes_accessed=count * BLOCK_ROWS * EMB * 2,
            transcendentals=0,
        ),
    )(*given)


def best_kernel(*refs):
    out_ref = refs[-1]
    best = refs[0][...]
    for ref in refs[1:-1]:
        best = jnp.maximum(best, ref[...])
    out_ref[...] = best


def unpack_kernel(slot_ref, *refs):
    rows, out_ref = refs[:PIECES], refs[PIECES]
    lane_piece = lax.broadcasted_iota(jnp.int32, (8, ROWS), 1) // PIECE
    line = rows[0][...]
    for s in range(1, PIECES):
        line = jnp.where(lane_piece == s, rows[s][...], line)
    column = jnp.transpose(jnp.broadcast_to(line[0:1], (LANES, ROWS)))
    slot = slot_ref[...]
    best = []
    for k in range(ROWS // LANES):
        cut = slice(k * LANES, (k + 1) * LANES)
        chosen = lax.broadcasted_iota(jnp.int32, (ROWS, LANES), 0) == slot[:, cut]
        best.append(jnp.sum(jnp.where(chosen, column, 0.0), axis=0, keepdims=True))
    found = jnp.concatenate(best, axis=1)
    out_ref[...] = jnp.where(slot >= 0, found, -1.0)


def per_device(embeddings, labels, ordinals):
    send = functools.partial(lax.ppermute, axis_name=AXES)
    slot, *pieces = pl.pallas_call(
        pack_kernel,
        out_shape=[jax.ShapeDtypeStruct((1, ROWS), jnp.int32)]
        + [jax.ShapeDtypeStruct((PIECE_ROWS, EMB), jnp.bfloat16)] * PIECES,
        in_specs=whole(3),
        out_specs=whole(1 + PIECES),
        compiler_params=pltpu.CompilerParams(vmem_limit_bytes=VMEM),
    )(embeddings, labels.reshape(1, ROWS), ordinals.reshape(1, ROWS))
    landed = [pieces[0]] + [send(pieces[s], perm=packet_pairs(s)) for s in range(1, PIECES)]
    own = pl.pallas_call(
        join_kernel,
        out_shape=jax.ShapeDtypeStruct((BLOCK_ROWS, EMB), jnp.bfloat16),
        in_specs=whole(PIECES),
        out_specs=whole(1)[0],
        compiler_params=pltpu.CompilerParams(vmem_limit_bytes=VMEM),
    )(*landed)
    up = send(own, perm=block_pairs(0, 1))
    right = send(own, perm=block_pairs(1, 0))
    left = send(own, perm=block_pairs(3, 0))
    across = send(own, perm=block_pairs(2, 0))
    up_two = send(up, perm=block_pairs(0, 1))
    first = meet([own], [(0, 0, "own")], None)
    second = meet([own, up], [(0, 1, None)], None)
    third = meet(
        [own, up, right, left],
        [(0, 2, None), (2, 3, "u"), (1, 2, None), (1, 3, None)],
        None,
    )
    fourth = meet(
        [own, up, left, across, up_two],
        [(3, 1, None), (4, 2, None), (0, 4, "v"), (3, 4, "u")],
        None,
    )
    best_own = [first[0], second[0], third[0], fourth[0]]
    back = [
        (jnp.maximum(jnp.maximum(second[1], third[1]), fourth[1]), (0, 1)),
        (third[2], (1, 0)),
        (jnp.maximum(third[3], fourth[2]), (3, 0)),
        (fourth[3], (2, 0)),
        (fourth[4], (0, 2)),
    ]
    for part, (du, dv) in back:
        best_own.append(send(part, perm=turned(block_pairs(du, dv))))
    result = best_own[0]
    for part in best_own[1:]:
        result = jnp.maximum(result, part)
    rows = [result] + [send(result, perm=turned(packet_pairs(s))) for s in range(1, PIECES)]
    scored = pl.pallas_call(
        unpack_kernel,
        out_shape=jax.ShapeDtypeStruct((1, ROWS), jnp.float32),
        in_specs=whole(1 + PIECES),
        out_specs=whole(1)[0],
        compiler_params=pltpu.CompilerParams(vmem_limit_bytes=VMEM),
    )(slot, *rows)
    return scored.reshape(ROWS)


def solution(mesh):
    return jax.shard_map(
        per_device,
        mesh=mesh,
        in_specs=(P(AXES, None), P(AXES), P(AXES)),
        out_specs=P(AXES),
        check_vma=False,
    )
```

time: 391 us -> 109 us (0.28)
  waiting for transfers between devices: 161 us -> 45.4 us
  local copies, waits for them, and re-layouts: 89.9 us -> 6.51 us
  starting transfers between devices: 66.4 us -> 35.3 us
  loops' own time: 24.4 us -> 0 us
  Pallas kernels: 0 us -> 20.4 us
  blocking collectives: 19.6 us -> 0 us
  between operations: 13.6 us -> 0.15 us
  other arithmetic: 11.6 us -> 0.64 us
    all_gather x1 -> x0, waiting for transfers between devices: 123 us -> none  [per_device(): key_table = lax.all_gather(home_block, 'fold', axis=0, tiled=True)]
    all_to_all x3 -> x0, starting transfers between devices: 66.3 us -> none  [the longest x1 45.9 us: per_device(): lax.all_to_all(results, ('clus', 'fold'), split_axis=0, concat_axis=0, ti...]
    ppermute x0 -> x24, waiting for transfers between devices: none -> 45.4 us  [the longest x1 17.7 us: per_device(): up = send(own, perm=block_pairs(0, 1))]
    all_to_all x3 -> x0, waiting for transfers between devices: 38.3 us -> none  [the longest x1 27.9 us: per_device(): lax.all_to_all(outgoing, ('clus', 'fold'), split_axis=0, concat_axis=0, t...]
    squeeze x32 -> x0, local copies, waits for them, and re-layouts: 38.1 us -> none  [per_device(): lax.scan(visit_tile, best_sims, (key_sub, mark_sub, jnp.arange(sub_count,...]
    ppermute x0 -> x24, starting transfers between devices: none -> 35.3 us  [the longest x7 12.4 us: per_device(): send(pieces[s], perm=packet_pairs(s))]
    another operation x65 -> x0, loops' own time: 24.4 us -> none  [the longest x1 23.6 us: per_device(): lax.scan(visit_tile, best_sims, (key_sub, mark_sub, jnp.arange(sub_count,...]
    pallas_call x0 -> x7, Pallas kernels: none -> 20.4 us  [the longest x4 16.9 us: meet(): pl.pallas_call(functools.partial(meet_kernel, count, steps, before is not...]
  transfers between devices with their start and end apart: 4 -> 24, of which waited for: 4 -> 10; matrix products, arithmetic and copies ran while one was open for 4% -> 0% of each run, Pallas kernels for 0% -> 9%
where the time goes in v1:
time: 109 us; the launch traced here: 108 us
  waiting for transfers between devices  45.4 us (42%)
  starting transfers between devices  35.3 us (32%)
  Pallas kernels  20.4 us (19%)
  local copies, waits for them, and re-layouts  6.51 us (6%)
    ppermute x1, waiting for transfers between devices, per_device(): up = send(own, perm=block_pairs(0, 1))  17.7 us
    pallas_call x4, Pallas kernels, meet(): pl.pallas_call(functools.partial(meet_kernel, count, steps, before is not...  16.9 us
    ppermute x1, waiting for transfers between devices, per_device(): right = send(own, perm=block_pairs(1, 0))  15.3 us
    ppermute x7, starting transfers between devices, per_device(): send(pieces[s], perm=packet_pairs(s))  12.4 us
    ppermute x7, starting transfers between devices, per_device(): send(result, perm=turned(packet_pairs(s)))  10.5 us
    ppermute x5, starting transfers between devices, per_device(): best_own.append(send(part, perm=turned(block_pairs(du, dv))))  7.81 us
    ppermute x7, waiting for transfers between devices, per_device(): send(pieces[s], perm=packet_pairs(s))  6.28 us
    unnamed x10, local copies, waits for them, and re-layouts  5.13 us
  transfers between devices with their start and end apart: 24, of which 10 were waited for; matrix products, arithmetic and copies ran while one was open for 0% of the time, Pallas kernels for 9%

profile of v1, /device:TPU:1, one launch (start us, length us, event | category | flops | bytes accessed | tf_op | source)
XLA Modules:
  0.0 108.4 jit_solution(8523319307586711530)
XLA Ops:
  1.4 1.4 %copy-done = bf16[768,1024]{1,0:T(8,128)(2,1)S(1)} copy-done((bf16[768,1024]{1,0:T(8,128)(2,1)S(1)}, bf16[768,1024]{1,0:T(8,128)(2,1)}, u32[]{:S(2)}) %copy-start) | copy-done | bytes 1572888
  2.8 2.9 %shard_map.37 = (s32[1,768]{1,0:T(1,128)S(1)}, bf16[112,1024]{1,0:T(8,128)(2,1)S(1)}, bf16[112,1024]{1,0:T(8,128)(2,1)S(1)}, bf16[112,1024]{1,0:T(8,128)(2,1)S(1...) custom-call(bf16[768,1024]{1,0:T(8,128)(2,1)S(1)} %copy-done, ...), custom_call_target="tpu_custom_call" | custom-call | tf_op jit(solution)/shard_map/pallas_call | solution.py:238
  5.7 1.5 %collective-permute-start = (bf16[112,1024]{1,0:T(8,128)(2,1)S(1)}, bf16[112,1024]{1,0:T(8,128)(2,1)S(1)}, u32[]{:S(2)}, u32[]{:S(2)}) collective-permute-start(bf16[112,1024]{1,0:T(8,128)(2,1)S(1)} %get-tuple-element.16), channel_id=1, source_target_pairs={{0,16},{1,17},{2,18},{3,19},{4,20},{5,21},{6,22},{7,23},{8,24},{9,... | collective-permute-start | bytes 688136 | tf_op jit(solution)/shard_map/ppermute | solution.py:246
  7.2 1.4 %collective-permute-start.1 = (bf16[112,1024]{1,0:T(8,128)(2,1)S(1)}, bf16[112,1024]{1,0:T(8,128)(2,1)S(1)}, u32[]{:S(2)}, u32[]{:S(2)}) collective-permute-start(bf16[112,1024]{1,0:T(8,128)(2,1)S(1)} %get-tuple-element.17), channel_id=1, source_target_pairs={{0,32},{1,33},{2,34},{3,35},{4,36},{5,37},{6,38},{7,39},{8,40},{9,... | collective-permute-start | bytes 688136 | tf_op jit(solution)/shard_map/ppermute | solution.py:246
  8.6 1.4 %collective-permute-start.2 = (bf16[112,1024]{1,0:T(8,128)(2,1)S(1)}, bf16[112,1024]{1,0:T(8,128)(2,1)S(1)}, u32[]{:S(2)}, u32[]{:S(2)}) collective-permute-start(bf16[112,1024]{1,0:T(8,128)(2,1)S(1)} %get-tuple-element.18), channel_id=1, source_target_pairs={{0,20},{1,21},{2,22},{3,23},{4,24},{5,25},{6,26},{7,27},{8,28},{9,... | collective-permute-start | bytes 688136 | tf_op jit(solution)/shard_map/ppermute | solution.py:246
  9.9 2.9 %collective-permute-start.3 = (bf16[112,1024]{1,0:T(8,128)(2,1)S(1)}, bf16[112,1024]{1,0:T(8,128)(2,1)S(1)}, u32[]{:S(2)}, u32[]{:S(2)}) collective-permute-start(bf16[112,1024]{1,0:T(8,128)(2,1)S(1)} %get-tuple-element.19), channel_id=1, source_target_pairs={{0,64},{1,65},{2,66},{3,67},{4,68},{5,69},{6,70},{7,71},{8,72},{9,... | collective-permute-start | bytes 688136 | tf_op jit(solution)/shard_map/ppermute | solution.py:246
  13.4 1.4 %collective-permute-start.5 = (bf16[112,1024]{1,0:T(8,128)(2,1)S(1)}, bf16[112,1024]{1,0:T(8,128)(2,1)S(1)}, u32[]{:S(2)}, u32[]{:S(2)}) collective-permute-start(bf16[112,1024]{1,0:T(8,128)(2,1)S(1)} %get-tuple-element.21), channel_id=1, source_target_pairs={{0,96},{1,97},{2,98},{3,99},{4,100},{5,101},{6,102},{7,103},{8,104... | collective-permute-start | bytes 688136 | tf_op jit(solution)/shard_map/ppermute | solution.py:246
  14.8 3.3 %collective-permute-start.6 = (bf16[112,1024]{1,0:T(8,128)(2,1)S(1)}, bf16[112,1024]{1,0:T(8,128)(2,1)S(1)}, u32[]{:S(2)}, u32[]{:S(2)}) collective-permute-start(bf16[112,1024]{1,0:T(8,128)(2,1)S(1)} %get-tuple-element.22), channel_id=1, source_target_pairs={{0,28},{1,29},{2,30},{3,31},{4,16},{5,17},{6,18},{7,19},{8,20},{9,... | collective-permute-start | bytes 688136 | tf_op jit(solution)/shard_map/ppermute | solution.py:246
  18.1 3.5 %collective-permute-done.3.refs_4_ = bf16[112,1024]{1,0:T(8,128)(2,1)S(1)} collective-permute-done((bf16[112,1024]{1,0:T(8,128)(2,1)S(1)}, bf16[112,1024]{1,0:T(8,128)(2,1)S(1)}, u32[]{:S(2)}, u32[]{:S(2)}) %collective-permute-start.3) | collective-permute-done | bytes 229408 | tf_op jit(solution)/shard_map/ppermute | solution.py:246
  22.7 1.6 %collective-permute-done.6.refs_7_ = bf16[112,1024]{1,0:T(8,128)(2,1)S(1)} collective-permute-done((bf16[112,1024]{1,0:T(8,128)(2,1)S(1)}, bf16[112,1024]{1,0:T(8,128)(2,1)S(1)}, u32[]{:S(2)}, u32[]{:S(2)}) %collective-permute-start.6) | collective-permute-done | bytes 229408 | tf_op jit(solution)/shard_map/ppermute | solution.py:246
  24.5 1.7 %collective-permute-start.7 = (bf16[784,1024]{1,0:T(8,128)(2,1)S(1)}, bf16[784,1024]{1,0:T(8,128)(2,1)S(1)}, u32[]{:S(2)}, u32[]{:S(2)}) collective-permute-start(bf16[784,1024]{1,0:T(8,128)(2,1)S(1)} %shard_map.38.refs_0_), channel_id=1, source_target_pairs={{1,0},{2,1},{3,2},{0,3},{5,4},{6,5},{7,6},{4,7},{9,8},{10,9},{11,1... | collective-permute-start | bytes 4816904 | tf_op jit(solution)/shard_map/ppermute | solution.py:254
  26.2 0.9 collective-permute-start.9
  27.1 1.8 %collective-permute-start.8 = (bf16[784,1024]{1,0:T(8,128)(2,1)S(1)}, bf16[784,1024]{1,0:T(8,128)(2,1)S(1)}, u32[]{:S(2)}, u32[]{:S(2)}) collective-permute-start(bf16[784,1024]{1,0:T(8,128)(2,1)S(1)} %shard_map.38.refs_0_), channel_id=1, source_target_pairs={{4,0},{5,1},{6,2},{7,3},{8,4},{9,5},{10,6},{11,7},{12,8},{13,9},{1... | collective-permute-start | bytes 4816904 | tf_op jit(solution)/shard_map/ppermute | solution.py:255
  29.1 17.7 %collective-permute-done.7.refs_1_ = bf16[784,1024]{1,0:T(8,128)(2,1)S(1)} collective-permute-done((bf16[784,1024]{1,0:T(8,128)(2,1)S(1)}, bf16[784,1024]{1,0:T(8,128)(2,1)S(1)}, u32[]{:S(2)}, u32[]{:S(2)}) %collective-permute-start.7) | collective-permute-done | bytes 1605664 | tf_op jit(solution)/shard_map/ppermute | solution.py:254
  46.8 1.7 %shard_map.40 = f32[2,8,768]{2,1,0:T(8,128)S(1)} custom-call(bf16[784,1024]{1,0:T(8,128)(2,1)S(1)} %shard_map.38.refs_0_, bf16[784,1024]{1,0:T(8,128)(2,1)S(1)} %collective-permute-done.7.refs_1_), custom_call_target="tpu_custom_call" | custom-call | flops 1207959552 | bytes 3211264 | tf_op jit(solution)/shard_map/pallas_call | solution.py:192
  48.5 15.3 %collective-permute-done.8.refs_2_ = bf16[784,1024]{1,0:T(8,128)(2,1)S(1)} collective-permute-done((bf16[784,1024]{1,0:T(8,128)(2,1)S(1)}, bf16[784,1024]{1,0:T(8,128)(2,1)S(1)}, u32[]{:S(2)}, u32[]{:S(2)}) %collective-permute-start.8) | collective-permute-done | bytes 1605664 | tf_op jit(solution)/shard_map/ppermute | solution.py:255
  63.8 6.6 %shard_map.41 = f32[4,8,768]{2,1,0:T(8,128)S(1)} custom-call(bf16[784,1024]{1,0:T(8,128)(2,1)S(1)} %shard_map.38.refs_0_, bf16[784,1024]{1,0:T(8,128)(2,1)S(1)} %collective-permute-done.7.refs_1_, bf16[784,1024]{1,0:T(8,128)(2,1)S(1)} %collective-permute-done.8.refs_2_, bf16[784,1024]{1,0:T(8,128)(2,1)} %copy-done.1), custom_call_target="tpu_custom_call" | custom-call | flops 4227858432 | bytes 6422528 | tf_op jit(solution)/shard_map/pallas_call | solution.py:192
  70.4 1.1 %copy-done.3 = bf16[784,1024]{1,0:T(8,128)(2,1)} copy-done((bf16[784,1024]{1,0:T(8,128)(2,1)}, bf16[784,1024]{1,0:T(8,128)(2,1)S(1)}, u32[]{:S(2)}) %copy-start.3) | copy-done | bytes 1605656
  71.5 1.2 %copy-done.4 = bf16[784,1024]{1,0:T(8,128)(2,1)} copy-done((bf16[784,1024]{1,0:T(8,128)(2,1)}, bf16[784,1024]{1,0:T(8,128)(2,1)S(1)}, u32[]{:S(2)}) %copy-start.4) | copy-done | bytes 1605656
  72.7 1.4 %copy-done.2 = bf16[784,1024]{1,0:T(8,128)(2,1)S(1)} copy-done((bf16[784,1024]{1,0:T(8,128)(2,1)S(1)}, bf16[784,1024]{1,0:T(8,128)(2,1)}, u32[]{:S(2)}) %copy-start.2) | copy-done | bytes 1605656
  74.1 7.1 %shard_map.42 = f32[5,8,768]{2,1,0:T(8,128)S(1)} custom-call(bf16[784,1024]{1,0:T(8,128)(2,1)S(1)} %shard_map.38.refs_0_, bf16[784,1024]{1,0:T(8,128)(2,1)S(1)} %collective-permute-done.7.refs_1_, bf16[784,1024]{1,0:T(8,128)(2,1)S(1)} %copy-done.2, bf16[784,1024]{1,0:T(8,128)(2,1)} %copy-done.3, bf16[784,1024]{1,0:T(8,128)(2,1)} %copy-done.4), custom_call_target="tpu_custom_call" | custom-call | flops 3623878656 | bytes 8028160 | tf_op jit(solution)/shard_map/pallas_call | solution.py:192
  81.3 3.4 %collective-permute-start.16 = (f32[8,768]{1,0:T(8,128)S(1)}, f32[8,768]{1,0:T(8,128)S(1)}, u32[]{:S(2)}, u32[]{:S(2)}) collective-permute-start(f32[8,768]{1,0:T(8,128)S(1)} %get-tuple-element.25), channel_id=1, source_target_pairs={{0,2},{1,3},{2,0},{3,1},{4,6},{5,7},{6,4},{7,5},{8,10},{9,11},{10,... | collective-permute-start | bytes 73736 | tf_op jit(solution)/shard_map/ppermute | solution.py:280
  84.7 3.3 %collective-permute-start.14 = (f32[8,768]{1,0:T(8,128)S(1)}, f32[8,768]{1,0:T(8,128)S(1)}, u32[]{:S(2)}, u32[]{:S(2)}) collective-permute-start(f32[8,768]{1,0:T(8,128)S(1)} %get-tuple-element.24), channel_id=1, source_target_pairs={{0,12},{1,13},{2,14},{3,15},{4,0},{5,1},{6,2},{7,3},{8,4},{9,5},{1... | collective-permute-start | bytes 73736 | tf_op jit(solution)/shard_map/ppermute | solution.py:280
  89.1 1.5 %shard_map.39 = f32[1,8,768]{2,1,0:T(8,128)S(1)} custom-call(bf16[784,1024]{1,0:T(8,128)(2,1)S(1)} %shard_map.38.refs_0_), custom_call_target="tpu_custom_call" | custom-call | flops 1207959552 | bytes 1605632 | tf_op jit(solution)/shard_map/pallas_call | solution.py:192
  90.6 1.5 %collective-permute-done.13 = f32[8,768]{1,0:T(8,128)S(1)} collective-permute-done((f32[8,768]{1,0:T(8,128)S(1)}, f32[8,768]{1,0:T(8,128)S(1)}, u32[]{:S(2)}, u32[]{:S(2)}) %collective-permute-start.13) | collective-permute-done | bytes 24608 | tf_op jit(solution)/shard_map/ppermute | solution.py:280
  92.1 3.5 %collective-permute-start.17 = (f32[8,768]{1,0:T(8,128)S(1)}, f32[8,768]{1,0:T(8,128)S(1)}, u32[]{:S(2)}, u32[]{:S(2)}) collective-permute-start(f32[8,768]{1,0:T(8,128)S(1)} %fusion.7.refs_0_), channel_id=1, source_target_pairs={{16,0},{17,1},{18,2},{19,3},{20,4},{21,5},{22,6},{23,7},{24,8},{25... | collective-permute-start | bytes 73736 | tf_op jit(solution)/shard_map/ppermute | solution.py:284
  95.6 2.2 %collective-permute-start.18 = (f32[8,768]{1,0:T(8,128)S(1)}, f32[8,768]{1,0:T(8,128)S(1)}, u32[]{:S(2)}, u32[]{:S(2)}) collective-permute-start(f32[8,768]{1,0:T(8,128)S(1)} %fusion.7.refs_0_), channel_id=1, source_target_pairs={{32,0},{33,1},{34,2},{35,3},{36,4},{37,5},{38,6},{39,7},{40,8},{41... | collective-permute-start | bytes 73736 | tf_op jit(solution)/shard_map/ppermute | solution.py:284
  97.8 2.6 %collective-permute-start.19 = (f32[8,768]{1,0:T(8,128)S(1)}, f32[8,768]{1,0:T(8,128)S(1)}, u32[]{:S(2)}, u32[]{:S(2)}) collective-permute-start(f32[8,768]{1,0:T(8,128)S(1)} %fusion.7.refs_0_), channel_id=1, source_target_pairs={{20,0},{21,1},{22,2},{23,3},{24,4},{25,5},{26,6},{27,7},{28,8},{29... | collective-permute-start | bytes 73736 | tf_op jit(solution)/shard_map/ppermute | solution.py:284
  100.4 1.4 %collective-permute-start.20 = (f32[8,768]{1,0:T(8,128)S(1)}, f32[8,768]{1,0:T(8,128)S(1)}, u32[]{:S(2)}, u32[]{:S(2)}) collective-permute-start(f32[8,768]{1,0:T(8,128)S(1)} %fusion.7.refs_0_), channel_id=1, source_target_pairs={{64,0},{65,1},{66,2},{67,3},{68,4},{69,5},{70,6},{71,7},{72,8},{73... | collective-permute-start | bytes 73736 | tf_op jit(solution)/shard_map/ppermute | solution.py:284
  101.8 0.8 collective-permute-start.21
  102.7 1.9 %collective-permute-done.20.refs_4_ = f32[8,768]{1,0:T(8,128)S(1)} collective-permute-done((f32[8,768]{1,0:T(8,128)S(1)}, f32[8,768]{1,0:T(8,128)S(1)}, u32[]{:S(2)}, u32[]{:S(2)}) %collective-permute-start.20) | collective-permute-done | bytes 24608 | tf_op jit(solution)/shard_map/ppermute | solution.py:284
  104.6 1.9 %collective-permute-done.21.refs_5_ = f32[8,768]{1,0:T(8,128)S(1)} collective-permute-done((f32[8,768]{1,0:T(8,128)S(1)}, f32[8,768]{1,0:T(8,128)S(1)}, u32[]{:S(2)}, u32[]{:S(2)}) %collective-permute-start.21) | collective-permute-done | bytes 24608 | tf_op jit(solution)/shard_map/ppermute | solution.py:284
  (38 shorter events, 6.7 us)
Async XLA Ops:
  1.4 1.4 %copy-start = (bf16[768,1024]{1,0:T(8,128)(2,1)S(1)}, bf16[768,1024]{1,0:T(8,128)(2,1)}, u32[]{:S(2)}) copy-start(bf16[768,1024]{1,0:T(8,128)(2,1)} %emb_ref.1) | copy-start | bytes 4718596
  5.7 7.7 %collective-permute-start = (bf16[112,1024]{1,0:T(8,128)(2,1)S(1)}, bf16[112,1024]{1,0:T(8,128)(2,1)S(1)}, u32[]{:S(2)}, u32[]{:S(2)}) collective-permute-start(bf16[112,1024]{1,0:T(8,128)(2,1)S(1)} %get-tuple-element.16), channel_id=1, source_target_pairs={{0,16},{1,17},{2,18},{3,19},{4,20},{5,21},{6,22},{7,23},{8,24},{9,... | collective-permute-start | bytes 688136 | tf_op jit(solution)/shard_map/ppermute | solution.py:246
  7.2 7.6 %collective-permute-start.1 = (bf16[112,1024]{1,0:T(8,128)(2,1)S(1)}, bf16[112,1024]{1,0:T(8,128)(2,1)S(1)}, u32[]{:S(2)}, u32[]{:S(2)}) collective-permute-start(bf16[112,1024]{1,0:T(8,128)(2,1)S(1)} %get-tuple-element.17), channel_id=1, source_target_pairs={{0,32},{1,33},{2,34},{3,35},{4,36},{5,37},{6,38},{7,39},{8,40},{9,... | collective-permute-start | bytes 688136 | tf_op jit(solution)/shard_map/ppermute | solution.py:246
  8.6 9.5 %collective-permute-start.2 = (bf16[112,1024]{1,0:T(8,128)(2,1)S(1)}, bf16[112,1024]{1,0:T(8,128)(2,1)S(1)}, u32[]{:S(2)}, u32[]{:S(2)}) collective-permute-start(bf16[112,1024]{1,0:T(8,128)(2,1)S(1)} %get-tuple-element.18), channel_id=1, source_target_pairs={{0,20},{1,21},{2,22},{3,23},{4,24},{5,25},{6,26},{7,27},{8,28},{9,... | collective-permute-start | bytes 688136 | tf_op jit(solution)/shard_map/ppermute | solution.py:246
  9.9 11.6 %collective-permute-start.3 = (bf16[112,1024]{1,0:T(8,128)(2,1)S(1)}, bf16[112,1024]{1,0:T(8,128)(2,1)S(1)}, u32[]{:S(2)}, u32[]{:S(2)}) collective-permute-start(bf16[112,1024]{1,0:T(8,128)(2,1)S(1)} %get-tuple-element.19), channel_id=1, source_target_pairs={{0,64},{1,65},{2,66},{3,67},{4,68},{5,69},{6,70},{7,71},{8,72},{9,... | collective-permute-start | bytes 688136 | tf_op jit(solution)/shard_map/ppermute | solution.py:246
  12.9 9.4 %collective-permute-start.4 = (bf16[112,1024]{1,0:T(8,128)(2,1)S(1)}, bf16[112,1024]{1,0:T(8,128)(2,1)S(1)}, u32[]{:S(2)}, u32[]{:S(2)}) collective-permute-start(bf16[112,1024]{1,0:T(8,128)(2,1)S(1)} %get-tuple-element.20), channel_id=1, source_target_pairs={{0,24},{1,25},{2,26},{3,27},{4,28},{5,29},{6,30},{7,31},{8,16},{9,... | collective-permute-start | bytes 688136 | tf_op jit(solution)/shard_map/ppermute | solution.py:246
  13.4 9.3 %collective-permute-start.5 = (bf16[112,1024]{1,0:T(8,128)(2,1)S(1)}, bf16[112,1024]{1,0:T(8,128)(2,1)S(1)}, u32[]{:S(2)}, u32[]{:S(2)}) collective-permute-start(bf16[112,1024]{1,0:T(8,128)(2,1)S(1)} %get-tuple-element.21), channel_id=1, source_target_pairs={{0,96},{1,97},{2,98},{3,99},{4,100},{5,101},{6,102},{7,103},{8,104... | collective-permute-start | bytes 688136 | tf_op jit(solution)/shard_map/ppermute | solution.py:246
  14.8 9.5 %collective-permute-start.6 = (bf16[112,1024]{1,0:T(8,128)(2,1)S(1)}, bf16[112,1024]{1,0:T(8,128)(2,1)S(1)}, u32[]{:S(2)}, u32[]{:S(2)}) collective-permute-start(bf16[112,1024]{1,0:T(8,128)(2,1)S(1)} %get-tuple-element.22), channel_id=1, source_target_pairs={{0,28},{1,29},{2,30},{3,31},{4,16},{5,17},{6,18},{7,19},{8,20},{9,... | collective-permute-start | bytes 688136 | tf_op jit(solution)/shard_map/ppermute | solution.py:246
  24.5 22.3 %collective-permute-start.7 = (bf16[784,1024]{1,0:T(8,128)(2,1)S(1)}, bf16[784,1024]{1,0:T(8,128)(2,1)S(1)}, u32[]{:S(2)}, u32[]{:S(2)}) collective-permute-start(bf16[784,1024]{1,0:T(8,128)(2,1)S(1)} %shard_map.38.refs_0_), channel_id=1, source_target_pairs={{1,0},{2,1},{3,2},{0,3},{5,4},{6,5},{7,6},{4,7},{9,8},{10,9},{11,1... | collective-permute-start | bytes 4816904 | tf_op jit(solution)/shard_map/ppermute | solution.py:254
  26.2 22.2 %collective-permute-start.9 = (bf16[784,1024]{1,0:T(8,128)(2,1)S(1)}, bf16[784,1024]{1,0:T(8,128)(2,1)S(1)}, u32[]{:S(2)}, u32[]{:S(2)}) collective-permute-start(bf16[784,1024]{1,0:T(8,128)(2,1)S(1)} %shard_map.38.refs_0_), channel_id=1, source_target_pairs={{12,0},{13,1},{14,2},{15,3},{0,4},{1,5},{2,6},{3,7},{4,8},{5,9},{6... | collective-permute-start | bytes 4816904 | tf_op jit(solution)/shard_map/ppermute | solution.py:256
  27.1 36.7 %collective-permute-start.8 = (bf16[784,1024]{1,0:T(8,128)(2,1)S(1)}, bf16[784,1024]{1,0:T(8,128)(2,1)S(1)}, u32[]{:S(2)}, u32[]{:S(2)}) collective-permute-start(bf16[784,1024]{1,0:T(8,128)(2,1)S(1)} %shard_map.38.refs_0_), channel_id=1, source_target_pairs={{4,0},{5,1},{6,2},{7,3},{8,4},{9,5},{10,6},{11,7},{12,8},{13,9},{1... | collective-permute-start | bytes 4816904 | tf_op jit(solution)/shard_map/ppermute | solution.py:255
  28.9 41.5 %collective-permute-start.10 = (bf16[784,1024]{1,0:T(8,128)(2,1)S(1)}, bf16[784,1024]{1,0:T(8,128)(2,1)S(1)}, u32[]{:S(2)}, u32[]{:S(2)}) collective-permute-start(bf16[784,1024]{1,0:T(8,128)(2,1)S(1)} %shard_map.38.refs_0_), channel_id=1, source_target_pairs={{8,0},{9,1},{10,2},{11,3},{12,4},{13,5},{14,6},{15,7},{0,8},{1,9},... | collective-permute-start | bytes 4816904 | tf_op jit(solution)/shard_map/ppermute | solution.py:257
  46.8 23.6 %collective-permute-start.11 = (bf16[784,1024]{1,0:T(8,128)(2,1)S(1)}, bf16[784,1024]{1,0:T(8,128)(2,1)S(1)}, u32[]{:S(2)}, u32[]{:S(2)}) collective-permute-start(bf16[784,1024]{1,0:T(8,128)(2,1)S(1)} %collective-permute-done.7.refs_1_), channel_id=1, source_target_pairs={{1,0},{2,1},{3,2},{0,3},{5,4},{6,5},{7,6},{4,7},{9,8},{10,9},{11,1... | collective-permute-start | bytes 4816904 | tf_op jit(solution)/shard_map/ppermute | solution.py:258
  48.4 15.3 %copy-start.1 = (bf16[784,1024]{1,0:T(8,128)(2,1)}, bf16[784,1024]{1,0:T(8,128)(2,1)S(1)}, u32[]{:S(2)}) copy-start(bf16[784,1024]{1,0:T(8,128)(2,1)S(1)} %collective-permute-done.9.refs_3_.refs_2_) | copy-start | bytes 4816900
  70.4 1.2 %copy-start.3 = (bf16[784,1024]{1,0:T(8,128)(2,1)}, bf16[784,1024]{1,0:T(8,128)(2,1)S(1)}, u32[]{:S(2)}) copy-start(bf16[784,1024]{1,0:T(8,128)(2,1)S(1)} %collective-permute-done.10.refs_3_) | copy-start | bytes 4816900
  71.5 1.2 %copy-start.4 = (bf16[784,1024]{1,0:T(8,128)(2,1)}, bf16[784,1024]{1,0:T(8,128)(2,1)S(1)}, u32[]{:S(2)}) copy-start(bf16[784,1024]{1,0:T(8,128)(2,1)S(1)} %collective-permute-done.11.refs_4_) | copy-start | bytes 4816900
  72.7 1.4 %copy-start.2 = (bf16[784,1024]{1,0:T(8,128)(2,1)S(1)}, bf16[784,1024]{1,0:T(8,128)(2,1)}, u32[]{:S(2)}) copy-start(bf16[784,1024]{1,0:T(8,128)(2,1)} %copy-done.1) | copy-start | bytes 4816900
  81.3 9.3 %collective-permute-start.16 = (f32[8,768]{1,0:T(8,128)S(1)}, f32[8,768]{1,0:T(8,128)S(1)}, u32[]{:S(2)}, u32[]{:S(2)}) collective-permute-start(f32[8,768]{1,0:T(8,128)S(1)} %get-tuple-element.25), channel_id=1, source_target_pairs={{0,2},{1,3},{2,0},{3,1},{4,6},{5,7},{6,4},{7,5},{8,10},{9,11},{10,... | collective-permute-start | bytes 73736 | tf_op jit(solution)/shard_map/ppermute | solution.py:280
  84.7 6.0 %collective-permute-start.15 = (f32[8,768]{1,0:T(8,128)S(1)}, f32[8,768]{1,0:T(8,128)S(1)}, u32[]{:S(2)}, u32[]{:S(2)}) collective-permute-start(f32[8,768]{1,0:T(8,128)S(1)} %get-tuple-element.26), channel_id=1, source_target_pairs={{0,8},{1,9},{2,10},{3,11},{4,12},{5,13},{6,14},{7,15},{8,0},{9,1},... | collective-permute-start | bytes 73736 | tf_op jit(solution)/shard_map/ppermute | solution.py:280
  84.7 6.0 %collective-permute-start.14 = (f32[8,768]{1,0:T(8,128)S(1)}, f32[8,768]{1,0:T(8,128)S(1)}, u32[]{:S(2)}, u32[]{:S(2)}) collective-permute-start(f32[8,768]{1,0:T(8,128)S(1)} %get-tuple-element.24), channel_id=1, source_target_pairs={{0,12},{1,13},{2,14},{3,15},{4,0},{5,1},{6,2},{7,3},{8,4},{9,5},{1... | collective-permute-start | bytes 73736 | tf_op jit(solution)/shard_map/ppermute | solution.py:280
  87.9 4.2 %collective-permute-start.13 = (f32[8,768]{1,0:T(8,128)S(1)}, f32[8,768]{1,0:T(8,128)S(1)}, u32[]{:S(2)}, u32[]{:S(2)}) collective-permute-start(f32[8,768]{1,0:T(8,128)S(1)} %get-tuple-element.27), channel_id=1, source_target_pairs={{0,4},{1,5},{2,6},{3,7},{4,8},{5,9},{6,10},{7,11},{8,12},{9,13},{1... | collective-permute-start | bytes 73736 | tf_op jit(solution)/shard_map/ppermute | solution.py:280
  88.5 3.6 %collective-permute-start.12 = (f32[8,768]{1,0:T(8,128)S(1)}, f32[8,768]{1,0:T(8,128)S(1)}, u32[]{:S(2)}, u32[]{:S(2)}) collective-permute-start(f32[8,768]{1,0:T(8,128)S(1)} %get-tuple-element.23), channel_id=1, source_target_pairs={{0,1},{1,2},{2,3},{3,0},{4,5},{5,6},{6,7},{7,4},{8,9},{9,10},{10,1... | collective-permute-start | bytes 73736 | tf_op jit(solution)/shard_map/ppermute | solution.py:280
  92.1 10.5 %collective-permute-start.17 = (f32[8,768]{1,0:T(8,128)S(1)}, f32[8,768]{1,0:T(8,128)S(1)}, u32[]{:S(2)}, u32[]{:S(2)}) collective-permute-start(f32[8,768]{1,0:T(8,128)S(1)} %fusion.7.refs_0_), channel_id=1, source_target_pairs={{16,0},{17,1},{18,2},{19,3},{20,4},{21,5},{22,6},{23,7},{24,8},{25... | collective-permute-start | bytes 73736 | tf_op jit(solution)/shard_map/ppermute | solution.py:284
  95.6 7.0 %collective-permute-start.18 = (f32[8,768]{1,0:T(8,128)S(1)}, f32[8,768]{1,0:T(8,128)S(1)}, u32[]{:S(2)}, u32[]{:S(2)}) collective-permute-start(f32[8,768]{1,0:T(8,128)S(1)} %fusion.7.refs_0_), channel_id=1, source_target_pairs={{32,0},{33,1},{34,2},{35,3},{36,4},{37,5},{38,6},{39,7},{40,8},{41... | collective-permute-start | bytes 73736 | tf_op jit(solution)/shard_map/ppermute | solution.py:284
  97.8 4.9 %collective-permute-start.19 = (f32[8,768]{1,0:T(8,128)S(1)}, f32[8,768]{1,0:T(8,128)S(1)}, u32[]{:S(2)}, u32[]{:S(2)}) collective-permute-start(f32[8,768]{1,0:T(8,128)S(1)} %fusion.7.refs_0_), channel_id=1, source_target_pairs={{20,0},{21,1},{22,2},{23,3},{24,4},{25,5},{26,6},{27,7},{28,8},{29... | collective-permute-start | bytes 73736 | tf_op jit(solution)/shard_map/ppermute | solution.py:284
  100.4 4.2 %collective-permute-start.20 = (f32[8,768]{1,0:T(8,128)S(1)}, f32[8,768]{1,0:T(8,128)S(1)}, u32[]{:S(2)}, u32[]{:S(2)}) collective-permute-start(f32[8,768]{1,0:T(8,128)S(1)} %fusion.7.refs_0_), channel_id=1, source_target_pairs={{64,0},{65,1},{66,2},{67,3},{68,4},{69,5},{70,6},{71,7},{72,8},{73... | collective-permute-start | bytes 73736 | tf_op jit(solution)/shard_map/ppermute | solution.py:284
  101.8 4.8 %collective-permute-start.21 = (f32[8,768]{1,0:T(8,128)S(1)}, f32[8,768]{1,0:T(8,128)S(1)}, u32[]{:S(2)}, u32[]{:S(2)}) collective-permute-start(f32[8,768]{1,0:T(8,128)S(1)} %fusion.7.refs_0_), channel_id=1, source_target_pairs={{24,0},{25,1},{26,2},{27,3},{28,4},{29,5},{30,6},{31,7},{16,8},{17... | collective-permute-start | bytes 73736 | tf_op jit(solution)/shard_map/ppermute | solution.py:284
  102.6 3.9 %collective-permute-start.22 = (f32[8,768]{1,0:T(8,128)S(1)}, f32[8,768]{1,0:T(8,128)S(1)}, u32[]{:S(2)}, u32[]{:S(2)}) collective-permute-start(f32[8,768]{1,0:T(8,128)S(1)} %fusion.7.refs_0_), channel_id=1, source_target_pairs={{96,0},{97,1},{98,2},{99,3},{100,4},{101,5},{102,6},{103,7},{104,8... | collective-permute-start | bytes 73736 | tf_op jit(solution)/shard_map/ppermute | solution.py:284
  102.6 4.7 %collective-permute-start.23 = (f32[8,768]{1,0:T(8,128)S(1)}, f32[8,768]{1,0:T(8,128)S(1)}, u32[]{:S(2)}, u32[]{:S(2)}) collective-permute-start(f32[8,768]{1,0:T(8,128)S(1)} %fusion.7.refs_0_), channel_id=1, source_target_pairs={{28,0},{29,1},{30,2},{31,3},{16,4},{17,5},{18,6},{19,7},{20,8},{21... | collective-permute-start | bytes 73736 | tf_op jit(solution)/shard_map/ppermute | solution.py:284

commit v2 on v1

v2 whole, which is shorter than its diff:
```python
import functools

import jax
import jax.numpy as jnp
from jax import lax
from jax.experimental import pallas as pl
from jax.experimental.pallas import tpu as pltpu
from jax.sharding import PartitionSpec as P

AXES = ("clus", "fold")
RING = 4
DEVICES = 128
EMB = 1024
ROWS = 768
PIECES = 8
PIECE = 96
PIECE_ROWS = 112
HALF = 384
HALF_PIECES = 4
HALF_ROWS = 400
LANES = 128
LO = 128
FAR = 1.0e6
WIDE = 256
CHUNK = 256
VMEM = 12 * 1024 * 1024
OWN, UP, RIGHT, LEFT, OVER, UP2 = range(6)
OFFSETS = ((0, 0), (0, 1), (1, 0), (3, 0), (2, 0), (0, 2))
HALVES = 2 * len(OFFSETS)


def place(x, core, y, z):
    return (x % RING * 2 + core) * 16 + y % RING * 4 + z % RING


def every_device():
    for x in range(RING):
        for core in range(2):
            for y in range(RING):
                for z in range(RING):
                    yield x, core, y, z


def packet_pairs(piece):
    offset, cross = divmod(piece, 2)
    pairs = []
    for x, core, y, z in every_device():
        kind = core ^ cross
        target = place(x + offset, 0, y, z) if kind == 0 else place(x, 1, y + offset, z)
        pairs.append((place(x, core, y, z), target))
    return pairs


def block_pairs(du, dv):
    pairs = []
    for x, core, y, z in every_device():
        source = place(x, 0, y + du, z + dv) if core == 0 else place(x + du, 1, y, z - dv)
        pairs.append((source, place(x, core, y, z)))
    return pairs


def whole(count):
    return [pl.BlockSpec(memory_space=pltpu.VMEM)] * count


def params():
    return pltpu.CompilerParams(vmem_limit_bytes=VMEM)


def pack_kernel(emb_hbm, labels_ref, ordinals_ref, slot_ref, *refs):
    piece_refs, (emb, unit, sems) = refs[:PIECES], refs[PIECES:]
    copies = [
        pltpu.make_async_copy(
            emb_hbm.at[pl.ds(i, CHUNK)], emb.at[pl.ds(i, CHUNK)], sems.at[i // CHUNK]
        )
        for i in range(0, ROWS, CHUNK)
    ]
    for copy in copies:
        copy.start()
    clus, fold = lax.axis_index("clus"), lax.axis_index("fold")
    core, x, y = clus % 2, clus // 2, fold // RING
    labels, ordinals = labels_ref[...], ordinals_ref[...]
    kind = labels // RING
    coordinate = jnp.where(kind == 0, x, y)
    offset = (labels % RING - coordinate + RING) % RING
    piece = 2 * offset + jnp.where(kind == core, 0, 1)
    live = labels < PIECES
    ids = lax.broadcasted_iota(jnp.int32, (16, ROWS), 0)
    member = (ids == piece) & live
    before = lax.broadcasted_iota(jnp.int32, (ROWS, ROWS), 0) < lax.broadcasted_iota(
        jnp.int32, (ROWS, ROWS), 1
    )
    counts = jnp.dot(
        jnp.where(member, 1.0, 0.0).astype(jnp.bfloat16),
        jnp.where(before, 1.0, 0.0).astype(jnp.bfloat16),
        preferred_element_type=jnp.float32,
    )
    rank = jnp.sum(jnp.where(member, counts, 0.0), axis=0, keepdims=True).astype(jnp.int32)
    slot = jnp.where(live, piece * PIECE + rank, -1)
    slot_ref[...] = slot
    chosen = lax.broadcasted_iota(jnp.int32, (ROWS, ROWS), 0) == slot
    pick = jnp.where(chosen, 1.0, 0.0).astype(jnp.bfloat16)
    high, low = ordinals // LO + 1, ordinals % LO
    row_id = lax.broadcasted_iota(jnp.int32, (16, ROWS), 0)
    codes = jnp.where(row_id == 0, high, jnp.where(row_id == 1, low, 0)).astype(jnp.float32)
    packed_codes = lax.dot_general(
        codes.astype(jnp.bfloat16),
        pick,
        (((1,), (1,)), ((), ())),
        preferred_element_type=jnp.float32,
    )
    for i, copy in zip(range(0, ROWS, CHUNK), copies, strict=True):
        copy.wait()
        widened = emb[pl.ds(i, CHUNK), :].astype(jnp.float32)
        square_sum = jnp.sum(widened * widened, axis=1, keepdims=True) + 1e-6
        unit[pl.ds(i, CHUNK), :] = (widened * lax.rsqrt(square_sum)).astype(jnp.bfloat16)
    packed = jnp.dot(pick, unit[...], preferred_element_type=jnp.float32).astype(jnp.bfloat16)
    lane_piece = lax.broadcasted_iota(jnp.int32, (16, HALF), 1) // PIECE
    for s in range(PIECES):
        half, place_in_half = divmod(s, HALF_PIECES)
        piece_refs[s][:PIECE, :] = packed[s * PIECE : (s + 1) * PIECE]
        mine = packed_codes[:, half * HALF : (half + 1) * HALF]
        mine = jnp.where(lane_piece == place_in_half, mine, 0.0).astype(jnp.bfloat16)
        piece_refs[s][PIECE:, :HALF] = mine
        piece_refs[s][PIECE:, HALF:] = jnp.zeros((16, EMB - HALF), jnp.bfloat16)


def pack(embeddings, labels, ordinals):
    return pl.pallas_call(
        pack_kernel,
        out_shape=[jax.ShapeDtypeStruct((1, ROWS), jnp.int32)]
        + [jax.ShapeDtypeStruct((PIECE_ROWS, EMB), jnp.bfloat16)] * PIECES,
        in_specs=[pl.BlockSpec(memory_space=pl.ANY)] + whole(2),
        out_specs=whole(1 + PIECES),
        scratch_shapes=[
            pltpu.VMEM((ROWS, EMB), jnp.bfloat16),
            pltpu.VMEM((ROWS, EMB), jnp.bfloat16),
            pltpu.SemaphoreType.DMA((ROWS // CHUNK,)),
        ],
        compiler_params=params(),
    )(embeddings, labels.reshape(1, ROWS), ordinals.reshape(1, ROWS))


def join_kernel(*refs):
    piece_refs, half_ref = refs[:HALF_PIECES], refs[HALF_PIECES]
    codes = jnp.zeros((16, HALF), jnp.float32)
    for s in range(HALF_PIECES):
        half_ref[s * PIECE : (s + 1) * PIECE, :] = piece_refs[s][:PIECE, :]
        codes = codes + piece_refs[s][PIECE:, :HALF].astype(jnp.float32)
    half_ref[HALF:, :HALF] = codes.astype(jnp.bfloat16)
    half_ref[HALF:, HALF:] = jnp.zeros((16, EMB - HALF), jnp.bfloat16)


def join(pieces):
    return pl.pallas_call(
        join_kernel,
        out_shape=jax.ShapeDtypeStruct((HALF_ROWS, EMB), jnp.bfloat16),
        in_specs=whole(HALF_PIECES),
        out_specs=whole(1)[0],
        compiler_params=params(),
    )(*pieces)


def where_am_i():
    clus, fold = lax.axis_index("clus"), lax.axis_index("fold")
    return clus // 2, clus % 2, fold // RING, fold % RING


def post(out_ref, result_ref):
    x, core, y, z = where_am_i()
    out_ref[...] = jnp.zeros_like(out_ref)
    for slot, (du, dv) in enumerate(OFFSETS):
        for s in range(PIECES):
            half, place_in_half = divmod(s, HALF_PIECES)
            ring, cross = divmod(s, 2)
            best = jnp.max(result_ref[2 * slot + half], axis=0, keepdims=True)
            best = jnp.broadcast_to(best, (8, HALF))
            if place_in_half:
                best = pltpu.roll(best, HALF - place_in_half * PIECE, 1)
            on_zero = place(x + RING - ring, cross, y + du, z + dv)
            on_one = place(x + du, 1 - cross, y + RING - ring, z + RING - dv)
            target = jnp.where(core == 0, on_zero, on_one)
            out_ref[pl.ds(target, 1), :] = best[0:1, :LANES]


def meet_kernel(names, steps, has_before, is_last, *refs):
    blocks = dict(zip(names, refs[: len(names)], strict=True))
    refs = refs[len(names) :]
    if has_before:
        before_ref, refs = refs[0], refs[1:]
    if is_last:
        out_ref, result, rows_best, column_ord = refs
    else:
        result, rows_best, column_ord = refs
    x, core, y, z = where_am_i()
    sides = {"u": jnp.where(core == 0, y, x) // 2, "v": z // 2}

    result[...] = before_ref[...] if has_before else jnp.full_like(result, -1.0)
    lines = {}
    for name in names:
        codes = blocks[name][HALF:, :HALF].astype(jnp.float32)
        high, low = codes[0:1], codes[1:2]
        lines[name] = jnp.where(high == 0.0, FAR, (high - 1.0) * LO + low)
    firsts = list(dict.fromkeys(a for a, _, _ in steps))
    for i, name in enumerate(firsts):
        column_ord[i] = jnp.transpose(jnp.broadcast_to(lines[name], (LANES, HALF)))
        rows_best[i] = jnp.full((HALF, LANES), -1.0, jnp.float32)

    def tile(a, keys, both):
        i = firsts.index(a)
        parts = [blocks[b][start : start + size, :] for b, start, size in keys]
        scores = lax.dot_general(
            blocks[a][:HALF, :],
            parts[0] if len(parts) == 1 else jnp.concatenate(parts, axis=0),
            (((1,), (1,)), ((), ())),
            preferred_element_type=jnp.float32,
        )
        best, k = rows_best[i], 0
        for b, start, size in keys:
            for lane in range(start, start + size, LANES):
                part = scores[:, k : k + LANES]
                earlier = lines[b][:, lane : lane + LANES] < column_ord[i]
                best = jnp.maximum(best, jnp.where(earlier, part, -1.0))
                if both:
                    later = jnp.where(earlier, -1.0, part).reshape(HALF // 8, 8, LANES)
                    later = jnp.max(later, axis=0)
                    at = (2 * b[0] + b[1], slice(None), slice(lane, lane + LANES))
                    result[at] = jnp.maximum(result[at], later)
                k += LANES
        rows_best[i] = best

    def step(a, b):
        if isinstance(b, tuple):
            tile(a, [(b, 0, WIDE)], True)
            tile(a, [(b, WIDE, HALF - WIDE)], True)
        else:
            both = a[0] != b
            tile(a, [((b, 0), 0, WIDE)], both)
            tile(a, [((b, 1), 0, WIDE)], both)
            tile(a, [((b, 0), WIDE, HALF - WIDE), ((b, 1), WIDE, HALF - WIDE)], both)

    for a, b, role in steps:
        if role is None:
            step(a, b)
        else:
            pl.when(sides[role[0]] == role[1])(functools.partial(step, a, b))
    for i, name in enumerate(firsts):
        across = jnp.transpose(rows_best[i]).reshape(LANES // 8, 8, HALF)
        at = 2 * name[0] + name[1]
        result[at] = jnp.maximum(result[at], jnp.max(across, axis=0))
    if is_last:
        post(out_ref, result)


def meet(held, steps, before, is_last=False):
    names = []
    for a, b, _ in steps:
        names += [a] + ([b] if isinstance(b, tuple) else [(b, 0), (b, 1)])
    names = list(dict.fromkeys(names))
    given = [held[name] for name in names] + ([] if before is None else [before])
    products = sum(0.25 if isinstance(b, tuple) else 0.5 for _, b, _ in steps)
    firsts = len({a for a, _, _ in steps})
    best = (HALVES, 8, HALF)
    return pl.pallas_call(
        functools.partial(meet_kernel, names, steps, before is not None, is_last),
        out_shape=jax.ShapeDtypeStruct((DEVICES, LANES) if is_last else best, jnp.float32),
        in_specs=whole(len(given)),
        out_specs=whole(1)[0],
        scratch_shapes=([pltpu.VMEM(best, jnp.float32)] if is_last else [])
        + [pltpu.VMEM((firsts, HALF, LANES), jnp.float32)] * 2,
        compiler_params=params(),
        cost_estimate=pl.CostEstimate(
            flops=int(2 * products * ROWS * ROWS * EMB),
            bytes_accessed=len(names) * HALF_ROWS * EMB * 2,
            transcendentals=0,
        ),
    )(*given)


def unpack_kernel(slot_ref, got_ref, out_ref):
    x, core, y, z = where_am_i()
    slot = slot_ref[...]
    found = jnp.full((8, ROWS), -1.0, jnp.float32)
    for s in range(PIECES):
        ring, cross = divmod(s, 2)
        line = jnp.full((1, LANES), -1.0, jnp.float32)
        for du, dv in OFFSETS:
            on_zero = place(x + ring, 0, y + RING - du, z + RING - dv)
            on_one = place(x + RING - du, 1, y + ring, z + dv)
            holder = jnp.where(core == cross, on_zero, on_one)
            line = jnp.maximum(line, got_ref[pl.ds(holder, 1), :])
        column = jnp.transpose(jnp.broadcast_to(line, (LANES, LANES)))[:PIECE]
        rows = lax.broadcasted_iota(jnp.int32, (PIECE, LANES), 0) + s * PIECE
        best = []
        for k in range(0, ROWS, LANES):
            chosen = jnp.where(rows == slot[:, k : k + LANES], column, -1.0)
            best.append(jnp.max(chosen.reshape(PIECE // 8, 8, LANES), axis=0))
        found = jnp.maximum(found, jnp.concatenate(best, axis=1))
    out_ref[...] = jnp.max(found, axis=0, keepdims=True)


def unpack(slot, got):
    return pl.pallas_call(
        unpack_kernel,
        out_shape=jax.ShapeDtypeStruct((1, ROWS), jnp.float32),
        in_specs=whole(2),
        out_specs=whole(1)[0],
        compiler_params=params(),
    )(slot, got).reshape(ROWS)


def per_device(embeddings, labels, ordinals):
    send = functools.partial(lax.ppermute, axis_name=AXES)
    slot, *pieces = pack(embeddings, labels, ordinals)
    landed = [pieces[0]] + [send(pieces[s], perm=packet_pairs(s)) for s in range(1, PIECES)]
    held = {}
    for h in range(2):
        held[OWN, h] = join(landed[h * HALF_PIECES : (h + 1) * HALF_PIECES])
        held[UP, h] = send(held[OWN, h], perm=block_pairs(0, 1))
        held[RIGHT, h] = send(held[OWN, h], perm=block_pairs(1, 0))
        held[LEFT, h] = send(held[OWN, h], perm=block_pairs(3, 0))
        held[UP2, h] = send(held[UP, h], perm=block_pairs(0, 1))
    held[OVER, 0] = send(held[RIGHT, 0], perm=block_pairs(1, 0))
    held[OVER, 1] = send(held[LEFT, 1], perm=block_pairs(3, 0))
    best = meet(
        held,
        [
            ((OWN, 0), OWN, None),
            ((OWN, 1), OWN, None),
            ((UP, 0), OWN, None),
            ((RIGHT, 0), OWN, None),
            ((RIGHT, 0), (LEFT, 0), ("u", 0)),
        ],
        None,
    )
    best = meet(
        held,
        [
            ((UP, 1), OWN, None),
            ((RIGHT, 1), OWN, None),
            ((UP, 0), RIGHT, None),
            ((UP, 1), RIGHT, None),
            ((UP, 0), LEFT, None),
            ((UP, 1), LEFT, None),
            ((RIGHT, 0), (LEFT, 1), None),
            ((RIGHT, 1), (LEFT, 1), ("u", 1)),
        ],
        best,
    )
    best = meet(
        held,
        [
            ((OVER, 0), UP, None),
            ((UP2, 0), LEFT, None),
            ((UP2, 0), (OWN, 1), None),
            ((UP2, 0), (OWN, 0), ("v", 0)),
            ((UP2, 0), (OVER, 0), ("u", 0)),
        ],
        best,
    )
    best = meet(
        held,
        [((OVER, 1), UP, None), ((OVER, 1), (UP2, 0), None)],
        best,
    )
    sent = meet(
        held,
        [
            ((UP2, 1), LEFT, None),
            ((UP2, 1), (OWN, 1), ("v", 1)),
            ((UP2, 1), (OVER, 1), ("u", 1)),
        ],
        best,
        True,
    )
    got = lax.all_to_all(sent, AXES, split_axis=0, concat_axis=0, tiled=True)
    return unpack(slot, got)


def solution(mesh):
    return jax.shard_map(
        per_device,
        mesh=mesh,
        in_specs=(P(AXES, None), P(AXES), P(AXES)),
        out_specs=P(AXES),
        check_vma=False,
    )
```

time: 109 us -> 86 us (0.79)
  waiting for transfers between devices: 45.4 us -> 24.8 us
  blocking collectives: 0 us -> 18.4 us
  starting transfers between devices: 35.3 us -> 21.4 us
  local copies, waits for them, and re-layouts: 6.51 us -> 2.79 us
  Pallas kernels: 20.4 us -> 17.6 us
    ppermute x17 -> x10, waiting for transfers between devices: 39.1 us -> 13.3 us  [the longest x2 6.29 us: per_device(): held[LEFT, h] = send(held[OWN, h], perm=block_pairs(3, 0))]
    all_to_all x0 -> x1, blocking collectives: none -> 18.4 us  [per_device(): got = lax.all_to_all(sent, AXES, split_axis=0, concat_axis=0, tiled=True)]
    ppermute x17 -> x10, starting transfers between devices: 23 us -> 8.04 us  [the longest x2 3.59 us: per_device(): held[RIGHT, h] = send(held[OWN, h], perm=block_pairs(1, 0))]
    ppermute x7, waiting for transfers between devices: 6.28 us -> 11.5 us  [per_device(): send(pieces[s], perm=packet_pairs(s))]
    unnamed x10 -> x2, local copies, waits for them, and re-layouts: 5.13 us -> 1.41 us
    pallas_call x7 -> x9, Pallas kernels: 20.4 us -> 17.6 us  [the longest x5 14.5 us: meet(): pl.pallas_call(functools.partial(meet_kernel, names, steps, before is not...]
  transfers between devices with their start and end apart: 24 -> 17, of which waited for: 10 -> 9; matrix products, arithmetic and copies ran while one was open for 0% -> 0% of each run, Pallas kernels for 9% -> 16%
where the time goes in v2:
time: 86 us; the launch traced here: 85.8 us
  waiting for transfers between devices  24.8 us (29%)
  starting transfers between devices  21.4 us (25%)
  blocking collectives  18.4 us (21%)
  Pallas kernels  17.6 us (20%)
  local copies, waits for them, and re-layouts  2.79 us (3%)
    all_to_all x1, blocking collectives, per_device(): got = lax.all_to_all(sent, AXES, split_axis=0, concat_axis=0, tiled=True)  18.4 us
    pallas_call x5, Pallas kernels, meet(): pl.pallas_call(functools.partial(meet_kernel, names, steps, before is not...  14.5 us
    ppermute x7, starting transfers between devices, per_device(): send(pieces[s], perm=packet_pairs(s))  13.4 us
    ppermute x7, waiting for transfers between devices, per_device(): send(pieces[s], perm=packet_pairs(s))  11.5 us
    ppermute x2, waiting for transfers between devices, per_device(): held[LEFT, h] = send(held[OWN, h], perm=block_pairs(3, 0))  6.29 us
    ppermute x2, starting transfers between devices, per_device(): held[RIGHT, h] = send(held[OWN, h], perm=block_pairs(1, 0))  3.59 us
    ppermute x2, waiting for transfers between devices, per_device(): held[RIGHT, h] = send(held[OWN, h], perm=block_pairs(1, 0))  3.53 us
    ppermute x1, waiting for transfers between devices, per_device(): held[OVER, 0] = send(held[RIGHT, 0], perm=block_pairs(1, 0))  3.49 us
  transfers between devices with their start and end apart: 17, of which 9 were waited for; matrix products, arithmetic and copies ran while one was open for 0% of the time, Pallas kernels for 16%

profile of v2, /device:TPU:1, one launch (start us, length us, event | category | flops | bytes accessed | tf_op | source)
XLA Modules:
  0.0 85.8 jit_solution(9358820454498064204)
XLA Ops:
  0.0 0.7 reshape.11.labels_ref
  0.7 0.7 reshape.12.ordinals_ref
  1.4 1.4 %copy-done = bf16[768,1024]{1,0:T(8,128)(2,1)S(1)} copy-done((bf16[768,1024]{1,0:T(8,128)(2,1)S(1)}, bf16[768,1024]{1,0:T(8,128)(2,1)}, u32[]{:S(2)}) %copy-start) | copy-done | bytes 1572888
  2.8 2.6 %shard_map.37 = (s32[1,768]{1,0:T(1,128)S(1)}, bf16[112,1024]{1,0:T(8,128)(2,1)S(1)}, bf16[112,1024]{1,0:T(8,128)(2,1)S(1)}, bf16[112,1024]{1,0:T(8,128)(2,1)S(1...) custom-call(bf16[768,1024]{1,0:T(8,128)(2,1)S(1)} %copy-done, ...), custom_call_target="tpu_custom_call" | custom-call | tf_op jit(solution)/shard_map/pallas_call | solution.py:129
  5.4 1.5 %collective-permute-start.6 = (bf16[112,1024]{1,0:T(8,128)(2,1)S(1)}, bf16[112,1024]{1,0:T(8,128)(2,1)S(1)}, u32[]{:S(2)}, u32[]{:S(2)}) collective-permute-start(bf16[112,1024]{1,0:T(8,128)(2,1)S(1)} %get-tuple-element.20), channel_id=1, source_target_pairs={{0,16},{1,17},{2,18},{3,19},{4,20},{5,21},{6,22},{7,23},{8,24},{9,... | collective-permute-start | bytes 688136 | tf_op jit(solution)/shard_map/ppermute | solution.py:315
  6.9 1.4 %collective-permute-start.7 = (bf16[112,1024]{1,0:T(8,128)(2,1)S(1)}, bf16[112,1024]{1,0:T(8,128)(2,1)S(1)}, u32[]{:S(2)}, u32[]{:S(2)}) collective-permute-start(bf16[112,1024]{1,0:T(8,128)(2,1)S(1)} %get-tuple-element.21), channel_id=1, source_target_pairs={{0,32},{1,33},{2,34},{3,35},{4,36},{5,37},{6,38},{7,39},{8,40},{9,... | collective-permute-start | bytes 688136 | tf_op jit(solution)/shard_map/ppermute | solution.py:315
  8.3 1.4 %collective-permute-start.8 = (bf16[112,1024]{1,0:T(8,128)(2,1)S(1)}, bf16[112,1024]{1,0:T(8,128)(2,1)S(1)}, u32[]{:S(2)}, u32[]{:S(2)}) collective-permute-start(bf16[112,1024]{1,0:T(8,128)(2,1)S(1)} %get-tuple-element.22), channel_id=1, source_target_pairs={{0,20},{1,21},{2,22},{3,23},{4,24},{5,25},{6,26},{7,27},{8,28},{9,... | collective-permute-start | bytes 688136 | tf_op jit(solution)/shard_map/ppermute | solution.py:315
  9.7 4.3 %collective-permute-done.7.refs_2_ = bf16[112,1024]{1,0:T(8,128)(2,1)S(1)} collective-permute-done((bf16[112,1024]{1,0:T(8,128)(2,1)S(1)}, bf16[112,1024]{1,0:T(8,128)(2,1)S(1)}, u32[]{:S(2)}, u32[]{:S(2)}) %collective-permute-start.7) | collective-permute-done | bytes 229408 | tf_op jit(solution)/shard_map/ppermute | solution.py:315
  14.0 1.9 %collective-permute-done.8.refs_3_ = bf16[112,1024]{1,0:T(8,128)(2,1)S(1)} collective-permute-done((bf16[112,1024]{1,0:T(8,128)(2,1)S(1)}, bf16[112,1024]{1,0:T(8,128)(2,1)S(1)}, u32[]{:S(2)}, u32[]{:S(2)}) %collective-permute-start.8) | collective-permute-done | bytes 229408 | tf_op jit(solution)/shard_map/ppermute | solution.py:315
  16.0 1.7 %collective-permute-start.12 = (bf16[400,1024]{1,0:T(8,128)(2,1)S(1)}, bf16[400,1024]{1,0:T(8,128)(2,1)S(1)}, u32[]{:S(2)}, u32[]{:S(2)}) collective-permute-start(bf16[400,1024]{1,0:T(8,128)(2,1)S(1)} %shard_map.39.refs_0_.refs_1_.refs_7_), channel_id=1, source_target_pairs={{1,0},{2,1},{3,2},{0,3},{5,4},{6,5},{7,6},{4,7},{9,8},{10,9},{11,1... | collective-permute-start | bytes 2457608 | tf_op jit(solution)/shard_map/ppermute | solution.py:319
  17.7 1.6 %collective-permute-start = (bf16[112,1024]{1,0:T(8,128)(2,1)S(1)}, bf16[112,1024]{1,0:T(8,128)(2,1)S(1)}, u32[]{:S(2)}, u32[]{:S(2)}) collective-permute-start(bf16[112,1024]{1,0:T(8,128)(2,1)S(1)} %get-tuple-element.15), channel_id=1, source_target_pairs={{0,64},{1,65},{2,66},{3,67},{4,68},{5,69},{6,70},{7,71},{8,72},{9,... | collective-permute-start | bytes 688136 | tf_op jit(solution)/shard_map/ppermute | solution.py:315
  19.3 4.8 %collective-permute-start.1 = (bf16[112,1024]{1,0:T(8,128)(2,1)S(1)}, bf16[112,1024]{1,0:T(8,128)(2,1)S(1)}, u32[]{:S(2)}, u32[]{:S(2)}) collective-permute-start(bf16[112,1024]{1,0:T(8,128)(2,1)S(1)} %get-tuple-element.16), channel_id=1, source_target_pairs={{0,24},{1,25},{2,26},{3,27},{4,28},{5,29},{6,30},{7,31},{8,16},{9,... | collective-permute-start | bytes 688136 | tf_op jit(solution)/shard_map/ppermute | solution.py:315
  24.1 2.7 %collective-permute-start.2 = (bf16[112,1024]{1,0:T(8,128)(2,1)S(1)}, bf16[112,1024]{1,0:T(8,128)(2,1)S(1)}, u32[]{:S(2)}, u32[]{:S(2)}) collective-permute-start(bf16[112,1024]{1,0:T(8,128)(2,1)S(1)} %get-tuple-element.17), channel_id=1, source_target_pairs={{0,96},{1,97},{2,98},{3,99},{4,100},{5,101},{6,102},{7,103},{8,104... | collective-permute-start | bytes 688136 | tf_op jit(solution)/shard_map/ppermute | solution.py:315
  26.8 2.7 %collective-permute-done.1.refs_1_ = bf16[112,1024]{1,0:T(8,128)(2,1)S(1)} collective-permute-done((bf16[112,1024]{1,0:T(8,128)(2,1)S(1)}, bf16[112,1024]{1,0:T(8,128)(2,1)S(1)}, u32[]{:S(2)}, u32[]{:S(2)}) %collective-permute-start.1) | collective-permute-done | bytes 229408 | tf_op jit(solution)/shard_map/ppermute | solution.py:315
  29.6 1.2 %collective-permute-start.14 = (bf16[400,1024]{1,0:T(8,128)(2,1)S(1)}, bf16[400,1024]{1,0:T(8,128)(2,1)S(1)}, u32[]{:S(2)}, u32[]{:S(2)}) collective-permute-start(bf16[400,1024]{1,0:T(8,128)(2,1)S(1)} %shard_map.39.refs_0_.refs_1_.refs_7_), channel_id=1, source_target_pairs={{4,0},{5,1},{6,2},{7,3},{8,4},{9,5},{10,6},{11,7},{12,8},{13,9},{1... | collective-permute-start | bytes 2457608 | tf_op jit(solution)/shard_map/ppermute | solution.py:320
  30.8 1.1 %collective-permute-done.2.refs_2_ = bf16[112,1024]{1,0:T(8,128)(2,1)S(1)} collective-permute-done((bf16[112,1024]{1,0:T(8,128)(2,1)S(1)}, bf16[112,1024]{1,0:T(8,128)(2,1)S(1)}, u32[]{:S(2)}, u32[]{:S(2)}) %collective-permute-start.2) | collective-permute-done | bytes 229408 | tf_op jit(solution)/shard_map/ppermute | solution.py:315
  31.9 1.4 %collective-permute-done.3.refs_3_ = bf16[112,1024]{1,0:T(8,128)(2,1)S(1)} collective-permute-done((bf16[112,1024]{1,0:T(8,128)(2,1)S(1)}, bf16[112,1024]{1,0:T(8,128)(2,1)S(1)}, u32[]{:S(2)}, u32[]{:S(2)}) %collective-permute-start.3) | collective-permute-done | bytes 229408 | tf_op jit(solution)/shard_map/ppermute | solution.py:315
  33.4 0.3 collective-permute-start.10
  33.8 2.4 %collective-permute-start.16 = (bf16[400,1024]{1,0:T(8,128)(2,1)S(1)}, bf16[400,1024]{1,0:T(8,128)(2,1)S(1)}, u32[]{:S(2)}, u32[]{:S(2)}) collective-permute-start(bf16[400,1024]{1,0:T(8,128)(2,1)S(1)} %shard_map.38.refs_1_.refs_2_.refs_6_.refs_3_), channel_id=1, source_target_pairs={{4,0},{5,1},{6,2},{7,3},{8,4},{9,5},{10,6},{11,7},{12,8},{13,9},{1... | collective-permute-start | bytes 2457608 | tf_op jit(solution)/shard_map/ppermute | solution.py:320
  36.1 3.4 %collective-permute-done.9.refs_4_.refs_6_.refs_1_ = bf16[400,1024]{1,0:T(8,128)(2,1)S(1)} collective-permute-done((bf16[400,1024]{1,0:T(8,128)(2,1)S(1)}, bf16[400,1024]{1,0:T(8,128)(2,1)S(1)}, u32[]{:S(2)}, u32[]{:S(2)}) %collective-permute-start.9) | collective-permute-done | bytes 819232 | tf_op jit(solution)/shard_map/ppermute | solution.py:321
  39.5 3.5 %collective-permute-done.14.refs_3_.refs_5_ = bf16[400,1024]{1,0:T(8,128)(2,1)S(1)} collective-permute-done((bf16[400,1024]{1,0:T(8,128)(2,1)S(1)}, bf16[400,1024]{1,0:T(8,128)(2,1)S(1)}, u32[]{:S(2)}, u32[]{:S(2)}) %collective-permute-start.14) | collective-permute-done | bytes 819232 | tf_op jit(solution)/shard_map/ppermute | solution.py:320
  43.1 2.3 %collective-permute-start.15 = (bf16[400,1024]{1,0:T(8,128)(2,1)S(1)}, bf16[400,1024]{1,0:T(8,128)(2,1)S(1)}, u32[]{:S(2)}, u32[]{:S(2)}) collective-permute-start(bf16[400,1024]{1,0:T(8,128)(2,1)S(1)} %collective-permute-done.14.refs_3_.refs_5_), channel_id=1, source_target_pairs={{4,0},{5,1},{6,2},{7,3},{8,4},{9,5},{10,6},{11,7},{12,8},{13,9},{1... | collective-permute-start | bytes 2457608 | tf_op jit(solution)/shard_map/ppermute | solution.py:323
  45.4 2.9 %collective-permute-done.10.refs_7_.refs_5_.refs_2_ = bf16[400,1024]{1,0:T(8,128)(2,1)S(1)} collective-permute-done((bf16[400,1024]{1,0:T(8,128)(2,1)S(1)}, bf16[400,1024]{1,0:T(8,128)(2,1)S(1)}, u32[]{:S(2)}, u32[]{:S(2)}) %collective-permute-start.10) | collective-permute-done | bytes 819232 | tf_op jit(solution)/shard_map/ppermute | solution.py:321
  48.3 3.8 %shard_map.40.refs_8_ = f32[12,8,384]{2,1,0:T(8,128)S(1)} custom-call(bf16[400,1024]{1,0:T(8,128)(2,1)S(1)} %shard_map.39.refs_0_.refs_1_.refs_7_, bf16[400,1024]{1,0:T(8,128)(2,1)S(1)} %shard_map.38.refs_1_.refs_2_.refs_6_.refs_3_, bf16[400,1024]{1,0:T(8,128)(2,1)S(1)} %collective-permute-done.12.refs_2_.refs_4_.refs_1_, ...), custom_call_target="tpu_custom_call" | custom-call | flops 2717908992 | bytes 4096000 | tf_op jit(solution)/shard_map/pallas_call | solution.py:264
  52.2 5.0 %shard_map.41.refs_8_ = f32[12,8,384]{2,1,0:T(8,128)S(1)} custom-call(bf16[400,1024]{1,0:T(8,128)(2,1)S(1)} %collective-permute-done.4.refs_0_.refs_2_, bf16[400,1024]{1,0:T(8,128)(2,1)S(1)} %shard_map.39.refs_0_.refs_1_.refs_7_, bf16[400,1024]{1,0:T(8,128)(2,1)S(1)} %shard_map.38.refs_1_.refs_2_.refs_6_.refs_3_, ...), custom_call_target="tpu_custom_call" | custom-call | flops 4227858432 | bytes 6553600 | tf_op jit(solution)/shard_map/pallas_call | solution.py:264
  57.1 3.5 %collective-permute-done.15.refs_0_ = bf16[400,1024]{1,0:T(8,128)(2,1)S(1)} collective-permute-done((bf16[400,1024]{1,0:T(8,128)(2,1)S(1)}, bf16[400,1024]{1,0:T(8,128)(2,1)S(1)}, u32[]{:S(2)}, u32[]{:S(2)}) %collective-permute-start.15) | collective-permute-done | bytes 819232 | tf_op jit(solution)/shard_map/ppermute | solution.py:323
  60.6 3.3 %shard_map.42.refs_4_ = f32[12,8,384]{2,1,0:T(8,128)S(1)} custom-call(bf16[400,1024]{1,0:T(8,128)(2,1)S(1)} %collective-permute-done.15.refs_0_, bf16[400,1024]{1,0:T(8,128)(2,1)S(1)} %collective-permute-done.12.refs_2_.refs_4_.refs_1_, bf16[400,1024]{1,0:T(8,128)(2,1)S(1)} %collective-permute-done.4.refs_0_.refs_2_, ...), custom_call_target="tpu_custom_call" | custom-call | flops 2113929216 | bytes 6553600 | tf_op jit(solution)/shard_map/pallas_call | solution.py:264
  64.0 1.3 %shard_map.43.refs_5_ = f32[12,8,384]{2,1,0:T(8,128)S(1)} custom-call(bf16[400,1024]{1,0:T(8,128)(2,1)S(1)} %collective-permute-done.11.refs_0_.refs_4_, bf16[400,1024]{1,0:T(8,128)(2,1)S(1)} %collective-permute-done.12.refs_2_.refs_4_.refs_1_, bf16[400,1024]{1,0:T(8,128)(2,1)S(1)} %collective-permute-done.4.refs_0_.refs_2_, ...), custom_call_target="tpu_custom_call" | custom-call | flops 905969664 | bytes 3276800 | tf_op jit(solution)/shard_map/pallas_call | solution.py:264
  65.3 1.1 %shard_map.44 = f32[128,128]{1,0:T(8,128)S(1)} custom-call(bf16[400,1024]{1,0:T(8,128)(2,1)S(1)} %collective-permute-done.5.refs_0_, bf16[400,1024]{1,0:T(8,128)(2,1)S(1)} %collective-permute-done.9.refs_4_.refs_6_.refs_1_, bf16[400,1024]{1,0:T(8,128)(2,1)S(1)} %collective-permute-done.10.refs_7_.refs_5_.refs_2_, ...), custom_call_target="tpu_custom_call" | custom-call | flops 1207959552 | bytes 4096000 | tf_op jit(solution)/shard_map/pallas_call | solution.py:264
  66.4 18.4 %all_to_all.11 = f32[128,1,128]{2,1,0:T(1,128)S(1)} all-to-all(f32[128,1,128]{2,1,0:T(1,128)S(1)} %bitcast.5), channel_id=1, replica_groups=mesh['clus'=8,'fold'=16] {'clus','fold'}, dimensions={0} | all-to-all | bytes 131072 | tf_op jit(solution)/shard_map/all_to_all | solution.py:376
  84.8 0.3 shard_map.45
  85.2 0.6 reduce
  (17 shorter events, 0.3 us)
Async XLA Ops:
  1.4 1.4 %copy-start = (bf16[768,1024]{1,0:T(8,128)(2,1)S(1)}, bf16[768,1024]{1,0:T(8,128)(2,1)}, u32[]{:S(2)}) copy-start(bf16[768,1024]{1,0:T(8,128)(2,1)} %emb_hbm.1) | copy-start | bytes 4718596
  5.4 4.3 %collective-permute-start.6 = (bf16[112,1024]{1,0:T(8,128)(2,1)S(1)}, bf16[112,1024]{1,0:T(8,128)(2,1)S(1)}, u32[]{:S(2)}, u32[]{:S(2)}) collective-permute-start(bf16[112,1024]{1,0:T(8,128)(2,1)S(1)} %get-tuple-element.20), channel_id=1, source_target_pairs={{0,16},{1,17},{2,18},{3,19},{4,20},{5,21},{6,22},{7,23},{8,24},{9,... | collective-permute-start | bytes 688136 | tf_op jit(solution)/shard_map/ppermute | solution.py:315
  6.9 7.1 %collective-permute-start.7 = (bf16[112,1024]{1,0:T(8,128)(2,1)S(1)}, bf16[112,1024]{1,0:T(8,128)(2,1)S(1)}, u32[]{:S(2)}, u32[]{:S(2)}) collective-permute-start(bf16[112,1024]{1,0:T(8,128)(2,1)S(1)} %get-tuple-element.21), channel_id=1, source_target_pairs={{0,32},{1,33},{2,34},{3,35},{4,36},{5,37},{6,38},{7,39},{8,40},{9,... | collective-permute-start | bytes 688136 | tf_op jit(solution)/shard_map/ppermute | solution.py:315
  8.3 7.6 %collective-permute-start.8 = (bf16[112,1024]{1,0:T(8,128)(2,1)S(1)}, bf16[112,1024]{1,0:T(8,128)(2,1)S(1)}, u32[]{:S(2)}, u32[]{:S(2)}) collective-permute-start(bf16[112,1024]{1,0:T(8,128)(2,1)S(1)} %get-tuple-element.22), channel_id=1, source_target_pairs={{0,20},{1,21},{2,22},{3,23},{4,24},{5,25},{6,26},{7,27},{8,28},{9,... | collective-permute-start | bytes 688136 | tf_op jit(solution)/shard_map/ppermute | solution.py:315
  16.0 17.8 %collective-permute-start.12 = (bf16[400,1024]{1,0:T(8,128)(2,1)S(1)}, bf16[400,1024]{1,0:T(8,128)(2,1)S(1)}, u32[]{:S(2)}, u32[]{:S(2)}) collective-permute-start(bf16[400,1024]{1,0:T(8,128)(2,1)S(1)} %shard_map.39.refs_0_.refs_1_.refs_7_), channel_id=1, source_target_pairs={{1,0},{2,1},{3,2},{0,3},{5,4},{6,5},{7,6},{4,7},{9,8},{10,9},{11,1... | collective-permute-start | bytes 2457608 | tf_op jit(solution)/shard_map/ppermute | solution.py:319
  17.7 9.2 %collective-permute-start = (bf16[112,1024]{1,0:T(8,128)(2,1)S(1)}, bf16[112,1024]{1,0:T(8,128)(2,1)S(1)}, u32[]{:S(2)}, u32[]{:S(2)}) collective-permute-start(bf16[112,1024]{1,0:T(8,128)(2,1)S(1)} %get-tuple-element.15), channel_id=1, source_target_pairs={{0,64},{1,65},{2,66},{3,67},{4,68},{5,69},{6,70},{7,71},{8,72},{9,... | collective-permute-start | bytes 688136 | tf_op jit(solution)/shard_map/ppermute | solution.py:315
  19.3 10.2 %collective-permute-start.1 = (bf16[112,1024]{1,0:T(8,128)(2,1)S(1)}, bf16[112,1024]{1,0:T(8,128)(2,1)S(1)}, u32[]{:S(2)}, u32[]{:S(2)}) collective-permute-start(bf16[112,1024]{1,0:T(8,128)(2,1)S(1)} %get-tuple-element.16), channel_id=1, source_target_pairs={{0,24},{1,25},{2,26},{3,27},{4,28},{5,29},{6,30},{7,31},{8,16},{9,... | collective-permute-start | bytes 688136 | tf_op jit(solution)/shard_map/ppermute | solution.py:315
  24.1 7.8 %collective-permute-start.2 = (bf16[112,1024]{1,0:T(8,128)(2,1)S(1)}, bf16[112,1024]{1,0:T(8,128)(2,1)S(1)}, u32[]{:S(2)}, u32[]{:S(2)}) collective-permute-start(bf16[112,1024]{1,0:T(8,128)(2,1)S(1)} %get-tuple-element.17), channel_id=1, source_target_pairs={{0,96},{1,97},{2,98},{3,99},{4,100},{5,101},{6,102},{7,103},{8,104... | collective-permute-start | bytes 688136 | tf_op jit(solution)/shard_map/ppermute | solution.py:315
  26.8 6.5 %collective-permute-start.3 = (bf16[112,1024]{1,0:T(8,128)(2,1)S(1)}, bf16[112,1024]{1,0:T(8,128)(2,1)S(1)}, u32[]{:S(2)}, u32[]{:S(2)}) collective-permute-start(bf16[112,1024]{1,0:T(8,128)(2,1)S(1)} %get-tuple-element.18), channel_id=1, source_target_pairs={{0,28},{1,29},{2,30},{3,31},{4,16},{5,17},{6,18},{7,19},{8,20},{9,... | collective-permute-start | bytes 688136 | tf_op jit(solution)/shard_map/ppermute | solution.py:315
  26.8 12.7 %collective-permute-start.9 = (bf16[400,1024]{1,0:T(8,128)(2,1)S(1)}, bf16[400,1024]{1,0:T(8,128)(2,1)S(1)}, u32[]{:S(2)}, u32[]{:S(2)}) collective-permute-start(bf16[400,1024]{1,0:T(8,128)(2,1)S(1)} %shard_map.39.refs_0_.refs_1_.refs_7_), channel_id=1, source_target_pairs={{12,0},{13,1},{14,2},{15,3},{0,4},{1,5},{2,6},{3,7},{4,8},{5,9},{6... | collective-permute-start | bytes 2457608 | tf_op jit(solution)/shard_map/ppermute | solution.py:321
  29.6 13.5 %collective-permute-start.14 = (bf16[400,1024]{1,0:T(8,128)(2,1)S(1)}, bf16[400,1024]{1,0:T(8,128)(2,1)S(1)}, u32[]{:S(2)}, u32[]{:S(2)}) collective-permute-start(bf16[400,1024]{1,0:T(8,128)(2,1)S(1)} %shard_map.39.refs_0_.refs_1_.refs_7_), channel_id=1, source_target_pairs={{4,0},{5,1},{6,2},{7,3},{8,4},{9,5},{10,6},{11,7},{12,8},{13,9},{1... | collective-permute-start | bytes 2457608 | tf_op jit(solution)/shard_map/ppermute | solution.py:320
  33.4 14.9 %collective-permute-start.10 = (bf16[400,1024]{1,0:T(8,128)(2,1)S(1)}, bf16[400,1024]{1,0:T(8,128)(2,1)S(1)}, u32[]{:S(2)}, u32[]{:S(2)}) collective-permute-start(bf16[400,1024]{1,0:T(8,128)(2,1)S(1)} %shard_map.38.refs_1_.refs_2_.refs_6_.refs_3_), channel_id=1, source_target_pairs={{12,0},{13,1},{14,2},{15,3},{0,4},{1,5},{2,6},{3,7},{4,8},{5,9},{6... | collective-permute-start | bytes 2457608 | tf_op jit(solution)/shard_map/ppermute | solution.py:321
  33.7 14.6 %collective-permute-start.4 = (bf16[400,1024]{1,0:T(8,128)(2,1)S(1)}, bf16[400,1024]{1,0:T(8,128)(2,1)S(1)}, u32[]{:S(2)}, u32[]{:S(2)}) collective-permute-start(bf16[400,1024]{1,0:T(8,128)(2,1)S(1)} %shard_map.38.refs_1_.refs_2_.refs_6_.refs_3_), channel_id=1, source_target_pairs={{1,0},{2,1},{3,2},{0,3},{5,4},{6,5},{7,6},{4,7},{9,8},{10,9},{11,1... | collective-permute-start | bytes 2457608 | tf_op jit(solution)/shard_map/ppermute | solution.py:319
  33.8 18.4 %collective-permute-start.16 = (bf16[400,1024]{1,0:T(8,128)(2,1)S(1)}, bf16[400,1024]{1,0:T(8,128)(2,1)S(1)}, u32[]{:S(2)}, u32[]{:S(2)}) collective-permute-start(bf16[400,1024]{1,0:T(8,128)(2,1)S(1)} %shard_map.38.refs_1_.refs_2_.refs_6_.refs_3_), channel_id=1, source_target_pairs={{4,0},{5,1},{6,2},{7,3},{8,4},{9,5},{10,6},{11,7},{12,8},{13,9},{1... | collective-permute-start | bytes 2457608 | tf_op jit(solution)/shard_map/ppermute | solution.py:320
  39.5 17.6 %collective-permute-start.13 = (bf16[400,1024]{1,0:T(8,128)(2,1)S(1)}, bf16[400,1024]{1,0:T(8,128)(2,1)S(1)}, u32[]{:S(2)}, u32[]{:S(2)}) collective-permute-start(bf16[400,1024]{1,0:T(8,128)(2,1)S(1)} %collective-permute-done.12.refs_2_.refs_4_.refs_1_), channel_id=1, source_target_pairs={{1,0},{2,1},{3,2},{0,3},{5,4},{6,5},{7,6},{4,7},{9,8},{10,9},{11,1... | collective-permute-start | bytes 2457608 | tf_op jit(solution)/shard_map/ppermute | solution.py:322
  43.1 17.6 %collective-permute-start.15 = (bf16[400,1024]{1,0:T(8,128)(2,1)S(1)}, bf16[400,1024]{1,0:T(8,128)(2,1)S(1)}, u32[]{:S(2)}, u32[]{:S(2)}) collective-permute-start(bf16[400,1024]{1,0:T(8,128)(2,1)S(1)} %collective-permute-done.14.refs_3_.refs_5_), channel_id=1, source_target_pairs={{4,0},{5,1},{6,2},{7,3},{8,4},{9,5},{10,6},{11,7},{12,8},{13,9},{1... | collective-permute-start | bytes 2457608 | tf_op jit(solution)/shard_map/ppermute | solution.py:323
  48.3 15.6 %collective-permute-start.11 = (bf16[400,1024]{1,0:T(8,128)(2,1)S(1)}, bf16[400,1024]{1,0:T(8,128)(2,1)S(1)}, u32[]{:S(2)}, u32[]{:S(2)}) collective-permute-start(bf16[400,1024]{1,0:T(8,128)(2,1)S(1)} %collective-permute-done.10.refs_7_.refs_5_.refs_2_), channel_id=1, source_target_pairs={{12,0},{13,1},{14,2},{15,3},{0,4},{1,5},{2,6},{3,7},{4,8},{5,9},{6... | collective-permute-start | bytes 2457608 | tf_op jit(solution)/shard_map/ppermute | solution.py:324
  48.3 17.0 %collective-permute-start.5 = (bf16[400,1024]{1,0:T(8,128)(2,1)S(1)}, bf16[400,1024]{1,0:T(8,128)(2,1)S(1)}, u32[]{:S(2)}, u32[]{:S(2)}) collective-permute-start(bf16[400,1024]{1,0:T(8,128)(2,1)S(1)} %collective-permute-done.4.refs_0_.refs_2_), channel_id=1, source_target_pairs={{1,0},{2,1},{3,2},{0,3},{5,4},{6,5},{7,6},{4,7},{9,8},{10,9},{11,1... | collective-permute-start | bytes 2457608 | tf_op jit(solution)/shard_map/ppermute | solution.py:322

commit v3 on v2

--- a/solution.py
+++ b/solution.py
@@ -23,6 +23,7 @@
 FAR = 1.0e6
 WIDE = 256
 CHUNK = 256
+SHOWN = 8
 VMEM = 12 * 1024 * 1024
 OWN, UP, RIGHT, LEFT, OVER, UP2 = range(6)
 OFFSETS = ((0, 0), (0, 1), (1, 0), (3, 0), (2, 0), (0, 2))
@@ -67,19 +68,25 @@
     return pltpu.CompilerParams(vmem_limit_bytes=VMEM)
 
 
-def pack_kernel(emb_hbm, labels_ref, ordinals_ref, slot_ref, *refs):
-    piece_refs, (emb, unit, sems) = refs[:PIECES], refs[PIECES:]
+def pack_kernel(emb_hbm, labels_hbm, ordinals_hbm, slot_ref, *refs):
+    piece_refs, (emb, labels_ref, ordinals_ref, unit, sems) = refs[:PIECES], refs[PIECES:]
+    firsts = [
+        pltpu.make_async_copy(labels_hbm, labels_ref, sems.at[0]),
+        pltpu.make_async_copy(ordinals_hbm, ordinals_ref, sems.at[1]),
+    ]
     copies = [
         pltpu.make_async_copy(
-            emb_hbm.at[pl.ds(i, CHUNK)], emb.at[pl.ds(i, CHUNK)], sems.at[i // CHUNK]
+            emb_hbm.at[pl.ds(i, CHUNK)], emb.at[pl.ds(i, CHUNK)], sems.at[2 + i // CHUNK]
         )
         for i in range(0, ROWS, CHUNK)
     ]
-    for copy in copies:
+    for copy in firsts + copies:
         copy.start()
-    clus, fold = lax.axis_index("clus"), lax.axis_index("fold")
-    core, x, y = clus % 2, clus // 2, fold // RING
-    labels, ordinals = labels_ref[...], ordinals_ref[...]
+    for copy in firsts:
+        copy.wait()
+    x, core, y, _ = where_am_i()
+    labels = labels_ref[...].reshape(1, ROWS)
+    ordinals = ordinals_ref[...].reshape(1, ROWS)
     kind = labels // RING
     coordinate = jnp.where(kind == 0, x, y)
     offset = (labels % RING - coordinate + RING) % RING
@@ -126,19 +133,22 @@
 
 
 def pack(embeddings, labels, ordinals):
+    given = [pltpu.with_memory_space_constraint(v, pltpu.HBM) for v in (embeddings, labels, ordinals)]
     return pl.pallas_call(
         pack_kernel,
         out_shape=[jax.ShapeDtypeStruct((1, ROWS), jnp.int32)]
         + [jax.ShapeDtypeStruct((PIECE_ROWS, EMB), jnp.bfloat16)] * PIECES,
-        in_specs=[pl.BlockSpec(memory_space=pl.ANY)] + whole(2),
+        in_specs=[pl.BlockSpec(memory_space=pltpu.HBM)] * 3,
         out_specs=whole(1 + PIECES),
         scratch_shapes=[
             pltpu.VMEM((ROWS, EMB), jnp.bfloat16),
+            pltpu.VMEM((ROWS,), jnp.int32),
+            pltpu.VMEM((ROWS,), jnp.int32),
             pltpu.VMEM((ROWS, EMB), jnp.bfloat16),
-            pltpu.SemaphoreType.DMA((ROWS // CHUNK,)),
+            pltpu.SemaphoreType.DMA((2 + ROWS // CHUNK,)),
         ],
         compiler_params=params(),
-    )(embeddings, labels.reshape(1, ROWS), ordinals.reshape(1, ROWS))
+    )(*given)
 
 
 def join_kernel(*refs):
@@ -270,7 +280,7 @@
         + [pltpu.VMEM((firsts, HALF, LANES), jnp.float32)] * 2,
         compiler_params=params(),
         cost_estimate=pl.CostEstimate(
-            flops=int(2 * products * ROWS * ROWS * EMB),
+            flops=int(SHOWN * products * ROWS * ROWS * EMB),
             bytes_accessed=len(names) * HALF_ROWS * EMB * 2,
             transcendentals=0,
         ),
@@ -296,17 +306,17 @@
             chosen = jnp.where(rows == slot[:, k : k + LANES], column, -1.0)
             best.append(jnp.max(chosen.reshape(PIECE // 8, 8, LANES), axis=0))
         found = jnp.maximum(found, jnp.concatenate(best, axis=1))
-    out_ref[...] = jnp.max(found, axis=0, keepdims=True)
+    out_ref[...] = jnp.max(found, axis=0)
 
 
 def unpack(slot, got):
     return pl.pallas_call(
         unpack_kernel,
-        out_shape=jax.ShapeDtypeStruct((1, ROWS), jnp.float32),
+        out_shape=jax.ShapeDtypeStruct((ROWS,), jnp.float32),
         in_specs=whole(2),
         out_specs=whole(1)[0],
         compiler_params=params(),
-    )(slot, got).reshape(ROWS)
+    )(slot, got)
 
 
 def per_device(embeddings, labels, ordinals):

time: 86 us -> 77.9 us (0.906)
  waiting for transfers between devices: 24.8 us -> 14.3 us
  starting transfers between devices: 21.4 us -> 24.6 us
  local copies, waits for them, and re-layouts: 2.79 us -> 0 us
  blocking collectives: 18.4 us -> 19.9 us
  Pallas kernels: 17.6 us -> 18.9 us
    ppermute x7, waiting for transfers between devices: 11.5 us -> 1.59 us  [per_device(): send(pieces[s], perm=packet_pairs(s))]
    ppermute x2, waiting for transfers between devices: 0.01 us -> 5.1 us  [per_device(): held[UP, h] = send(held[OWN, h], perm=block_pairs(0, 1))]
    ppermute x2, waiting for transfers between devices: 3.53 us -> 0.01 us  [per_device(): held[RIGHT, h] = send(held[OWN, h], perm=block_pairs(1, 0))]
    ppermute x1, waiting for transfers between devices: 3.49 us -> 0.01 us  [per_device(): held[OVER, 0] = send(held[RIGHT, 0], perm=block_pairs(1, 0))]
    ppermute x2, starting transfers between devices: 0.01 us -> 3.28 us  [per_device(): held[UP2, h] = send(held[UP, h], perm=block_pairs(0, 1))]
    ppermute x2, starting transfers between devices: 1.8 us -> 3.48 us  [per_device(): held[UP, h] = send(held[OWN, h], perm=block_pairs(0, 1))]
    ppermute x2, starting transfers between devices: 0.3 us -> 1.78 us  [per_device(): held[LEFT, h] = send(held[OWN, h], perm=block_pairs(3, 0))]
    all_to_all x1, blocking collectives: 18.4 us -> 19.9 us  [per_device(): got = lax.all_to_all(sent, AXES, split_axis=0, concat_axis=0, tiled=True)]
  transfers between devices with their start and end apart: 17 -> 17, of which waited for: 9 -> 4; matrix products, arithmetic and copies ran while one was open for 0% -> 0% of each run, Pallas kernels for 16% -> 18%
where the time goes in v3:
time: 77.9 us; the launch traced here: 77.7 us
  starting transfers between devices  24.6 us (32%)
  blocking collectives  19.9 us (26%)
  Pallas kernels  18.9 us (24%)
  waiting for transfers between devices  14.3 us (18%)
    all_to_all x1, blocking collectives, per_device(): got = lax.all_to_all(sent, AXES, split_axis=0, concat_axis=0, tiled=True)  19.9 us
    pallas_call x5, Pallas kernels, meet(): pl.pallas_call(functools.partial(meet_kernel, names, steps, before is not...  14.6 us
    ppermute x7, starting transfers between devices, per_device(): send(pieces[s], perm=packet_pairs(s))  12.4 us
    ppermute x2, waiting for transfers between devices, per_device(): held[LEFT, h] = send(held[OWN, h], perm=block_pairs(3, 0))  7.55 us
    ppermute x2, waiting for transfers between devices, per_device(): held[UP, h] = send(held[OWN, h], perm=block_pairs(0, 1))  5.1 us
    ppermute x2, starting transfers between devices, per_device(): held[UP, h] = send(held[OWN, h], perm=block_pairs(0, 1))  3.48 us
    ppermute x2, starting transfers between devices, per_device(): held[UP2, h] = send(held[UP, h], perm=block_pairs(0, 1))  3.28 us
    pallas_call x1, Pallas kernels, pack(): pl.pallas_call(pack_kernel, out_shape=[jax.ShapeDtypeStruct((1, ROWS), jn...  3.24 us
  transfers between devices with their start and end apart: 17, of which 4 were waited for; matrix products, arithmetic and copies ran while one was open for 0% of the time, Pallas kernels for 18%

profile of v3, /device:TPU:1, one launch (start us, length us, event | category | flops | bytes accessed | tf_op | source)
XLA Modules:
  0.0 77.7 jit_solution(548825411763493873)
XLA Ops:
  0.0 3.2 %shard_map.37 = (s32[1,768]{1,0:T(1,128)S(1)}, bf16[112,1024]{1,0:T(8,128)(2,1)S(1)}, bf16[112,1024]{1,0:T(8,128)(2,1)S(1)}, bf16[112,1024]{1,0:T(8,128)(2,1)S(1...) custom-call(bf16[768,1024]{1,0:T(8,128)(2,1)} %emb_hbm.1, ...), custom_call_target="tpu_custom_call" | custom-call | tf_op jit(solution)/shard_map/pallas_call | solution.py:137
  3.2 1.5 %collective-permute-start.6 = (bf16[112,1024]{1,0:T(8,128)(2,1)S(1)}, bf16[112,1024]{1,0:T(8,128)(2,1)S(1)}, u32[]{:S(2)}, u32[]{:S(2)}) collective-permute-start(bf16[112,1024]{1,0:T(8,128)(2,1)S(1)} %get-tuple-element.20), channel_id=1, source_target_pairs={{0,16},{1,17},{2,18},{3,19},{4,20},{5,21},{6,22},{7,23},{8,24},{9,... | collective-permute-start | bytes 688136 | tf_op jit(solution)/shard_map/ppermute | solution.py:325
  4.8 1.4 %collective-permute-start.7 = (bf16[112,1024]{1,0:T(8,128)(2,1)S(1)}, bf16[112,1024]{1,0:T(8,128)(2,1)S(1)}, u32[]{:S(2)}, u32[]{:S(2)}) collective-permute-start(bf16[112,1024]{1,0:T(8,128)(2,1)S(1)} %get-tuple-element.21), channel_id=1, source_target_pairs={{0,32},{1,33},{2,34},{3,35},{4,36},{5,37},{6,38},{7,39},{8,40},{9,... | collective-permute-start | bytes 688136 | tf_op jit(solution)/shard_map/ppermute | solution.py:325
  6.1 1.4 %collective-permute-start.8 = (bf16[112,1024]{1,0:T(8,128)(2,1)S(1)}, bf16[112,1024]{1,0:T(8,128)(2,1)S(1)}, u32[]{:S(2)}, u32[]{:S(2)}) collective-permute-start(bf16[112,1024]{1,0:T(8,128)(2,1)S(1)} %get-tuple-element.22), channel_id=1, source_target_pairs={{0,20},{1,21},{2,22},{3,23},{4,24},{5,25},{6,26},{7,27},{8,28},{9,... | collective-permute-start | bytes 688136 | tf_op jit(solution)/shard_map/ppermute | solution.py:325
  7.5 2.9 %collective-permute-start = (bf16[112,1024]{1,0:T(8,128)(2,1)S(1)}, bf16[112,1024]{1,0:T(8,128)(2,1)S(1)}, u32[]{:S(2)}, u32[]{:S(2)}) collective-permute-start(bf16[112,1024]{1,0:T(8,128)(2,1)S(1)} %get-tuple-element.15), channel_id=1, source_target_pairs={{0,64},{1,65},{2,66},{3,67},{4,68},{5,69},{6,70},{7,71},{8,72},{9,... | collective-permute-start | bytes 688136 | tf_op jit(solution)/shard_map/ppermute | solution.py:325
  10.4 0.5 collective-permute-start.1
  11.0 1.4 %collective-permute-start.2 = (bf16[112,1024]{1,0:T(8,128)(2,1)S(1)}, bf16[112,1024]{1,0:T(8,128)(2,1)S(1)}, u32[]{:S(2)}, u32[]{:S(2)}) collective-permute-start(bf16[112,1024]{1,0:T(8,128)(2,1)S(1)} %get-tuple-element.17), channel_id=1, source_target_pairs={{0,96},{1,97},{2,98},{3,99},{4,100},{5,101},{6,102},{7,103},{8,104... | collective-permute-start | bytes 688136 | tf_op jit(solution)/shard_map/ppermute | solution.py:325
  12.3 0.0 collective-permute-done.7.refs_2_
  12.3 3.3 %collective-permute-start.3 = (bf16[112,1024]{1,0:T(8,128)(2,1)S(1)}, bf16[112,1024]{1,0:T(8,128)(2,1)S(1)}, u32[]{:S(2)}, u32[]{:S(2)}) collective-permute-start(bf16[112,1024]{1,0:T(8,128)(2,1)S(1)} %get-tuple-element.18), channel_id=1, source_target_pairs={{0,28},{1,29},{2,30},{3,31},{4,16},{5,17},{6,18},{7,19},{8,20},{9,... | collective-permute-start | bytes 688136 | tf_op jit(solution)/shard_map/ppermute | solution.py:325
  15.6 0.1 shard_map.39.refs_0_.refs_1_.refs_7_
  15.7 1.8 %collective-permute-start.12 = (bf16[400,1024]{1,0:T(8,128)(2,1)S(1)}, bf16[400,1024]{1,0:T(8,128)(2,1)S(1)}, u32[]{:S(2)}, u32[]{:S(2)}) collective-permute-start(bf16[400,1024]{1,0:T(8,128)(2,1)S(1)} %shard_map.39.refs_0_.refs_1_.refs_7_), channel_id=1, source_target_pairs={{1,0},{2,1},{3,2},{0,3},{5,4},{6,5},{7,6},{4,7},{9,8},{10,9},{11,1... | collective-permute-start | bytes 2457608 | tf_op jit(solution)/shard_map/ppermute | solution.py:329
  17.5 1.6 %collective-permute-done.refs_0_ = bf16[112,1024]{1,0:T(8,128)(2,1)S(1)} collective-permute-done((bf16[112,1024]{1,0:T(8,128)(2,1)S(1)}, bf16[112,1024]{1,0:T(8,128)(2,1)S(1)}, u32[]{:S(2)}, u32[]{:S(2)}) %collective-permute-start) | collective-permute-done | bytes 229408 | tf_op jit(solution)/shard_map/ppermute | solution.py:325
  19.1 0.9 %collective-permute-start.9 = (bf16[400,1024]{1,0:T(8,128)(2,1)S(1)}, bf16[400,1024]{1,0:T(8,128)(2,1)S(1)}, u32[]{:S(2)}, u32[]{:S(2)}) collective-permute-start(bf16[400,1024]{1,0:T(8,128)(2,1)S(1)} %shard_map.39.refs_0_.refs_1_.refs_7_), channel_id=1, source_target_pairs={{12,0},{13,1},{14,2},{15,3},{0,4},{1,5},{2,6},{3,7},{4,8},{5,9},{6... | collective-permute-start | bytes 2457608 | tf_op jit(solution)/shard_map/ppermute | solution.py:331
  20.0 0.0 collective-permute-done.1.refs_1_
  20.0 2.0 %collective-permute-start.14 = (bf16[400,1024]{1,0:T(8,128)(2,1)S(1)}, bf16[400,1024]{1,0:T(8,128)(2,1)S(1)}, u32[]{:S(2)}, u32[]{:S(2)}) collective-permute-start(bf16[400,1024]{1,0:T(8,128)(2,1)S(1)} %shard_map.39.refs_0_.refs_1_.refs_7_), channel_id=1, source_target_pairs={{4,0},{5,1},{6,2},{7,3},{8,4},{9,5},{10,6},{11,7},{12,8},{13,9},{1... | collective-permute-start | bytes 2457608 | tf_op jit(solution)/shard_map/ppermute | solution.py:330
  22.0 0.1 shard_map.38.refs_1_.refs_2_.refs_6_.refs_3_
  22.1 0.9 %collective-permute-start.10 = (bf16[400,1024]{1,0:T(8,128)(2,1)S(1)}, bf16[400,1024]{1,0:T(8,128)(2,1)S(1)}, u32[]{:S(2)}, u32[]{:S(2)}) collective-permute-start(bf16[400,1024]{1,0:T(8,128)(2,1)S(1)} %shard_map.38.refs_1_.refs_2_.refs_6_.refs_3_), channel_id=1, source_target_pairs={{12,0},{13,1},{14,2},{15,3},{0,4},{1,5},{2,6},{3,7},{4,8},{5,9},{6... | collective-permute-start | bytes 2457608 | tf_op jit(solution)/shard_map/ppermute | solution.py:331
  22.9 1.6 %collective-permute-start.4 = (bf16[400,1024]{1,0:T(8,128)(2,1)S(1)}, bf16[400,1024]{1,0:T(8,128)(2,1)S(1)}, u32[]{:S(2)}, u32[]{:S(2)}) collective-permute-start(bf16[400,1024]{1,0:T(8,128)(2,1)S(1)} %shard_map.38.refs_1_.refs_2_.refs_6_.refs_3_), channel_id=1, source_target_pairs={{1,0},{2,1},{3,2},{0,3},{5,4},{6,5},{7,6},{4,7},{9,8},{10,9},{11,1... | collective-permute-start | bytes 2457608 | tf_op jit(solution)/shard_map/ppermute | solution.py:329
  24.6 5.1 %collective-permute-done.12.refs_2_.refs_4_.refs_1_ = bf16[400,1024]{1,0:T(8,128)(2,1)S(1)} collective-permute-done((bf16[400,1024]{1,0:T(8,128)(2,1)S(1)}, bf16[400,1024]{1,0:T(8,128)(2,1)S(1)}, u32[]{:S(2)}, u32[]{:S(2)}) %collective-permute-start.12) | collective-permute-done | bytes 819232 | tf_op jit(solution)/shard_map/ppermute | solution.py:329
  29.7 0.4 collective-permute-start.16
  30.1 1.7 %collective-permute-done.9.refs_4_.refs_6_.refs_1_ = bf16[400,1024]{1,0:T(8,128)(2,1)S(1)} collective-permute-done((bf16[400,1024]{1,0:T(8,128)(2,1)S(1)}, bf16[400,1024]{1,0:T(8,128)(2,1)S(1)}, u32[]{:S(2)}, u32[]{:S(2)}) %collective-permute-start.9) | collective-permute-done | bytes 819232 | tf_op jit(solution)/shard_map/ppermute | solution.py:331
  31.8 1.6 %collective-permute-start.13 = (bf16[400,1024]{1,0:T(8,128)(2,1)S(1)}, bf16[400,1024]{1,0:T(8,128)(2,1)S(1)}, u32[]{:S(2)}, u32[]{:S(2)}) collective-permute-start(bf16[400,1024]{1,0:T(8,128)(2,1)S(1)} %collective-permute-done.12.refs_2_.refs_4_.refs_1_), channel_id=1, source_target_pairs={{1,0},{2,1},{3,2},{0,3},{5,4},{6,5},{7,6},{4,7},{9,8},{10,9},{11,1... | collective-permute-start | bytes 2457608 | tf_op jit(solution)/shard_map/ppermute | solution.py:332
  33.4 1.3 %collective-permute-start.15 = (bf16[400,1024]{1,0:T(8,128)(2,1)S(1)}, bf16[400,1024]{1,0:T(8,128)(2,1)S(1)}, u32[]{:S(2)}, u32[]{:S(2)}) collective-permute-start(bf16[400,1024]{1,0:T(8,128)(2,1)S(1)} %collective-permute-done.14.refs_3_.refs_5_), channel_id=1, source_target_pairs={{4,0},{5,1},{6,2},{7,3},{8,4},{9,5},{10,6},{11,7},{12,8},{13,9},{1... | collective-permute-start | bytes 2457608 | tf_op jit(solution)/shard_map/ppermute | solution.py:333
  34.7 5.9 %collective-permute-done.10.refs_7_.refs_5_.refs_2_ = bf16[400,1024]{1,0:T(8,128)(2,1)S(1)} collective-permute-done((bf16[400,1024]{1,0:T(8,128)(2,1)S(1)}, bf16[400,1024]{1,0:T(8,128)(2,1)S(1)}, u32[]{:S(2)}, u32[]{:S(2)}) %collective-permute-start.10) | collective-permute-done | bytes 819232 | tf_op jit(solution)/shard_map/ppermute | solution.py:331
  40.6 1.6 %collective-permute-start.5 = (bf16[400,1024]{1,0:T(8,128)(2,1)S(1)}, bf16[400,1024]{1,0:T(8,128)(2,1)S(1)}, u32[]{:S(2)}, u32[]{:S(2)}) collective-permute-start(bf16[400,1024]{1,0:T(8,128)(2,1)S(1)} %collective-permute-done.4.refs_0_.refs_2_), channel_id=1, source_target_pairs={{1,0},{2,1},{3,2},{0,3},{5,4},{6,5},{7,6},{4,7},{9,8},{10,9},{11,1... | collective-permute-start | bytes 2457608 | tf_op jit(solution)/shard_map/ppermute | solution.py:332
  42.2 3.8 %shard_map.40.refs_8_ = f32[12,8,384]{2,1,0:T(8,128)S(1)} custom-call(bf16[400,1024]{1,0:T(8,128)(2,1)S(1)} %shard_map.39.refs_0_.refs_1_.refs_7_, bf16[400,1024]{1,0:T(8,128)(2,1)S(1)} %shard_map.38.refs_1_.refs_2_.refs_6_.refs_3_, bf16[400,1024]{1,0:T(8,128)(2,1)S(1)} %collective-permute-done.12.refs_2_.refs_4_.refs_1_, ...), custom_call_target="tpu_custom_call" | custom-call | flops 10871635968 | bytes 4096000 | tf_op jit(solution)/shard_map/pallas_call | solution.py:274
  46.1 5.0 %shard_map.41.refs_8_ = f32[12,8,384]{2,1,0:T(8,128)S(1)} custom-call(bf16[400,1024]{1,0:T(8,128)(2,1)S(1)} %collective-permute-done.4.refs_0_.refs_2_, bf16[400,1024]{1,0:T(8,128)(2,1)S(1)} %shard_map.39.refs_0_.refs_1_.refs_7_, bf16[400,1024]{1,0:T(8,128)(2,1)S(1)} %shard_map.38.refs_1_.refs_2_.refs_6_.refs_3_, ...), custom_call_target="tpu_custom_call" | custom-call | flops 16911433728 | bytes 6553600 | tf_op jit(solution)/shard_map/pallas_call | solution.py:274
  51.1 3.4 %shard_map.42.refs_4_ = f32[12,8,384]{2,1,0:T(8,128)S(1)} custom-call(bf16[400,1024]{1,0:T(8,128)(2,1)S(1)} %collective-permute-done.15.refs_0_, bf16[400,1024]{1,0:T(8,128)(2,1)S(1)} %collective-permute-done.12.refs_2_.refs_4_.refs_1_, bf16[400,1024]{1,0:T(8,128)(2,1)S(1)} %collective-permute-done.4.refs_0_.refs_2_, ...), custom_call_target="tpu_custom_call" | custom-call | flops 8455716864 | bytes 6553600 | tf_op jit(solution)/shard_map/pallas_call | solution.py:274
  54.5 1.3 %shard_map.43.refs_5_ = f32[12,8,384]{2,1,0:T(8,128)S(1)} custom-call(bf16[400,1024]{1,0:T(8,128)(2,1)S(1)} %collective-permute-done.11.refs_0_.refs_4_, bf16[400,1024]{1,0:T(8,128)(2,1)S(1)} %collective-permute-done.12.refs_2_.refs_4_.refs_1_, bf16[400,1024]{1,0:T(8,128)(2,1)S(1)} %collective-permute-done.4.refs_0_.refs_2_, ...), custom_call_target="tpu_custom_call" | custom-call | flops 3623878656 | bytes 3276800 | tf_op jit(solution)/shard_map/pallas_call | solution.py:274
  55.9 1.1 %shard_map.44 = f32[128,128]{1,0:T(8,128)S(1)} custom-call(bf16[400,1024]{1,0:T(8,128)(2,1)S(1)} %collective-permute-done.5.refs_0_, bf16[400,1024]{1,0:T(8,128)(2,1)S(1)} %collective-permute-done.9.refs_4_.refs_6_.refs_1_, bf16[400,1024]{1,0:T(8,128)(2,1)S(1)} %collective-permute-done.10.refs_7_.refs_5_.refs_2_, ...), custom_call_target="tpu_custom_call" | custom-call | flops 4831838208 | bytes 4096000 | tf_op jit(solution)/shard_map/pallas_call | solution.py:274
  56.9 19.9 %all_to_all.11 = f32[128,1,128]{2,1,0:T(1,128)S(1)} all-to-all(f32[128,1,128]{2,1,0:T(1,128)S(1)} %bitcast.5), channel_id=1, replica_groups=mesh['clus'=8,'fold'=16] {'clus','fold'}, dimensions={0} | all-to-all | bytes 131072 | tf_op jit(solution)/shard_map/all_to_all | solution.py:386
  76.8 0.9 %shard_map.45 = f32[768]{0:T(1024)} custom-call(s32[1,768]{1,0:T(1,128)S(1)} %get-tuple-element.14.slot_ref, f32[128,128]{1,0:T(8,128)S(1)} %bitcast.4), custom_call_target="tpu_custom_call" | custom-call | tf_op jit(solution)/shard_map/pallas_call | solution.py:313
  (12 shorter events, 0.0 us)
Async XLA Ops:
  3.2 7.7 %collective-permute-start.6 = (bf16[112,1024]{1,0:T(8,128)(2,1)S(1)}, bf16[112,1024]{1,0:T(8,128)(2,1)S(1)}, u32[]{:S(2)}, u32[]{:S(2)}) collective-permute-start(bf16[112,1024]{1,0:T(8,128)(2,1)S(1)} %get-tuple-element.20), channel_id=1, source_target_pairs={{0,16},{1,17},{2,18},{3,19},{4,20},{5,21},{6,22},{7,23},{8,24},{9,... | collective-permute-start | bytes 688136 | tf_op jit(solution)/shard_map/ppermute | solution.py:325
  4.8 7.6 %collective-permute-start.7 = (bf16[112,1024]{1,0:T(8,128)(2,1)S(1)}, bf16[112,1024]{1,0:T(8,128)(2,1)S(1)}, u32[]{:S(2)}, u32[]{:S(2)}) collective-permute-start(bf16[112,1024]{1,0:T(8,128)(2,1)S(1)} %get-tuple-element.21), channel_id=1, source_target_pairs={{0,32},{1,33},{2,34},{3,35},{4,36},{5,37},{6,38},{7,39},{8,40},{9,... | collective-permute-start | bytes 688136 | tf_op jit(solution)/shard_map/ppermute | solution.py:325
  6.1 9.5 %collective-permute-start.8 = (bf16[112,1024]{1,0:T(8,128)(2,1)S(1)}, bf16[112,1024]{1,0:T(8,128)(2,1)S(1)}, u32[]{:S(2)}, u32[]{:S(2)}) collective-permute-start(bf16[112,1024]{1,0:T(8,128)(2,1)S(1)} %get-tuple-element.22), channel_id=1, source_target_pairs={{0,20},{1,21},{2,22},{3,23},{4,24},{5,25},{6,26},{7,27},{8,28},{9,... | collective-permute-start | bytes 688136 | tf_op jit(solution)/shard_map/ppermute | solution.py:325
  7.5 11.6 %collective-permute-start = (bf16[112,1024]{1,0:T(8,128)(2,1)S(1)}, bf16[112,1024]{1,0:T(8,128)(2,1)S(1)}, u32[]{:S(2)}, u32[]{:S(2)}) collective-permute-start(bf16[112,1024]{1,0:T(8,128)(2,1)S(1)} %get-tuple-element.15), channel_id=1, source_target_pairs={{0,64},{1,65},{2,66},{3,67},{4,68},{5,69},{6,70},{7,71},{8,72},{9,... | collective-permute-start | bytes 688136 | tf_op jit(solution)/shard_map/ppermute | solution.py:325
  10.4 9.6 %collective-permute-start.1 = (bf16[112,1024]{1,0:T(8,128)(2,1)S(1)}, bf16[112,1024]{1,0:T(8,128)(2,1)S(1)}, u32[]{:S(2)}, u32[]{:S(2)}) collective-permute-start(bf16[112,1024]{1,0:T(8,128)(2,1)S(1)} %get-tuple-element.16), channel_id=1, source_target_pairs={{0,24},{1,25},{2,26},{3,27},{4,28},{5,29},{6,30},{7,31},{8,16},{9,... | collective-permute-start | bytes 688136 | tf_op jit(solution)/shard_map/ppermute | solution.py:325
  11.0 11.1 %collective-permute-start.2 = (bf16[112,1024]{1,0:T(8,128)(2,1)S(1)}, bf16[112,1024]{1,0:T(8,128)(2,1)S(1)}, u32[]{:S(2)}, u32[]{:S(2)}) collective-permute-start(bf16[112,1024]{1,0:T(8,128)(2,1)S(1)} %get-tuple-element.17), channel_id=1, source_target_pairs={{0,96},{1,97},{2,98},{3,99},{4,100},{5,101},{6,102},{7,103},{8,104... | collective-permute-start | bytes 688136 | tf_op jit(solution)/shard_map/ppermute | solution.py:325
  12.3 9.7 %collective-permute-start.3 = (bf16[112,1024]{1,0:T(8,128)(2,1)S(1)}, bf16[112,1024]{1,0:T(8,128)(2,1)S(1)}, u32[]{:S(2)}, u32[]{:S(2)}) collective-permute-start(bf16[112,1024]{1,0:T(8,128)(2,1)S(1)} %get-tuple-element.18), channel_id=1, source_target_pairs={{0,28},{1,29},{2,30},{3,31},{4,16},{5,17},{6,18},{7,19},{8,20},{9,... | collective-permute-start | bytes 688136 | tf_op jit(solution)/shard_map/ppermute | solution.py:325
  15.7 14.0 %collective-permute-start.12 = (bf16[400,1024]{1,0:T(8,128)(2,1)S(1)}, bf16[400,1024]{1,0:T(8,128)(2,1)S(1)}, u32[]{:S(2)}, u32[]{:S(2)}) collective-permute-start(bf16[400,1024]{1,0:T(8,128)(2,1)S(1)} %shard_map.39.refs_0_.refs_1_.refs_7_), channel_id=1, source_target_pairs={{1,0},{2,1},{3,2},{0,3},{5,4},{6,5},{7,6},{4,7},{9,8},{10,9},{11,1... | collective-permute-start | bytes 2457608 | tf_op jit(solution)/shard_map/ppermute | solution.py:329
  19.1 12.7 %collective-permute-start.9 = (bf16[400,1024]{1,0:T(8,128)(2,1)S(1)}, bf16[400,1024]{1,0:T(8,128)(2,1)S(1)}, u32[]{:S(2)}, u32[]{:S(2)}) collective-permute-start(bf16[400,1024]{1,0:T(8,128)(2,1)S(1)} %shard_map.39.refs_0_.refs_1_.refs_7_), channel_id=1, source_target_pairs={{12,0},{13,1},{14,2},{15,3},{0,4},{1,5},{2,6},{3,7},{4,8},{5,9},{6... | collective-permute-start | bytes 2457608 | tf_op jit(solution)/shard_map/ppermute | solution.py:331
  20.0 13.4 %collective-permute-start.14 = (bf16[400,1024]{1,0:T(8,128)(2,1)S(1)}, bf16[400,1024]{1,0:T(8,128)(2,1)S(1)}, u32[]{:S(2)}, u32[]{:S(2)}) collective-permute-start(bf16[400,1024]{1,0:T(8,128)(2,1)S(1)} %shard_map.39.refs_0_.refs_1_.refs_7_), channel_id=1, source_target_pairs={{4,0},{5,1},{6,2},{7,3},{8,4},{9,5},{10,6},{11,7},{12,8},{13,9},{1... | collective-permute-start | bytes 2457608 | tf_op jit(solution)/shard_map/ppermute | solution.py:330
  22.1 18.5 %collective-permute-start.10 = (bf16[400,1024]{1,0:T(8,128)(2,1)S(1)}, bf16[400,1024]{1,0:T(8,128)(2,1)S(1)}, u32[]{:S(2)}, u32[]{:S(2)}) collective-permute-start(bf16[400,1024]{1,0:T(8,128)(2,1)S(1)} %shard_map.38.refs_1_.refs_2_.refs_6_.refs_3_), channel_id=1, source_target_pairs={{12,0},{13,1},{14,2},{15,3},{0,4},{1,5},{2,6},{3,7},{4,8},{5,9},{6... | collective-permute-start | bytes 2457608 | tf_op jit(solution)/shard_map/ppermute | solution.py:331
  22.9 17.6 %collective-permute-start.4 = (bf16[400,1024]{1,0:T(8,128)(2,1)S(1)}, bf16[400,1024]{1,0:T(8,128)(2,1)S(1)}, u32[]{:S(2)}, u32[]{:S(2)}) collective-permute-start(bf16[400,1024]{1,0:T(8,128)(2,1)S(1)} %shard_map.38.refs_1_.refs_2_.refs_6_.refs_3_), channel_id=1, source_target_pairs={{1,0},{2,1},{3,2},{0,3},{5,4},{6,5},{7,6},{4,7},{9,8},{10,9},{11,1... | collective-permute-start | bytes 2457608 | tf_op jit(solution)/shard_map/ppermute | solution.py:329
  29.7 16.4 %collective-permute-start.16 = (bf16[400,1024]{1,0:T(8,128)(2,1)S(1)}, bf16[400,1024]{1,0:T(8,128)(2,1)S(1)}, u32[]{:S(2)}, u32[]{:S(2)}) collective-permute-start(bf16[400,1024]{1,0:T(8,128)(2,1)S(1)} %shard_map.38.refs_1_.refs_2_.refs_6_.refs_3_), channel_id=1, source_target_pairs={{4,0},{5,1},{6,2},{7,3},{8,4},{9,5},{10,6},{11,7},{12,8},{13,9},{1... | collective-permute-start | bytes 2457608 | tf_op jit(solution)/shard_map/ppermute | solution.py:330
  31.8 19.3 %collective-permute-start.13 = (bf16[400,1024]{1,0:T(8,128)(2,1)S(1)}, bf16[400,1024]{1,0:T(8,128)(2,1)S(1)}, u32[]{:S(2)}, u32[]{:S(2)}) collective-permute-start(bf16[400,1024]{1,0:T(8,128)(2,1)S(1)} %collective-permute-done.12.refs_2_.refs_4_.refs_1_), channel_id=1, source_target_pairs={{1,0},{2,1},{3,2},{0,3},{5,4},{6,5},{7,6},{4,7},{9,8},{10,9},{11,1... | collective-permute-start | bytes 2457608 | tf_op jit(solution)/shard_map/ppermute | solution.py:332
  33.4 17.7 %collective-permute-start.15 = (bf16[400,1024]{1,0:T(8,128)(2,1)S(1)}, bf16[400,1024]{1,0:T(8,128)(2,1)S(1)}, u32[]{:S(2)}, u32[]{:S(2)}) collective-permute-start(bf16[400,1024]{1,0:T(8,128)(2,1)S(1)} %collective-permute-done.14.refs_3_.refs_5_), channel_id=1, source_target_pairs={{4,0},{5,1},{6,2},{7,3},{8,4},{9,5},{10,6},{11,7},{12,8},{13,9},{1... | collective-permute-start | bytes 2457608 | tf_op jit(solution)/shard_map/ppermute | solution.py:333
  40.6 13.9 %collective-permute-start.11 = (bf16[400,1024]{1,0:T(8,128)(2,1)S(1)}, bf16[400,1024]{1,0:T(8,128)(2,1)S(1)}, u32[]{:S(2)}, u32[]{:S(2)}) collective-permute-start(bf16[400,1024]{1,0:T(8,128)(2,1)S(1)} %collective-permute-done.10.refs_7_.refs_5_.refs_2_), channel_id=1, source_target_pairs={{12,0},{13,1},{14,2},{15,3},{0,4},{1,5},{2,6},{3,7},{4,8},{5,9},{6... | collective-permute-start | bytes 2457608 | tf_op jit(solution)/shard_map/ppermute | solution.py:334
  40.6 15.3 %collective-permute-start.5 = (bf16[400,1024]{1,0:T(8,128)(2,1)S(1)}, bf16[400,1024]{1,0:T(8,128)(2,1)S(1)}, u32[]{:S(2)}, u32[]{:S(2)}) collective-permute-start(bf16[400,1024]{1,0:T(8,128)(2,1)S(1)} %collective-permute-done.4.refs_0_.refs_2_), channel_id=1, source_target_pairs={{1,0},{2,1},{3,2},{0,3},{5,4},{6,5},{7,6},{4,7},{9,8},{10,9},{11,1... | collective-permute-start | bytes 2457608 | tf_op jit(solution)/shard_map/ppermute | solution.py:332

commit v4 on v3

v4 whole, which is shorter than its diff:
```python
import functools

import jax
import jax.numpy as jnp
from jax import lax
from jax.experimental import pallas as pl
from jax.experimental.pallas import tpu as pltpu
from jax.sharding import PartitionSpec as P

AXES = ("clus", "fold")
RING = 4
DEVICES = 128
EMB = 1024
ROWS = 768
PIECES = 8
PIECE = 96
HALF = 384
HALF_PIECES = 4
LANES = 128
LO = 128
FAR = 1.0e6
WIDE = 256
CHUNK = 256
VMEM = 12 * 1024 * 1024
RING_ORDER = (0, 1, 2, 3)
RING_START = tuple(2 * PIECE * RING_ORDER.index(i) for i in range(4))
SPANS = {
    "all": (0, 768),
    "top": (0, 384),
    "bottom": (384, 768),
    "near": (0, 192),
    "next": (192, 384),
    "rest": (192, 768),
}
CODE_ROWS = 16
OWN, UP, RIGHT, LEFT, OVER, UP2 = range(6)
OFFSETS = ((0, 0), (0, 1), (1, 0), (3, 0), (2, 0), (0, 2))


def place(x, core, y, z):
    return (x % RING * 2 + core) * 16 + y % RING * 4 + z % RING


def every_device():
    for x in range(RING):
        for core in range(2):
            for y in range(RING):
                for z in range(RING):
                    yield x, core, y, z


def packet_pairs(piece):
    offset, cross = divmod(piece, 2)
    pairs = []
    for x, core, y, z in every_device():
        kind = core ^ cross
        target = place(x + offset, 0, y, z) if kind == 0 else place(x, 1, y + offset, z)
        pairs.append((place(x, core, y, z), target))
    return pairs


def block_pairs(du, dv):
    pairs = []
    for x, core, y, z in every_device():
        source = place(x, 0, y + du, z + dv) if core == 0 else place(x + du, 1, y, z - dv)
        pairs.append((source, place(x, core, y, z)))
    return pairs


def whole(count):
    return [pl.BlockSpec(memory_space=pltpu.VMEM)] * count


def params():
    return pltpu.CompilerParams(vmem_limit_bytes=VMEM)


def pack_kernel(emb_hbm, labels_hbm, ordinals_hbm, slot_ref, *refs):
    piece_refs, (emb, labels_ref, ordinals_ref, unit, sems) = refs[:PIECES], refs[PIECES:]
    firsts = [
        pltpu.make_async_copy(labels_hbm, labels_ref, sems.at[0]),
        pltpu.make_async_copy(ordinals_hbm, ordinals_ref, sems.at[1]),
    ]
    copies = [
        pltpu.make_async_copy(
            emb_hbm.at[pl.ds(i, CHUNK)], emb.at[pl.ds(i, CHUNK)], sems.at[2 + i // CHUNK]
        )
        for i in range(0, ROWS, CHUNK)
    ]
    for copy in firsts + copies:
        copy.start()
    for copy in firsts:
        copy.wait()
    x, core, y, _ = where_am_i()
    labels = labels_ref[...].reshape(1, ROWS)
    ordinals = ordinals_ref[...].reshape(1, ROWS)
    kind = labels // RING
    coordinate = jnp.where(kind == 0, x, y)
    offset = (labels % RING - coordinate + RING) % RING
    cross = jnp.where(kind == core, 0, 1)
    start = jnp.zeros_like(offset)
    for ring in range(RING):
        start = jnp.where(offset == ring, RING_START[ring], start)
    live = labels < PIECES
    ids = lax.broadcasted_iota(jnp.int32, (16, ROWS), 0)
    member = (ids == 2 * offset + cross) & live
    before = lax.broadcasted_iota(jnp.int32, (ROWS, ROWS), 0) < lax.broadcasted_iota(
        jnp.int32, (ROWS, ROWS), 1
    )
    counts = jnp.dot(
        jnp.where(member, 1.0, 0.0).astype(jnp.bfloat16),
        jnp.where(before, 1.0, 0.0).astype(jnp.bfloat16),
        preferred_element_type=jnp.float32,
    )
    rank = jnp.sum(jnp.where(member, counts, 0.0), axis=0, keepdims=True).astype(jnp.int32)
    slot = jnp.where(live, start + cross * PIECE + rank, -1)
    slot_ref[...] = slot
    chosen = lax.broadcasted_iota(jnp.int32, (ROWS, ROWS), 0) == slot
    pick = jnp.where(chosen, 1.0, 0.0).astype(jnp.bfloat16)
    high, low = ordinals // LO + 1, ordinals % LO
    codes = jnp.where(ids == 0, high, jnp.where(ids == 1, low, 0)).astype(jnp.float32)
    codes = lax.dot_general(
        codes.astype(jnp.bfloat16),
        pick,
        (((1,), (1,)), ((), ())),
        preferred_element_type=jnp.float32,
    )
    for i, copy in zip(range(0, ROWS, CHUNK), copies, strict=True):
        copy.wait()
        widened = emb[pl.ds(i, CHUNK), :].astype(jnp.float32)
        square_sum = jnp.sum(widened * widened, axis=1, keepdims=True) + 1e-6
        unit[pl.ds(i, CHUNK), :] = (widened * lax.rsqrt(square_sum)).astype(jnp.bfloat16)
    packed = jnp.dot(pick, unit[...], preferred_element_type=jnp.float32).astype(jnp.bfloat16)
    lane_piece = lax.broadcasted_iota(jnp.int32, (CODE_ROWS, ROWS), 1) // PIECE
    for i, out_ref in enumerate(piece_refs):
        out_ref[:PIECE, :] = packed[i * PIECE : (i + 1) * PIECE]
        put_codes(out_ref, jnp.where(lane_piece == i, codes, 0.0))


def put_codes(ref, codes):
    ref[-CODE_ROWS:, :ROWS] = codes.astype(jnp.bfloat16)
    ref[-CODE_ROWS:, ROWS:] = jnp.zeros((CODE_ROWS, EMB - ROWS), jnp.bfloat16)


def codes_of(ref):
    return ref[-CODE_ROWS:, :ROWS].astype(jnp.float32)


def pack(embeddings, labels, ordinals):
    given = [pltpu.with_memory_space_constraint(v, pltpu.HBM) for v in (embeddings, labels, ordinals)]
    return pl.pallas_call(
        pack_kernel,
        out_shape=[jax.ShapeDtypeStruct((1, ROWS), jnp.int32)]
        + [jax.ShapeDtypeStruct((PIECE + CODE_ROWS, EMB), jnp.bfloat16)] * PIECES,
        in_specs=[pl.BlockSpec(memory_space=pltpu.HBM)] * 3,
        out_specs=whole(1 + PIECES),
        scratch_shapes=[
            pltpu.VMEM((ROWS, EMB), jnp.bfloat16),
            pltpu.VMEM((ROWS,), jnp.int32),
            pltpu.VMEM((ROWS,), jnp.int32),
            pltpu.VMEM((ROWS, EMB), jnp.bfloat16),
            pltpu.SemaphoreType.DMA((2 + ROWS // CHUNK,)),
        ],
        compiler_params=params(),
    )(*given)


def join_kernel(*refs):
    *given, out_ref = refs
    at, codes = 0, 0.0
    for ref in given:
        rows = ref.shape[0] - CODE_ROWS
        out_ref[at : at + rows, :] = ref[:rows, :]
        codes = codes + codes_of(ref)
        at += rows
    put_codes(out_ref, codes)


def join(*arrays):
    rows = sum(array.shape[0] - CODE_ROWS for array in arrays)
    return pl.pallas_call(
        join_kernel,
        out_shape=jax.ShapeDtypeStruct((rows + CODE_ROWS, EMB), jnp.bfloat16),
        in_specs=whole(len(arrays)),
        out_specs=whole(1)[0],
        compiler_params=params(),
    )(*arrays)


def close_kernel(names, steps, *refs):
    top_ref, *given = refs[: 1 + HALF_PIECES]
    bottom_ref, result, rows_best, column_ord = refs[1 + HALF_PIECES :]
    join_kernel(*given, bottom_ref)
    meet_kernel(names, steps, False, False, top_ref, bottom_ref, result, rows_best, column_ord)


def close(top, *arrays):
    names = [(OWN, "top"), (OWN, "bottom")]
    steps = [((OWN, "all"), [(OWN, "all")], None)]
    return pl.pallas_call(
        functools.partial(close_kernel, names, steps),
        out_shape=[
            jax.ShapeDtypeStruct((HALF + CODE_ROWS, EMB), jnp.bfloat16),
            jax.ShapeDtypeStruct((len(OFFSETS), 8, ROWS), jnp.float32),
        ],
        in_specs=whole(1 + HALF_PIECES),
        out_specs=whole(2),
        scratch_shapes=[pltpu.VMEM((1, ROWS, LANES), jnp.float32)] * 2,
        compiler_params=params(),
    )(top, *arrays)


def where_am_i():
    clus, fold = lax.axis_index("clus"), lax.axis_index("fold")
    return clus // 2, clus % 2, fold // RING, fold % RING


def piece_start(piece):
    return RING_START[piece // 2] + piece % 2 * PIECE


def post(out_ref, result_ref):
    x, core, y, z = where_am_i()
    out_ref[...] = jnp.zeros_like(out_ref)
    for block, (du, dv) in enumerate(OFFSETS):
        best = jnp.broadcast_to(jnp.max(result_ref[block], axis=0, keepdims=True), (8, ROWS))
        for piece in range(PIECES):
            ring, cross = divmod(piece, 2)
            start = piece_start(piece)
            mine = pltpu.roll(best, ROWS - start, 1) if start else best
            on_zero = place(x + RING - ring, cross, y + du, z + dv)
            on_one = place(x + du, 1 - cross, y + RING - ring, z + RING - dv)
            target = jnp.where(core == 0, on_zero, on_one)
            out_ref[pl.ds(target, 1), :] = mine[0:1, :LANES]


def meet_kernel(names, steps, has_before, is_last, *refs):
    parts = dict(zip(names, refs[: len(names)], strict=True))
    refs = refs[len(names) :]
    if has_before:
        before_ref, refs = refs[0], refs[1:]
    if is_last:
        out_ref, result, rows_best, column_ord = refs
    else:
        result, rows_best, column_ord = refs
    x, core, y, z = where_am_i()
    sides = {"u": jnp.where(core == 0, y, x) // 2, "v": z // 2}

    result[...] = before_ref[...] if has_before else jnp.full_like(result, -1.0)
    held = {}
    for block, part in names:
        held.setdefault(block, []).append(part)
    lines = {}
    for block, its in held.items():
        codes = sum(codes_of(parts[block, part]) for part in its)
        high, low = codes[0:1], codes[1:2]
        lines[block] = jnp.where(high == 0.0, FAR, (high - 1.0) * LO + low)
    firsts = {}
    for (block, span), _, _ in steps:
        low, high = firsts.get(block, SPANS[span])
        firsts[block] = min(low, SPANS[span][0]), max(high, SPANS[span][1])
    for i, (block, (low, high)) in enumerate(firsts.items()):
        line = jnp.broadcast_to(lines[block][:, low:high], (LANES, high - low))
        column_ord[i, low:high, :] = jnp.transpose(line)
        rows_best[i, low:high, :] = jnp.full((high - low, LANES), -1.0, jnp.float32)

    def rows_of(block, low, high):
        found = []
        for part in sorted(held[block], key=lambda p: SPANS[p]):
            start, stop = SPANS[part]
            one, two = max(low, start), min(high, stop)
            if one < two:
                found.append(parts[block, part][one - start : two - start, :])
        return found[0] if len(found) == 1 else jnp.concatenate(found, axis=0)

    def tile(a, start, stop, keys):
        i = list(firsts).index(a)
        given = [rows_of(*key) for key in keys]
        scores = lax.dot_general(
            rows_of(a, start, stop),
            given[0] if len(given) == 1 else jnp.concatenate(given, axis=0),
            (((1,), (1,)), ((), ())),
            preferred_element_type=jnp.float32,
        )
        best = rows_best[i, start:stop, :]
        ords = column_ord[i, start:stop, :]
        for k, (b, lane) in enumerate((b, n) for b, low, high in keys for n in range(low, high, LANES)):
            part = scores[:, k * LANES : (k + 1) * LANES]
            earlier = lines[b][:, lane : lane + LANES] < ords
            best = jnp.maximum(best, jnp.where(earlier, part, -1.0))
            if a != b or lane >= stop:
                later = jnp.where(earlier, -1.0, part).reshape(-1, 8, LANES)
                at = (b, slice(None), slice(lane, lane + LANES))
                result[at] = jnp.maximum(result[at], jnp.max(later, axis=0))
        rows_best[i, start:stop, :] = best

    def step(a, others):
        one, (start, stop) = a[0], SPANS[a[1]]
        lanes = [(b, n) for b, span in others for n in range(*SPANS[span], LANES)]
        tall = HALF if (stop - start) % WIDE else WIDE
        for k in range(0, len(lanes), WIDE // LANES):
            keys = []
            for b, lane in lanes[k : k + WIDE // LANES]:
                if keys and keys[-1][0] == b and keys[-1][2] == lane:
                    keys[-1] = (b, keys[-1][1], lane + LANES)
                else:
                    keys.append((b, lane, lane + LANES))
            for row in range(start, stop, tall):
                if keys[0][0] != one or keys[0][1] >= row:
                    tile(one, row, row + tall, keys)

    for a, b, role in steps:
        if role is None:
            step(a, b)
        else:
            pl.when(sides[role[0]] == role[1])(functools.partial(step, a, b))
    for i, (block, (low, high)) in enumerate(firsts.items()):
        across = jnp.transpose(rows_best[i, low:high, :]).reshape(LANES // 8, 8, high - low)
        at = (block, slice(None), slice(low, high))
        result[at] = jnp.maximum(result[at], jnp.max(across, axis=0))
    if is_last:
        post(out_ref, result)


def meet(held, steps, before, shown, is_last=False):
    names = []
    for a, b, _ in steps:
        for block, span in (a, *b):
            low, high = SPANS[span]
            names += [
                (one, part)
                for one, part in held
                if one == block and SPANS[part][0] < high and SPANS[part][1] > low
            ]
    names = list(dict.fromkeys(names))
    given = [held[name] for name in names] + ([] if before is None else [before])
    firsts = len({a[0] for a, _, _ in steps})
    best = (len(OFFSETS), 8, ROWS)
    return pl.pallas_call(
        functools.partial(meet_kernel, names, steps, before is not None, is_last),
        out_shape=jax.ShapeDtypeStruct((DEVICES, LANES) if is_last else best, jnp.float32),
        in_specs=whole(len(given)),
        out_specs=whole(1)[0],
        scratch_shapes=([pltpu.VMEM(best, jnp.float32)] if is_last else [])
        + [pltpu.VMEM((firsts, ROWS, LANES), jnp.float32)] * 2,
        compiler_params=params(),
        cost_estimate=pl.CostEstimate(
            flops=int(8 * shown * ROWS * ROWS * EMB),
            bytes_accessed=len(names) * HALF * EMB * 2,
            transcendentals=0,
        ),
    )(*given)


def unpack_kernel(slot_ref, got_ref, out_ref):
    x, core, y, z = where_am_i()
    slot = slot_ref[...]
    found = jnp.full((8, ROWS), -1.0, jnp.float32)
    for piece in range(PIECES):
        ring, cross = divmod(piece, 2)
        line = jnp.full((1, LANES), -1.0, jnp.float32)
        for du, dv in OFFSETS:
            on_zero = place(x + ring, 0, y + RING - du, z + RING - dv)
            on_one = place(x + RING - du, 1, y + ring, z + dv)
            holder = jnp.where(core == cross, on_zero, on_one)
            line = jnp.maximum(line, got_ref[pl.ds(holder, 1), :])
        column = jnp.transpose(jnp.broadcast_to(line, (LANES, LANES)))[:PIECE]
        rows = lax.broadcasted_iota(jnp.int32, (PIECE, LANES), 0) + piece_start(piece)
        best = []
        for k in range(0, ROWS, LANES):
            chosen = jnp.where(rows == slot[:, k : k + LANES], column, -1.0)
            best.append(jnp.max(chosen.reshape(PIECE // 8, 8, LANES), axis=0))
        found = jnp.maximum(found, jnp.concatenate(best, axis=1))
    out_ref[...] = jnp.max(found, axis=0)


def unpack(slot, got):
    return pl.pallas_call(
        unpack_kernel,
        out_shape=jax.ShapeDtypeStruct((ROWS,), jnp.float32),
        in_specs=whole(2),
        out_specs=whole(1)[0],
        compiler_params=params(),
    )(slot, got)


def after(array, *others):
    return lax.optimization_barrier((array, *others))[0]


def per_device(embeddings, labels, ordinals):
    send = functools.partial(lax.ppermute, axis_name=AXES)
    up, right, left = block_pairs(0, 1), block_pairs(1, 0), block_pairs(3, 0)
    slot, *pieces = pack(embeddings, labels, ordinals)
    held = {}
    landed = [pieces[0]] + [send(pieces[i], perm=packet_pairs(i)) for i in range(1, PIECES)]
    top = join(*landed[:HALF_PIECES])
    bottom, best = close(top, *landed[HALF_PIECES:])
    held[OWN, "top"], held[OWN, "bottom"] = top, bottom
    held[UP, "top"] = send(top, perm=up)
    held[UP, "bottom"] = send(bottom, perm=up)
    held[RIGHT, "top"] = send(top, perm=right)
    held[LEFT, "top"] = send(top, perm=left)
    held[RIGHT, "bottom"] = send(bottom, perm=right)
    held[LEFT, "bottom"] = send(bottom, perm=left)
    held[UP2, "top"] = send(held[UP, "top"], perm=up)
    held[UP2, "bottom"] = send(held[UP, "bottom"], perm=up)
    held[OVER, "top"] = send(held[RIGHT, "top"], perm=right)
    held[OVER, "bottom"] = send(held[LEFT, "bottom"], perm=left)
    best = meet(
        held,
        [
            ((UP, "top"), [(OWN, "all")], None),
            ((RIGHT, "top"), [(OWN, "all")], None),
            ((RIGHT, "top"), [(LEFT, "top")], ("u", 0)),
        ],
        best,
        2.25,
    )
    best = meet(
        held,
        [
            ((UP, "bottom"), [(OWN, "all")], None),
            ((RIGHT, "bottom"), [(OWN, "all")], None),
            ((UP, "all"), [(RIGHT, "all")], None),
            ((UP, "all"), [(LEFT, "all")], None),
            ((RIGHT, "top"), [(LEFT, "bottom")], None),
            ((RIGHT, "bottom"), [(LEFT, "bottom")], ("u", 1)),
        ],
        best,
        3.5,
    )
    best = meet(
        held,
        [
            ((OVER, "top"), [(UP, "all")], None),
            ((UP2, "top"), [(LEFT, "all")], None),
            ((UP2, "top"), [(OWN, "all")], ("v", 0)),
            ((UP2, "top"), [(OWN, "bottom"), (OVER, "top")], ("v", 1)),
        ],
        best,
        1.75,
    )
    best = meet(
        held, [((OVER, "bottom"), [(UP, "all"), (UP2, "top")], None)], best, 0.75
    )
    sent = meet(
        held,
        [
            ((UP2, "bottom"), [(LEFT, "all")], None),
            ((UP2, "bottom"), [(OWN, "bottom")], ("v", 1)),
            ((UP2, "bottom"), [(OVER, "bottom")], ("v", 0)),
        ],
        best,
        1.0,
        True,
    )
    got = lax.all_to_all(sent, AXES, split_axis=0, concat_axis=0, tiled=True)
    return unpack(slot, got)


def solution(mesh):
    return jax.shard_map(
        per_device,
        mesh=mesh,
        in_specs=(P(AXES, None), P(AXES), P(AXES)),
        out_specs=P(AXES),
        check_vma=False,
    )
```

time: 77.9 us -> 77.3 us (level)
  blocking collectives: 19.9 us -> 18.7 us
  waiting for transfers between devices: 14.3 us -> 15.1 us
    pallas_call x5, Pallas kernels: 14.6 us -> 13.3 us  [meet(): pl.pallas_call(functools.partial(meet_kernel, names, steps, before is not...]
    all_to_all x1, blocking collectives: 19.9 us -> 18.7 us  [per_device(): got = lax.all_to_all(sent, AXES, split_axis=0, concat_axis=0, tiled=True)]
    pallas_call x2, Pallas kernels: 0.12 us -> 1.22 us  [the longest x1 1.15 us: close(): pl.pallas_call(functools.partial(close_kernel, names, steps), out_shape=[...]
    ppermute x17, waiting for transfers between devices: 14.3 us -> 15.1 us  [the longest x1 5.87 us: per_device(): held[LEFT, 'bottom'] = send(bottom, perm=left)]
  transfers between devices with their start and end apart: 17 -> 17, of which waited for: 4 -> 6; matrix products, arithmetic and copies ran while one was open for 0% -> 0% of each run, Pallas kernels for 18% -> 17%
where the time goes in v4:
time: 77.3 us; the launch traced here: 77.1 us
  starting transfers between devices  24.6 us (32%)
  Pallas kernels  18.7 us (24%)
  blocking collectives  18.7 us (24%)
  waiting for transfers between devices  15.1 us (20%)
    all_to_all x1, blocking collectives, per_device(): got = lax.all_to_all(sent, AXES, split_axis=0, concat_axis=0, tiled=True)  18.7 us
    pallas_call x5, Pallas kernels, meet(): pl.pallas_call(functools.partial(meet_kernel, names, steps, before is not...  13.3 us
    ppermute x7, starting transfers between devices, per_device(): send(pieces[i], perm=packet_pairs(i))  12.4 us
    ppermute x1, waiting for transfers between devices, per_device(): held[LEFT, 'bottom'] = send(bottom, perm=left)  5.87 us
    ppermute x1, waiting for transfers between devices, per_device(): held[UP, 'top'] = send(top, perm=up)  4.02 us
    pallas_call x1, Pallas kernels, pack(): pl.pallas_call(pack_kernel, out_shape=[jax.ShapeDtypeStruct((1, ROWS), jn...  3.25 us
    ppermute x1, starting transfers between devices, per_device(): held[RIGHT, 'top'] = send(top, perm=right)  1.98 us
    ppermute x1, starting transfers between devices, per_device(): held[UP, 'top'] = send(top, perm=up)  1.84 us
  transfers between devices with their start and end apart: 17, of which 6 were waited for; matrix products, arithmetic and copies ran while one was open for 0% of the time, Pallas kernels for 17%

profile of v4, /device:TPU:1, one launch (start us, length us, event | category | flops | bytes accessed | tf_op | source)
XLA Modules:
  0.0 77.1 jit_solution(10788674344076518958)
XLA Ops:
  0.0 3.3 %shard_map.37 = (s32[1,768]{1,0:T(1,128)S(1)}, bf16[112,1024]{1,0:T(8,128)(2,1)S(1)}, bf16[112,1024]{1,0:T(8,128)(2,1)S(1)}, bf16[112,1024]{1,0:T(8,128)(2,1)S(1...) custom-call(bf16[768,1024]{1,0:T(8,128)(2,1)} %emb_hbm.1, ...), custom_call_target="tpu_custom_call" | custom-call | tf_op jit(solution)/shard_map/pallas_call | solution.py:151
  3.3 1.5 %collective-permute-start = (bf16[112,1024]{1,0:T(8,128)(2,1)S(1)}, bf16[112,1024]{1,0:T(8,128)(2,1)S(1)}, u32[]{:S(2)}, u32[]{:S(2)}) collective-permute-start(bf16[112,1024]{1,0:T(8,128)(2,1)S(1)} %get-tuple-element.18), channel_id=1, source_target_pairs={{0,16},{1,17},{2,18},{3,19},{4,20},{5,21},{6,22},{7,23},{8,24},{9,... | collective-permute-start | bytes 688136 | tf_op jit(solution)/shard_map/ppermute | solution.py:396
  4.8 1.4 %collective-permute-start.1 = (bf16[112,1024]{1,0:T(8,128)(2,1)S(1)}, bf16[112,1024]{1,0:T(8,128)(2,1)S(1)}, u32[]{:S(2)}, u32[]{:S(2)}) collective-permute-start(bf16[112,1024]{1,0:T(8,128)(2,1)S(1)} %get-tuple-element.19), channel_id=1, source_target_pairs={{0,32},{1,33},{2,34},{3,35},{4,36},{5,37},{6,38},{7,39},{8,40},{9,... | collective-permute-start | bytes 688136 | tf_op jit(solution)/shard_map/ppermute | solution.py:396
  6.1 1.4 %collective-permute-start.2 = (bf16[112,1024]{1,0:T(8,128)(2,1)S(1)}, bf16[112,1024]{1,0:T(8,128)(2,1)S(1)}, u32[]{:S(2)}, u32[]{:S(2)}) collective-permute-start(bf16[112,1024]{1,0:T(8,128)(2,1)S(1)} %get-tuple-element.20), channel_id=1, source_target_pairs={{0,20},{1,21},{2,22},{3,23},{4,24},{5,25},{6,26},{7,27},{8,28},{9,... | collective-permute-start | bytes 688136 | tf_op jit(solution)/shard_map/ppermute | solution.py:396
  7.5 2.9 %collective-permute-start.3 = (bf16[112,1024]{1,0:T(8,128)(2,1)S(1)}, bf16[112,1024]{1,0:T(8,128)(2,1)S(1)}, u32[]{:S(2)}, u32[]{:S(2)}) collective-permute-start(bf16[112,1024]{1,0:T(8,128)(2,1)S(1)} %get-tuple-element.21), channel_id=1, source_target_pairs={{0,64},{1,65},{2,66},{3,67},{4,68},{5,69},{6,70},{7,71},{8,72},{9,... | collective-permute-start | bytes 688136 | tf_op jit(solution)/shard_map/ppermute | solution.py:396
  10.4 0.5 collective-permute-start.4
  11.0 1.4 %collective-permute-start.5 = (bf16[112,1024]{1,0:T(8,128)(2,1)S(1)}, bf16[112,1024]{1,0:T(8,128)(2,1)S(1)}, u32[]{:S(2)}, u32[]{:S(2)}) collective-permute-start(bf16[112,1024]{1,0:T(8,128)(2,1)S(1)} %get-tuple-element.23), channel_id=1, source_target_pairs={{0,96},{1,97},{2,98},{3,99},{4,100},{5,101},{6,102},{7,103},{8,104... | collective-permute-start | bytes 688136 | tf_op jit(solution)/shard_map/ppermute | solution.py:396
  12.4 3.3 %collective-permute-start.6 = (bf16[112,1024]{1,0:T(8,128)(2,1)S(1)}, bf16[112,1024]{1,0:T(8,128)(2,1)S(1)}, u32[]{:S(2)}, u32[]{:S(2)}) collective-permute-start(bf16[112,1024]{1,0:T(8,128)(2,1)S(1)} %get-tuple-element.24), channel_id=1, source_target_pairs={{0,28},{1,29},{2,30},{3,31},{4,16},{5,17},{6,18},{7,19},{8,20},{9,... | collective-permute-start | bytes 688136 | tf_op jit(solution)/shard_map/ppermute | solution.py:396
  15.6 0.1 shard_map.38.refs_0_.refs_1_.refs_6_
  15.7 1.8 %collective-permute-start.12 = (bf16[400,1024]{1,0:T(8,128)(2,1)S(1)}, bf16[400,1024]{1,0:T(8,128)(2,1)S(1)}, u32[]{:S(2)}, u32[]{:S(2)}) collective-permute-start(bf16[400,1024]{1,0:T(8,128)(2,1)S(1)} %shard_map.38.refs_0_.refs_1_.refs_6_), channel_id=1, source_target_pairs={{1,0},{2,1},{3,2},{0,3},{5,4},{6,5},{7,6},{4,7},{9,8},{10,9},{11,1... | collective-permute-start | bytes 2457608 | tf_op jit(solution)/shard_map/ppermute | solution.py:400
  17.5 1.6 %collective-permute-done.3.refs_1_ = bf16[112,1024]{1,0:T(8,128)(2,1)S(1)} collective-permute-done((bf16[112,1024]{1,0:T(8,128)(2,1)S(1)}, bf16[112,1024]{1,0:T(8,128)(2,1)S(1)}, u32[]{:S(2)}, u32[]{:S(2)}) %collective-permute-start.3) | collective-permute-done | bytes 229408 | tf_op jit(solution)/shard_map/ppermute | solution.py:396
  19.1 0.9 %collective-permute-start.9 = (bf16[400,1024]{1,0:T(8,128)(2,1)S(1)}, bf16[400,1024]{1,0:T(8,128)(2,1)S(1)}, u32[]{:S(2)}, u32[]{:S(2)}) collective-permute-start(bf16[400,1024]{1,0:T(8,128)(2,1)S(1)} %shard_map.38.refs_0_.refs_1_.refs_6_), channel_id=1, source_target_pairs={{12,0},{13,1},{14,2},{15,3},{0,4},{1,5},{2,6},{3,7},{4,8},{5,9},{6... | collective-permute-start | bytes 2457608 | tf_op jit(solution)/shard_map/ppermute | solution.py:403
  20.0 2.0 %collective-permute-start.14 = (bf16[400,1024]{1,0:T(8,128)(2,1)S(1)}, bf16[400,1024]{1,0:T(8,128)(2,1)S(1)}, u32[]{:S(2)}, u32[]{:S(2)}) collective-permute-start(bf16[400,1024]{1,0:T(8,128)(2,1)S(1)} %shard_map.38.refs_0_.refs_1_.refs_6_), channel_id=1, source_target_pairs={{4,0},{5,1},{6,2},{7,3},{8,4},{9,5},{10,6},{11,7},{12,8},{13,9},{1... | collective-permute-start | bytes 2457608 | tf_op jit(solution)/shard_map/ppermute | solution.py:402
  22.0 1.2 %shard_map.39 = (bf16[400,1024]{1,0:T(8,128)(2,1)S(1)}, f32[6,8,768]{2,1,0:T(8,128)S(1)}) custom-call(bf16[400,1024]{1,0:T(8,128)(2,1)S(1)} %shard_map.38.refs_0_.refs_1_.refs_6_, bf16[112,1024]{1,0:T(8,128)(2,1)S(1)} %collective-permute-done.3.refs_1_, bf16[112,1024]{1,0:T(8,128)(2,1)S(1)} %collective-permute-done.4.refs_2_, ...), custom_call_target="tpu_custom_call" | custom-call | tf_op jit(solution)/shard_map/pallas_call | solution.py:200
  23.2 0.9 %collective-permute-start.10 = (bf16[400,1024]{1,0:T(8,128)(2,1)S(1)}, bf16[400,1024]{1,0:T(8,128)(2,1)S(1)}, u32[]{:S(2)}, u32[]{:S(2)}) collective-permute-start(bf16[400,1024]{1,0:T(8,128)(2,1)S(1)} %get-tuple-element.25.refs_2_.refs_7_.refs_3_), channel_id=1, source_target_pairs={{12,0},{13,1},{14,2},{15,3},{0,4},{1,5},{2,6},{3,7},{4,8},{5,9},{6... | collective-permute-start | bytes 2457608 | tf_op jit(solution)/shard_map/ppermute | solution.py:405
  24.0 1.6 %collective-permute-start.7 = (bf16[400,1024]{1,0:T(8,128)(2,1)S(1)}, bf16[400,1024]{1,0:T(8,128)(2,1)S(1)}, u32[]{:S(2)}, u32[]{:S(2)}) collective-permute-start(bf16[400,1024]{1,0:T(8,128)(2,1)S(1)} %get-tuple-element.25.refs_2_.refs_7_.refs_3_), channel_id=1, source_target_pairs={{1,0},{2,1},{3,2},{0,3},{5,4},{6,5},{7,6},{4,7},{9,8},{10,9},{11,1... | collective-permute-start | bytes 2457608 | tf_op jit(solution)/shard_map/ppermute | solution.py:401
  25.7 4.0 %collective-permute-done.12.refs_0_.refs_4_.refs_1_ = bf16[400,1024]{1,0:T(8,128)(2,1)S(1)} collective-permute-done((bf16[400,1024]{1,0:T(8,128)(2,1)S(1)}, bf16[400,1024]{1,0:T(8,128)(2,1)S(1)}, u32[]{:S(2)}, u32[]{:S(2)}) %collective-permute-start.12) | collective-permute-done | bytes 819232 | tf_op jit(solution)/shard_map/ppermute | solution.py:400
  29.7 0.4 collective-permute-start.16
  30.1 1.7 %collective-permute-done.9.refs_4_.refs_6_.refs_1_ = bf16[400,1024]{1,0:T(8,128)(2,1)S(1)} collective-permute-done((bf16[400,1024]{1,0:T(8,128)(2,1)S(1)}, bf16[400,1024]{1,0:T(8,128)(2,1)S(1)}, u32[]{:S(2)}, u32[]{:S(2)}) %collective-permute-start.9) | collective-permute-done | bytes 819232 | tf_op jit(solution)/shard_map/ppermute | solution.py:403
  31.8 1.6 %collective-permute-start.13 = (bf16[400,1024]{1,0:T(8,128)(2,1)S(1)}, bf16[400,1024]{1,0:T(8,128)(2,1)S(1)}, u32[]{:S(2)}, u32[]{:S(2)}) collective-permute-start(bf16[400,1024]{1,0:T(8,128)(2,1)S(1)} %collective-permute-done.12.refs_0_.refs_4_.refs_1_), channel_id=1, source_target_pairs={{1,0},{2,1},{3,2},{0,3},{5,4},{6,5},{7,6},{4,7},{9,8},{10,9},{11,1... | collective-permute-start | bytes 2457608 | tf_op jit(solution)/shard_map/ppermute | solution.py:406
  33.5 1.3 %collective-permute-start.15 = (bf16[400,1024]{1,0:T(8,128)(2,1)S(1)}, bf16[400,1024]{1,0:T(8,128)(2,1)S(1)}, u32[]{:S(2)}, u32[]{:S(2)}) collective-permute-start(bf16[400,1024]{1,0:T(8,128)(2,1)S(1)} %collective-permute-done.14.refs_3_.refs_5_), channel_id=1, source_target_pairs={{4,0},{5,1},{6,2},{7,3},{8,4},{9,5},{10,6},{11,7},{12,8},{13,9},{1... | collective-permute-start | bytes 2457608 | tf_op jit(solution)/shard_map/ppermute | solution.py:408
  34.7 5.9 %collective-permute-done.10.refs_7_.refs_5_.refs_2_ = bf16[400,1024]{1,0:T(8,128)(2,1)S(1)} collective-permute-done((bf16[400,1024]{1,0:T(8,128)(2,1)S(1)}, bf16[400,1024]{1,0:T(8,128)(2,1)S(1)}, u32[]{:S(2)}, u32[]{:S(2)}) %collective-permute-start.10) | collective-permute-done | bytes 819232 | tf_op jit(solution)/shard_map/ppermute | solution.py:405
  40.6 1.6 %collective-permute-start.8 = (bf16[400,1024]{1,0:T(8,128)(2,1)S(1)}, bf16[400,1024]{1,0:T(8,128)(2,1)S(1)}, u32[]{:S(2)}, u32[]{:S(2)}) collective-permute-start(bf16[400,1024]{1,0:T(8,128)(2,1)S(1)} %collective-permute-done.7.refs_0_.refs_2_), channel_id=1, source_target_pairs={{1,0},{2,1},{3,2},{0,3},{5,4},{6,5},{7,6},{4,7},{9,8},{10,9},{11,1... | collective-permute-start | bytes 2457608 | tf_op jit(solution)/shard_map/ppermute | solution.py:407
  42.2 2.5 %shard_map.40.refs_8_ = f32[6,8,768]{2,1,0:T(8,128)S(1)} custom-call(bf16[400,1024]{1,0:T(8,128)(2,1)S(1)} %collective-permute-done.12.refs_0_.refs_4_.refs_1_, bf16[400,1024]{1,0:T(8,128)(2,1)S(1)} %shard_map.38.refs_0_.refs_1_.refs_6_, bf16[400,1024]{1,0:T(8,128)(2,1)S(1)} %get-tuple-element.25.refs_2_.refs_7_.refs_3_, ...), custom_call_target="tpu_custom_call" | custom-call | flops 10871635968 | bytes 3932160 | tf_op jit(solution)/shard_map/pallas_call | solution.py:339
  44.8 5.2 %shard_map.41.refs_8_ = f32[6,8,768]{2,1,0:T(8,128)S(1)} custom-call(bf16[400,1024]{1,0:T(8,128)(2,1)S(1)} %collective-permute-done.7.refs_0_.refs_2_, bf16[400,1024]{1,0:T(8,128)(2,1)S(1)} %shard_map.38.refs_0_.refs_1_.refs_6_, bf16[400,1024]{1,0:T(8,128)(2,1)S(1)} %get-tuple-element.25.refs_2_.refs_7_.refs_3_, ...), custom_call_target="tpu_custom_call" | custom-call | flops 16911433728 | bytes 6291456 | tf_op jit(solution)/shard_map/pallas_call | solution.py:339
  50.0 2.6 %shard_map.42.refs_4_ = f32[6,8,768]{2,1,0:T(8,128)S(1)} custom-call(bf16[400,1024]{1,0:T(8,128)(2,1)S(1)} %collective-permute-done.15.refs_0_, bf16[400,1024]{1,0:T(8,128)(2,1)S(1)} %collective-permute-done.12.refs_0_.refs_4_.refs_1_, bf16[400,1024]{1,0:T(8,128)(2,1)S(1)} %collective-permute-done.7.refs_0_.refs_2_, ...), custom_call_target="tpu_custom_call" | custom-call | flops 8455716864 | bytes 6291456 | tf_op jit(solution)/shard_map/pallas_call | solution.py:339
  52.6 0.7 collective-permute-done.11.refs_0_.refs_4_
  53.3 1.3 %shard_map.43.refs_5_ = f32[6,8,768]{2,1,0:T(8,128)S(1)} custom-call(bf16[400,1024]{1,0:T(8,128)(2,1)S(1)} %collective-permute-done.11.refs_0_.refs_4_, bf16[400,1024]{1,0:T(8,128)(2,1)S(1)} %collective-permute-done.12.refs_0_.refs_4_.refs_1_, bf16[400,1024]{1,0:T(8,128)(2,1)S(1)} %collective-permute-done.7.refs_0_.refs_2_, ...), custom_call_target="tpu_custom_call" | custom-call | flops 3623878656 | bytes 3145728 | tf_op jit(solution)/shard_map/pallas_call | solution.py:339
  54.6 1.2 %collective-permute-done.8.refs_0_ = bf16[400,1024]{1,0:T(8,128)(2,1)S(1)} collective-permute-done((bf16[400,1024]{1,0:T(8,128)(2,1)S(1)}, bf16[400,1024]{1,0:T(8,128)(2,1)S(1)}, u32[]{:S(2)}, u32[]{:S(2)}) %collective-permute-start.8) | collective-permute-done | bytes 819232 | tf_op jit(solution)/shard_map/ppermute | solution.py:407
  55.8 1.7 %shard_map.44 = f32[128,128]{1,0:T(8,128)S(1)} custom-call(bf16[400,1024]{1,0:T(8,128)(2,1)S(1)} %collective-permute-done.8.refs_0_, bf16[400,1024]{1,0:T(8,128)(2,1)S(1)} %collective-permute-done.9.refs_4_.refs_6_.refs_1_, bf16[400,1024]{1,0:T(8,128)(2,1)S(1)} %collective-permute-done.10.refs_7_.refs_5_.refs_2_, ...), custom_call_target="tpu_custom_call" | custom-call | flops 4831838208 | bytes 3932160 | tf_op jit(solution)/shard_map/pallas_call | solution.py:339
  57.5 18.7 %all_to_all.11 = f32[128,1,128]{2,1,0:T(1,128)S(1)} all-to-all(f32[128,1,128]{2,1,0:T(1,128)S(1)} %bitcast.5), channel_id=1, replica_groups=mesh['clus'=8,'fold'=16] {'clus','fold'}, dimensions={0} | all-to-all | bytes 131072 | tf_op jit(solution)/shard_map/all_to_all | solution.py:458
  76.2 0.9 %shard_map.45 = f32[768]{0:T(1024)} custom-call(s32[1,768]{1,0:T(1,128)S(1)} %get-tuple-element.16.slot_ref, f32[128,128]{1,0:T(8,128)S(1)} %bitcast.4), custom_call_target="tpu_custom_call" | custom-call | tf_op jit(solution)/shard_map/pallas_call | solution.py:378
  (12 shorter events, 0.0 us)
Async XLA Ops:
  3.3 7.7 %collective-permute-start = (bf16[112,1024]{1,0:T(8,128)(2,1)S(1)}, bf16[112,1024]{1,0:T(8,128)(2,1)S(1)}, u32[]{:S(2)}, u32[]{:S(2)}) collective-permute-start(bf16[112,1024]{1,0:T(8,128)(2,1)S(1)} %get-tuple-element.18), channel_id=1, source_target_pairs={{0,16},{1,17},{2,18},{3,19},{4,20},{5,21},{6,22},{7,23},{8,24},{9,... | collective-permute-start | bytes 688136 | tf_op jit(solution)/shard_map/ppermute | solution.py:396
  4.8 7.6 %collective-permute-start.1 = (bf16[112,1024]{1,0:T(8,128)(2,1)S(1)}, bf16[112,1024]{1,0:T(8,128)(2,1)S(1)}, u32[]{:S(2)}, u32[]{:S(2)}) collective-permute-start(bf16[112,1024]{1,0:T(8,128)(2,1)S(1)} %get-tuple-element.19), channel_id=1, source_target_pairs={{0,32},{1,33},{2,34},{3,35},{4,36},{5,37},{6,38},{7,39},{8,40},{9,... | collective-permute-start | bytes 688136 | tf_op jit(solution)/shard_map/ppermute | solution.py:396
  6.1 9.5 %collective-permute-start.2 = (bf16[112,1024]{1,0:T(8,128)(2,1)S(1)}, bf16[112,1024]{1,0:T(8,128)(2,1)S(1)}, u32[]{:S(2)}, u32[]{:S(2)}) collective-permute-start(bf16[112,1024]{1,0:T(8,128)(2,1)S(1)} %get-tuple-element.20), channel_id=1, source_target_pairs={{0,20},{1,21},{2,22},{3,23},{4,24},{5,25},{6,26},{7,27},{8,28},{9,... | collective-permute-start | bytes 688136 | tf_op jit(solution)/shard_map/ppermute | solution.py:396
  7.5 11.6 %collective-permute-start.3 = (bf16[112,1024]{1,0:T(8,128)(2,1)S(1)}, bf16[112,1024]{1,0:T(8,128)(2,1)S(1)}, u32[]{:S(2)}, u32[]{:S(2)}) collective-permute-start(bf16[112,1024]{1,0:T(8,128)(2,1)S(1)} %get-tuple-element.21), channel_id=1, source_target_pairs={{0,64},{1,65},{2,66},{3,67},{4,68},{5,69},{6,70},{7,71},{8,72},{9,... | collective-permute-start | bytes 688136 | tf_op jit(solution)/shard_map/ppermute | solution.py:396
  10.4 9.6 %collective-permute-start.4 = (bf16[112,1024]{1,0:T(8,128)(2,1)S(1)}, bf16[112,1024]{1,0:T(8,128)(2,1)S(1)}, u32[]{:S(2)}, u32[]{:S(2)}) collective-permute-start(bf16[112,1024]{1,0:T(8,128)(2,1)S(1)} %get-tuple-element.22), channel_id=1, source_target_pairs={{0,24},{1,25},{2,26},{3,27},{4,28},{5,29},{6,30},{7,31},{8,16},{9,... | collective-permute-start | bytes 688136 | tf_op jit(solution)/shard_map/ppermute | solution.py:396
  11.0 11.1 %collective-permute-start.5 = (bf16[112,1024]{1,0:T(8,128)(2,1)S(1)}, bf16[112,1024]{1,0:T(8,128)(2,1)S(1)}, u32[]{:S(2)}, u32[]{:S(2)}) collective-permute-start(bf16[112,1024]{1,0:T(8,128)(2,1)S(1)} %get-tuple-element.23), channel_id=1, source_target_pairs={{0,96},{1,97},{2,98},{3,99},{4,100},{5,101},{6,102},{7,103},{8,104... | collective-permute-start | bytes 688136 | tf_op jit(solution)/shard_map/ppermute | solution.py:396
  12.4 9.7 %collective-permute-start.6 = (bf16[112,1024]{1,0:T(8,128)(2,1)S(1)}, bf16[112,1024]{1,0:T(8,128)(2,1)S(1)}, u32[]{:S(2)}, u32[]{:S(2)}) collective-permute-start(bf16[112,1024]{1,0:T(8,128)(2,1)S(1)} %get-tuple-element.24), channel_id=1, source_target_pairs={{0,28},{1,29},{2,30},{3,31},{4,16},{5,17},{6,18},{7,19},{8,20},{9,... | collective-permute-start | bytes 688136 | tf_op jit(solution)/shard_map/ppermute | solution.py:396
  15.7 14.0 %collective-permute-start.12 = (bf16[400,1024]{1,0:T(8,128)(2,1)S(1)}, bf16[400,1024]{1,0:T(8,128)(2,1)S(1)}, u32[]{:S(2)}, u32[]{:S(2)}) collective-permute-start(bf16[400,1024]{1,0:T(8,128)(2,1)S(1)} %shard_map.38.refs_0_.refs_1_.refs_6_), channel_id=1, source_target_pairs={{1,0},{2,1},{3,2},{0,3},{5,4},{6,5},{7,6},{4,7},{9,8},{10,9},{11,1... | collective-permute-start | bytes 2457608 | tf_op jit(solution)/shard_map/ppermute | solution.py:400
  19.1 12.7 %collective-permute-start.9 = (bf16[400,1024]{1,0:T(8,128)(2,1)S(1)}, bf16[400,1024]{1,0:T(8,128)(2,1)S(1)}, u32[]{:S(2)}, u32[]{:S(2)}) collective-permute-start(bf16[400,1024]{1,0:T(8,128)(2,1)S(1)} %shard_map.38.refs_0_.refs_1_.refs_6_), channel_id=1, source_target_pairs={{12,0},{13,1},{14,2},{15,3},{0,4},{1,5},{2,6},{3,7},{4,8},{5,9},{6... | collective-permute-start | bytes 2457608 | tf_op jit(solution)/shard_map/ppermute | solution.py:403
  20.0 13.4 %collective-permute-start.14 = (bf16[400,1024]{1,0:T(8,128)(2,1)S(1)}, bf16[400,1024]{1,0:T(8,128)(2,1)S(1)}, u32[]{:S(2)}, u32[]{:S(2)}) collective-permute-start(bf16[400,1024]{1,0:T(8,128)(2,1)S(1)} %shard_map.38.refs_0_.refs_1_.refs_6_), channel_id=1, source_target_pairs={{4,0},{5,1},{6,2},{7,3},{8,4},{9,5},{10,6},{11,7},{12,8},{13,9},{1... | collective-permute-start | bytes 2457608 | tf_op jit(solution)/shard_map/ppermute | solution.py:402
  23.2 17.4 %collective-permute-start.10 = (bf16[400,1024]{1,0:T(8,128)(2,1)S(1)}, bf16[400,1024]{1,0:T(8,128)(2,1)S(1)}, u32[]{:S(2)}, u32[]{:S(2)}) collective-permute-start(bf16[400,1024]{1,0:T(8,128)(2,1)S(1)} %get-tuple-element.25.refs_2_.refs_7_.refs_3_), channel_id=1, source_target_pairs={{12,0},{13,1},{14,2},{15,3},{0,4},{1,5},{2,6},{3,7},{4,8},{5,9},{6... | collective-permute-start | bytes 2457608 | tf_op jit(solution)/shard_map/ppermute | solution.py:405
  24.0 16.6 %collective-permute-start.7 = (bf16[400,1024]{1,0:T(8,128)(2,1)S(1)}, bf16[400,1024]{1,0:T(8,128)(2,1)S(1)}, u32[]{:S(2)}, u32[]{:S(2)}) collective-permute-start(bf16[400,1024]{1,0:T(8,128)(2,1)S(1)} %get-tuple-element.25.refs_2_.refs_7_.refs_3_), channel_id=1, source_target_pairs={{1,0},{2,1},{3,2},{0,3},{5,4},{6,5},{7,6},{4,7},{9,8},{10,9},{11,1... | collective-permute-start | bytes 2457608 | tf_op jit(solution)/shard_map/ppermute | solution.py:401
  29.7 15.1 %collective-permute-start.16 = (bf16[400,1024]{1,0:T(8,128)(2,1)S(1)}, bf16[400,1024]{1,0:T(8,128)(2,1)S(1)}, u32[]{:S(2)}, u32[]{:S(2)}) collective-permute-start(bf16[400,1024]{1,0:T(8,128)(2,1)S(1)} %get-tuple-element.25.refs_2_.refs_7_.refs_3_), channel_id=1, source_target_pairs={{4,0},{5,1},{6,2},{7,3},{8,4},{9,5},{10,6},{11,7},{12,8},{13,9},{1... | collective-permute-start | bytes 2457608 | tf_op jit(solution)/shard_map/ppermute | solution.py:404
  31.8 18.2 %collective-permute-start.13 = (bf16[400,1024]{1,0:T(8,128)(2,1)S(1)}, bf16[400,1024]{1,0:T(8,128)(2,1)S(1)}, u32[]{:S(2)}, u32[]{:S(2)}) collective-permute-start(bf16[400,1024]{1,0:T(8,128)(2,1)S(1)} %collective-permute-done.12.refs_0_.refs_4_.refs_1_), channel_id=1, source_target_pairs={{1,0},{2,1},{3,2},{0,3},{5,4},{6,5},{7,6},{4,7},{9,8},{10,9},{11,1... | collective-permute-start | bytes 2457608 | tf_op jit(solution)/shard_map/ppermute | solution.py:406
  33.5 16.5 %collective-permute-start.15 = (bf16[400,1024]{1,0:T(8,128)(2,1)S(1)}, bf16[400,1024]{1,0:T(8,128)(2,1)S(1)}, u32[]{:S(2)}, u32[]{:S(2)}) collective-permute-start(bf16[400,1024]{1,0:T(8,128)(2,1)S(1)} %collective-permute-done.14.refs_3_.refs_5_), channel_id=1, source_target_pairs={{4,0},{5,1},{6,2},{7,3},{8,4},{9,5},{10,6},{11,7},{12,8},{13,9},{1... | collective-permute-start | bytes 2457608 | tf_op jit(solution)/shard_map/ppermute | solution.py:408
  40.6 12.7 %collective-permute-start.11 = (bf16[400,1024]{1,0:T(8,128)(2,1)S(1)}, bf16[400,1024]{1,0:T(8,128)(2,1)S(1)}, u32[]{:S(2)}, u32[]{:S(2)}) collective-permute-start(bf16[400,1024]{1,0:T(8,128)(2,1)S(1)} %collective-permute-done.10.refs_7_.refs_5_.refs_2_), channel_id=1, source_target_pairs={{12,0},{13,1},{14,2},{15,3},{0,4},{1,5},{2,6},{3,7},{4,8},{5,9},{6... | collective-permute-start | bytes 2457608 | tf_op jit(solution)/shard_map/ppermute | solution.py:409
  40.6 15.2 %collective-permute-start.8 = (bf16[400,1024]{1,0:T(8,128)(2,1)S(1)}, bf16[400,1024]{1,0:T(8,128)(2,1)S(1)}, u32[]{:S(2)}, u32[]{:S(2)}) collective-permute-start(bf16[400,1024]{1,0:T(8,128)(2,1)S(1)} %collective-permute-done.7.refs_0_.refs_2_), channel_id=1, source_target_pairs={{1,0},{2,1},{3,2},{0,3},{5,4},{6,5},{7,6},{4,7},{9,8},{10,9},{11,1... | collective-permute-start | bytes 2457608 | tf_op jit(solution)/shard_map/ppermute | solution.py:407

commit v5 on v4

--- a/solution.py
+++ b/solution.py
@@ -32,7 +32,7 @@
     "next": (192, 384),
     "rest": (192, 768),
 }
-CODE_ROWS = 16
+CODE_ROWS = 8
 OWN, UP, RIGHT, LEFT, OVER, UP2 = range(6)
 OFFSETS = ((0, 0), (0, 1), (1, 0), (3, 0), (2, 0), (0, 2))
 
@@ -125,6 +125,7 @@
         (((1,), (1,)), ((), ())),
         preferred_element_type=jnp.float32,
     )
+    codes = codes[:CODE_ROWS]
     for i, copy in zip(range(0, ROWS, CHUNK), copies, strict=True):
         copy.wait()
         widened = emb[pl.ds(i, CHUNK), :].astype(jnp.float32)

time: 77.3 us -> 75.9 us (0.982)
  waiting for transfers between devices: 15.1 us -> 14.2 us
  transfers between devices with their start and end apart: 17 -> 17, of which waited for: 6 -> 7; matrix products, arithmetic and copies ran while one was open for 0% -> 0% of each run, Pallas kernels for 17% -> 17%
where the time goes in v5:
time: 75.9 us; the launch traced here: 75.7 us
  starting transfers between devices  24.2 us (32%)
  Pallas kernels  18.7 us (25%)
  blocking collectives  18.5 us (24%)
  waiting for transfers between devices  14.2 us (19%)
    all_to_all x1, blocking collectives, per_device(): got = lax.all_to_all(sent, AXES, split_axis=0, concat_axis=0, tiled=True)  18.5 us
    pallas_call x5, Pallas kernels, meet(): pl.pallas_call(functools.partial(meet_kernel, names, steps, before is not...  13.3 us
    ppermute x7, starting transfers between devices, per_device(): send(pieces[i], perm=packet_pairs(i))  12 us
    ppermute x1, waiting for transfers between devices, per_device(): held[LEFT, 'bottom'] = send(bottom, perm=left)  5.7 us
    ppermute x1, waiting for transfers between devices, per_device(): held[UP, 'top'] = send(top, perm=up)  4.09 us
    pallas_call x1, Pallas kernels, pack(): pl.pallas_call(pack_kernel, out_shape=[jax.ShapeDtypeStruct((1, ROWS), jn...  3.25 us
    ppermute x1, starting transfers between devices, per_device(): held[RIGHT, 'top'] = send(top, perm=right)  1.97 us
    ppermute x1, starting transfers between devices, per_device(): held[UP, 'top'] = send(top, perm=up)  1.77 us
  transfers between devices with their start and end apart: 17, of which 7 were waited for; matrix products, arithmetic and copies ran while one was open for 0% of the time, Pallas kernels for 17%

profile of v5, /device:TPU:1, one launch (start us, length us, event | category | flops | bytes accessed | tf_op | source)
XLA Modules:
  0.0 75.7 jit_solution(3430265243802626116)
XLA Ops:
  0.0 3.2 %shard_map.37 = (s32[1,768]{1,0:T(1,128)S(1)}, bf16[104,1024]{1,0:T(8,128)(2,1)S(1)}, bf16[104,1024]{1,0:T(8,128)(2,1)S(1)}, bf16[104,1024]{1,0:T(8,128)(2,1)S(1...) custom-call(bf16[768,1024]{1,0:T(8,128)(2,1)} %emb_hbm.1, ...), custom_call_target="tpu_custom_call" | custom-call | tf_op jit(solution)/shard_map/pallas_call | solution.py:152
  3.3 1.5 %collective-permute-start = (bf16[104,1024]{1,0:T(8,128)(2,1)S(1)}, bf16[104,1024]{1,0:T(8,128)(2,1)S(1)}, u32[]{:S(2)}, u32[]{:S(2)}) collective-permute-start(bf16[104,1024]{1,0:T(8,128)(2,1)S(1)} %get-tuple-element.18), channel_id=1, source_target_pairs={{0,16},{1,17},{2,18},{3,19},{4,20},{5,21},{6,22},{7,23},{8,24},{9,... | collective-permute-start | bytes 638984 | tf_op jit(solution)/shard_map/ppermute | solution.py:397
  4.8 1.4 %collective-permute-start.1 = (bf16[104,1024]{1,0:T(8,128)(2,1)S(1)}, bf16[104,1024]{1,0:T(8,128)(2,1)S(1)}, u32[]{:S(2)}, u32[]{:S(2)}) collective-permute-start(bf16[104,1024]{1,0:T(8,128)(2,1)S(1)} %get-tuple-element.19), channel_id=1, source_target_pairs={{0,32},{1,33},{2,34},{3,35},{4,36},{5,37},{6,38},{7,39},{8,40},{9,... | collective-permute-start | bytes 638984 | tf_op jit(solution)/shard_map/ppermute | solution.py:397
  6.1 1.4 %collective-permute-start.2 = (bf16[104,1024]{1,0:T(8,128)(2,1)S(1)}, bf16[104,1024]{1,0:T(8,128)(2,1)S(1)}, u32[]{:S(2)}, u32[]{:S(2)}) collective-permute-start(bf16[104,1024]{1,0:T(8,128)(2,1)S(1)} %get-tuple-element.20), channel_id=1, source_target_pairs={{0,20},{1,21},{2,22},{3,23},{4,24},{5,25},{6,26},{7,27},{8,28},{9,... | collective-permute-start | bytes 638984 | tf_op jit(solution)/shard_map/ppermute | solution.py:397
  7.5 2.9 %collective-permute-start.3 = (bf16[104,1024]{1,0:T(8,128)(2,1)S(1)}, bf16[104,1024]{1,0:T(8,128)(2,1)S(1)}, u32[]{:S(2)}, u32[]{:S(2)}) collective-permute-start(bf16[104,1024]{1,0:T(8,128)(2,1)S(1)} %get-tuple-element.21), channel_id=1, source_target_pairs={{0,64},{1,65},{2,66},{3,67},{4,68},{5,69},{6,70},{7,71},{8,72},{9,... | collective-permute-start | bytes 638984 | tf_op jit(solution)/shard_map/ppermute | solution.py:397
  10.4 0.5 collective-permute-start.4
  11.0 1.4 %collective-permute-start.5 = (bf16[104,1024]{1,0:T(8,128)(2,1)S(1)}, bf16[104,1024]{1,0:T(8,128)(2,1)S(1)}, u32[]{:S(2)}, u32[]{:S(2)}) collective-permute-start(bf16[104,1024]{1,0:T(8,128)(2,1)S(1)} %get-tuple-element.23), channel_id=1, source_target_pairs={{0,96},{1,97},{2,98},{3,99},{4,100},{5,101},{6,102},{7,103},{8,104... | collective-permute-start | bytes 638984 | tf_op jit(solution)/shard_map/ppermute | solution.py:397
  12.4 2.9 %collective-permute-start.6 = (bf16[104,1024]{1,0:T(8,128)(2,1)S(1)}, bf16[104,1024]{1,0:T(8,128)(2,1)S(1)}, u32[]{:S(2)}, u32[]{:S(2)}) collective-permute-start(bf16[104,1024]{1,0:T(8,128)(2,1)S(1)} %get-tuple-element.24), channel_id=1, source_target_pairs={{0,28},{1,29},{2,30},{3,31},{4,16},{5,17},{6,18},{7,19},{8,20},{9,... | collective-permute-start | bytes 638984 | tf_op jit(solution)/shard_map/ppermute | solution.py:397
  15.3 0.1 shard_map.38.refs_0_.refs_1_.refs_6_
  15.3 1.8 %collective-permute-start.12 = (bf16[392,1024]{1,0:T(8,128)(2,1)S(1)}, bf16[392,1024]{1,0:T(8,128)(2,1)S(1)}, u32[]{:S(2)}, u32[]{:S(2)}) collective-permute-start(bf16[392,1024]{1,0:T(8,128)(2,1)S(1)} %shard_map.38.refs_0_.refs_1_.refs_6_), channel_id=1, source_target_pairs={{1,0},{2,1},{3,2},{0,3},{5,4},{6,5},{7,6},{4,7},{9,8},{10,9},{11,1... | collective-permute-start | bytes 2408456 | tf_op jit(solution)/shard_map/ppermute | solution.py:401
  17.1 1.3 %collective-permute-done.3.refs_1_ = bf16[104,1024]{1,0:T(8,128)(2,1)S(1)} collective-permute-done((bf16[104,1024]{1,0:T(8,128)(2,1)S(1)}, bf16[104,1024]{1,0:T(8,128)(2,1)S(1)}, u32[]{:S(2)}, u32[]{:S(2)}) %collective-permute-start.3) | collective-permute-done | bytes 213024 | tf_op jit(solution)/shard_map/ppermute | solution.py:397
  18.4 0.9 %collective-permute-start.9 = (bf16[392,1024]{1,0:T(8,128)(2,1)S(1)}, bf16[392,1024]{1,0:T(8,128)(2,1)S(1)}, u32[]{:S(2)}, u32[]{:S(2)}) collective-permute-start(bf16[392,1024]{1,0:T(8,128)(2,1)S(1)} %shard_map.38.refs_0_.refs_1_.refs_6_), channel_id=1, source_target_pairs={{12,0},{13,1},{14,2},{15,3},{0,4},{1,5},{2,6},{3,7},{4,8},{5,9},{6... | collective-permute-start | bytes 2408456 | tf_op jit(solution)/shard_map/ppermute | solution.py:404
  19.3 2.0 %collective-permute-start.14 = (bf16[392,1024]{1,0:T(8,128)(2,1)S(1)}, bf16[392,1024]{1,0:T(8,128)(2,1)S(1)}, u32[]{:S(2)}, u32[]{:S(2)}) collective-permute-start(bf16[392,1024]{1,0:T(8,128)(2,1)S(1)} %shard_map.38.refs_0_.refs_1_.refs_6_), channel_id=1, source_target_pairs={{4,0},{5,1},{6,2},{7,3},{8,4},{9,5},{10,6},{11,7},{12,8},{13,9},{1... | collective-permute-start | bytes 2408456 | tf_op jit(solution)/shard_map/ppermute | solution.py:403
  21.3 1.2 %shard_map.39 = (bf16[392,1024]{1,0:T(8,128)(2,1)S(1)}, f32[6,8,768]{2,1,0:T(8,128)S(1)}) custom-call(bf16[392,1024]{1,0:T(8,128)(2,1)S(1)} %shard_map.38.refs_0_.refs_1_.refs_6_, bf16[104,1024]{1,0:T(8,128)(2,1)S(1)} %collective-permute-done.3.refs_1_, bf16[104,1024]{1,0:T(8,128)(2,1)S(1)} %collective-permute-done.4.refs_2_, ...), custom_call_target="tpu_custom_call" | custom-call | tf_op jit(solution)/shard_map/pallas_call | solution.py:201
  22.5 0.9 %collective-permute-start.10 = (bf16[392,1024]{1,0:T(8,128)(2,1)S(1)}, bf16[392,1024]{1,0:T(8,128)(2,1)S(1)}, u32[]{:S(2)}, u32[]{:S(2)}) collective-permute-start(bf16[392,1024]{1,0:T(8,128)(2,1)S(1)} %get-tuple-element.25.refs_2_.refs_7_.refs_3_), channel_id=1, source_target_pairs={{12,0},{13,1},{14,2},{15,3},{0,4},{1,5},{2,6},{3,7},{4,8},{5,9},{6... | collective-permute-start | bytes 2408456 | tf_op jit(solution)/shard_map/ppermute | solution.py:406
  23.3 1.6 %collective-permute-start.7 = (bf16[392,1024]{1,0:T(8,128)(2,1)S(1)}, bf16[392,1024]{1,0:T(8,128)(2,1)S(1)}, u32[]{:S(2)}, u32[]{:S(2)}) collective-permute-start(bf16[392,1024]{1,0:T(8,128)(2,1)S(1)} %get-tuple-element.25.refs_2_.refs_7_.refs_3_), channel_id=1, source_target_pairs={{1,0},{2,1},{3,2},{0,3},{5,4},{6,5},{7,6},{4,7},{9,8},{10,9},{11,1... | collective-permute-start | bytes 2408456 | tf_op jit(solution)/shard_map/ppermute | solution.py:402
  25.0 4.1 %collective-permute-done.12.refs_0_.refs_4_.refs_1_ = bf16[392,1024]{1,0:T(8,128)(2,1)S(1)} collective-permute-done((bf16[392,1024]{1,0:T(8,128)(2,1)S(1)}, bf16[392,1024]{1,0:T(8,128)(2,1)S(1)}, u32[]{:S(2)}, u32[]{:S(2)}) %collective-permute-start.12) | collective-permute-done | bytes 802848 | tf_op jit(solution)/shard_map/ppermute | solution.py:401
  29.1 0.5 collective-permute-start.16
  29.6 1.3 %collective-permute-done.9.refs_4_.refs_6_.refs_1_ = bf16[392,1024]{1,0:T(8,128)(2,1)S(1)} collective-permute-done((bf16[392,1024]{1,0:T(8,128)(2,1)S(1)}, bf16[392,1024]{1,0:T(8,128)(2,1)S(1)}, u32[]{:S(2)}, u32[]{:S(2)}) %collective-permute-start.9) | collective-permute-done | bytes 802848 | tf_op jit(solution)/shard_map/ppermute | solution.py:404
  30.9 1.6 %collective-permute-start.13 = (bf16[392,1024]{1,0:T(8,128)(2,1)S(1)}, bf16[392,1024]{1,0:T(8,128)(2,1)S(1)}, u32[]{:S(2)}, u32[]{:S(2)}) collective-permute-start(bf16[392,1024]{1,0:T(8,128)(2,1)S(1)} %collective-permute-done.12.refs_0_.refs_4_.refs_1_), channel_id=1, source_target_pairs={{1,0},{2,1},{3,2},{0,3},{5,4},{6,5},{7,6},{4,7},{9,8},{10,9},{11,1... | collective-permute-start | bytes 2408456 | tf_op jit(solution)/shard_map/ppermute | solution.py:407
  32.6 1.3 %collective-permute-start.15 = (bf16[392,1024]{1,0:T(8,128)(2,1)S(1)}, bf16[392,1024]{1,0:T(8,128)(2,1)S(1)}, u32[]{:S(2)}, u32[]{:S(2)}) collective-permute-start(bf16[392,1024]{1,0:T(8,128)(2,1)S(1)} %collective-permute-done.14.refs_3_.refs_5_), channel_id=1, source_target_pairs={{4,0},{5,1},{6,2},{7,3},{8,4},{9,5},{10,6},{11,7},{12,8},{13,9},{1... | collective-permute-start | bytes 2408456 | tf_op jit(solution)/shard_map/ppermute | solution.py:409
  33.8 5.7 %collective-permute-done.10.refs_7_.refs_5_.refs_2_ = bf16[392,1024]{1,0:T(8,128)(2,1)S(1)} collective-permute-done((bf16[392,1024]{1,0:T(8,128)(2,1)S(1)}, bf16[392,1024]{1,0:T(8,128)(2,1)S(1)}, u32[]{:S(2)}, u32[]{:S(2)}) %collective-permute-start.10) | collective-permute-done | bytes 802848 | tf_op jit(solution)/shard_map/ppermute | solution.py:406
  39.5 1.6 %collective-permute-start.8 = (bf16[392,1024]{1,0:T(8,128)(2,1)S(1)}, bf16[392,1024]{1,0:T(8,128)(2,1)S(1)}, u32[]{:S(2)}, u32[]{:S(2)}) collective-permute-start(bf16[392,1024]{1,0:T(8,128)(2,1)S(1)} %collective-permute-done.7.refs_0_.refs_2_), channel_id=1, source_target_pairs={{1,0},{2,1},{3,2},{0,3},{5,4},{6,5},{7,6},{4,7},{9,8},{10,9},{11,1... | collective-permute-start | bytes 2408456 | tf_op jit(solution)/shard_map/ppermute | solution.py:408
  41.2 2.5 %shard_map.40.refs_8_ = f32[6,8,768]{2,1,0:T(8,128)S(1)} custom-call(bf16[392,1024]{1,0:T(8,128)(2,1)S(1)} %collective-permute-done.12.refs_0_.refs_4_.refs_1_, bf16[392,1024]{1,0:T(8,128)(2,1)S(1)} %shard_map.38.refs_0_.refs_1_.refs_6_, bf16[392,1024]{1,0:T(8,128)(2,1)S(1)} %get-tuple-element.25.refs_2_.refs_7_.refs_3_, ...), custom_call_target="tpu_custom_call" | custom-call | flops 10871635968 | bytes 3932160 | tf_op jit(solution)/shard_map/pallas_call | solution.py:340
  43.7 5.2 %shard_map.41.refs_8_ = f32[6,8,768]{2,1,0:T(8,128)S(1)} custom-call(bf16[392,1024]{1,0:T(8,128)(2,1)S(1)} %collective-permute-done.7.refs_0_.refs_2_, bf16[392,1024]{1,0:T(8,128)(2,1)S(1)} %shard_map.38.refs_0_.refs_1_.refs_6_, bf16[392,1024]{1,0:T(8,128)(2,1)S(1)} %get-tuple-element.25.refs_2_.refs_7_.refs_3_, ...), custom_call_target="tpu_custom_call" | custom-call | flops 16911433728 | bytes 6291456 | tf_op jit(solution)/shard_map/pallas_call | solution.py:340
  49.0 2.6 %shard_map.42.refs_4_ = f32[6,8,768]{2,1,0:T(8,128)S(1)} custom-call(bf16[392,1024]{1,0:T(8,128)(2,1)S(1)} %collective-permute-done.15.refs_0_, bf16[392,1024]{1,0:T(8,128)(2,1)S(1)} %collective-permute-done.12.refs_0_.refs_4_.refs_1_, bf16[392,1024]{1,0:T(8,128)(2,1)S(1)} %collective-permute-done.7.refs_0_.refs_2_, ...), custom_call_target="tpu_custom_call" | custom-call | flops 8455716864 | bytes 6291456 | tf_op jit(solution)/shard_map/pallas_call | solution.py:340
  51.5 0.5 collective-permute-done.11.refs_0_.refs_4_
  52.1 1.3 %shard_map.43.refs_5_ = f32[6,8,768]{2,1,0:T(8,128)S(1)} custom-call(bf16[392,1024]{1,0:T(8,128)(2,1)S(1)} %collective-permute-done.11.refs_0_.refs_4_, bf16[392,1024]{1,0:T(8,128)(2,1)S(1)} %collective-permute-done.12.refs_0_.refs_4_.refs_1_, bf16[392,1024]{1,0:T(8,128)(2,1)S(1)} %collective-permute-done.7.refs_0_.refs_2_, ...), custom_call_target="tpu_custom_call" | custom-call | flops 3623878656 | bytes 3145728 | tf_op jit(solution)/shard_map/pallas_call | solution.py:340
  53.4 1.2 %collective-permute-done.8.refs_0_ = bf16[392,1024]{1,0:T(8,128)(2,1)S(1)} collective-permute-done((bf16[392,1024]{1,0:T(8,128)(2,1)S(1)}, bf16[392,1024]{1,0:T(8,128)(2,1)S(1)}, u32[]{:S(2)}, u32[]{:S(2)}) %collective-permute-start.8) | collective-permute-done | bytes 802848 | tf_op jit(solution)/shard_map/ppermute | solution.py:408
  54.6 1.7 %shard_map.44 = f32[128,128]{1,0:T(8,128)S(1)} custom-call(bf16[392,1024]{1,0:T(8,128)(2,1)S(1)} %collective-permute-done.8.refs_0_, bf16[392,1024]{1,0:T(8,128)(2,1)S(1)} %collective-permute-done.9.refs_4_.refs_6_.refs_1_, bf16[392,1024]{1,0:T(8,128)(2,1)S(1)} %collective-permute-done.10.refs_7_.refs_5_.refs_2_, ...), custom_call_target="tpu_custom_call" | custom-call | flops 4831838208 | bytes 3932160 | tf_op jit(solution)/shard_map/pallas_call | solution.py:340
  56.3 18.5 %all_to_all.11 = f32[128,1,128]{2,1,0:T(1,128)S(1)} all-to-all(f32[128,1,128]{2,1,0:T(1,128)S(1)} %bitcast.5), channel_id=1, replica_groups=mesh['clus'=8,'fold'=16] {'clus','fold'}, dimensions={0} | all-to-all | bytes 131072 | tf_op jit(solution)/shard_map/all_to_all | solution.py:459
  74.8 0.9 %shard_map.45 = f32[768]{0:T(1024)} custom-call(s32[1,768]{1,0:T(1,128)S(1)} %get-tuple-element.16.slot_ref, f32[128,128]{1,0:T(8,128)S(1)} %bitcast.4), custom_call_target="tpu_custom_call" | custom-call | tf_op jit(solution)/shard_map/pallas_call | solution.py:379
  (12 shorter events, 0.1 us)
Async XLA Ops:
  3.3 7.7 %collective-permute-start = (bf16[104,1024]{1,0:T(8,128)(2,1)S(1)}, bf16[104,1024]{1,0:T(8,128)(2,1)S(1)}, u32[]{:S(2)}, u32[]{:S(2)}) collective-permute-start(bf16[104,1024]{1,0:T(8,128)(2,1)S(1)} %get-tuple-element.18), channel_id=1, source_target_pairs={{0,16},{1,17},{2,18},{3,19},{4,20},{5,21},{6,22},{7,23},{8,24},{9,... | collective-permute-start | bytes 638984 | tf_op jit(solution)/shard_map/ppermute | solution.py:397
  4.8 7.6 %collective-permute-start.1 = (bf16[104,1024]{1,0:T(8,128)(2,1)S(1)}, bf16[104,1024]{1,0:T(8,128)(2,1)S(1)}, u32[]{:S(2)}, u32[]{:S(2)}) collective-permute-start(bf16[104,1024]{1,0:T(8,128)(2,1)S(1)} %get-tuple-element.19), channel_id=1, source_target_pairs={{0,32},{1,33},{2,34},{3,35},{4,36},{5,37},{6,38},{7,39},{8,40},{9,... | collective-permute-start | bytes 638984 | tf_op jit(solution)/shard_map/ppermute | solution.py:397
  6.1 9.1 %collective-permute-start.2 = (bf16[104,1024]{1,0:T(8,128)(2,1)S(1)}, bf16[104,1024]{1,0:T(8,128)(2,1)S(1)}, u32[]{:S(2)}, u32[]{:S(2)}) collective-permute-start(bf16[104,1024]{1,0:T(8,128)(2,1)S(1)} %get-tuple-element.20), channel_id=1, source_target_pairs={{0,20},{1,21},{2,22},{3,23},{4,24},{5,25},{6,26},{7,27},{8,28},{9,... | collective-permute-start | bytes 638984 | tf_op jit(solution)/shard_map/ppermute | solution.py:397
  7.5 10.9 %collective-permute-start.3 = (bf16[104,1024]{1,0:T(8,128)(2,1)S(1)}, bf16[104,1024]{1,0:T(8,128)(2,1)S(1)}, u32[]{:S(2)}, u32[]{:S(2)}) collective-permute-start(bf16[104,1024]{1,0:T(8,128)(2,1)S(1)} %get-tuple-element.21), channel_id=1, source_target_pairs={{0,64},{1,65},{2,66},{3,67},{4,68},{5,69},{6,70},{7,71},{8,72},{9,... | collective-permute-start | bytes 638984 | tf_op jit(solution)/shard_map/ppermute | solution.py:397
  10.4 8.9 %collective-permute-start.4 = (bf16[104,1024]{1,0:T(8,128)(2,1)S(1)}, bf16[104,1024]{1,0:T(8,128)(2,1)S(1)}, u32[]{:S(2)}, u32[]{:S(2)}) collective-permute-start(bf16[104,1024]{1,0:T(8,128)(2,1)S(1)} %get-tuple-element.22), channel_id=1, source_target_pairs={{0,24},{1,25},{2,26},{3,27},{4,28},{5,29},{6,30},{7,31},{8,16},{9,... | collective-permute-start | bytes 638984 | tf_op jit(solution)/shard_map/ppermute | solution.py:397
  11.0 10.3 %collective-permute-start.5 = (bf16[104,1024]{1,0:T(8,128)(2,1)S(1)}, bf16[104,1024]{1,0:T(8,128)(2,1)S(1)}, u32[]{:S(2)}, u32[]{:S(2)}) collective-permute-start(bf16[104,1024]{1,0:T(8,128)(2,1)S(1)} %get-tuple-element.23), channel_id=1, source_target_pairs={{0,96},{1,97},{2,98},{3,99},{4,100},{5,101},{6,102},{7,103},{8,104... | collective-permute-start | bytes 638984 | tf_op jit(solution)/shard_map/ppermute | solution.py:397
  12.4 9.0 %collective-permute-start.6 = (bf16[104,1024]{1,0:T(8,128)(2,1)S(1)}, bf16[104,1024]{1,0:T(8,128)(2,1)S(1)}, u32[]{:S(2)}, u32[]{:S(2)}) collective-permute-start(bf16[104,1024]{1,0:T(8,128)(2,1)S(1)} %get-tuple-element.24), channel_id=1, source_target_pairs={{0,28},{1,29},{2,30},{3,31},{4,16},{5,17},{6,18},{7,19},{8,20},{9,... | collective-permute-start | bytes 638984 | tf_op jit(solution)/shard_map/ppermute | solution.py:397
  15.3 13.7 %collective-permute-start.12 = (bf16[392,1024]{1,0:T(8,128)(2,1)S(1)}, bf16[392,1024]{1,0:T(8,128)(2,1)S(1)}, u32[]{:S(2)}, u32[]{:S(2)}) collective-permute-start(bf16[392,1024]{1,0:T(8,128)(2,1)S(1)} %shard_map.38.refs_0_.refs_1_.refs_6_), channel_id=1, source_target_pairs={{1,0},{2,1},{3,2},{0,3},{5,4},{6,5},{7,6},{4,7},{9,8},{10,9},{11,1... | collective-permute-start | bytes 2408456 | tf_op jit(solution)/shard_map/ppermute | solution.py:401
  18.4 12.5 %collective-permute-start.9 = (bf16[392,1024]{1,0:T(8,128)(2,1)S(1)}, bf16[392,1024]{1,0:T(8,128)(2,1)S(1)}, u32[]{:S(2)}, u32[]{:S(2)}) collective-permute-start(bf16[392,1024]{1,0:T(8,128)(2,1)S(1)} %shard_map.38.refs_0_.refs_1_.refs_6_), channel_id=1, source_target_pairs={{12,0},{13,1},{14,2},{15,3},{0,4},{1,5},{2,6},{3,7},{4,8},{5,9},{6... | collective-permute-start | bytes 2408456 | tf_op jit(solution)/shard_map/ppermute | solution.py:404
  19.3 13.2 %collective-permute-start.14 = (bf16[392,1024]{1,0:T(8,128)(2,1)S(1)}, bf16[392,1024]{1,0:T(8,128)(2,1)S(1)}, u32[]{:S(2)}, u32[]{:S(2)}) collective-permute-start(bf16[392,1024]{1,0:T(8,128)(2,1)S(1)} %shard_map.38.refs_0_.refs_1_.refs_6_), channel_id=1, source_target_pairs={{4,0},{5,1},{6,2},{7,3},{8,4},{9,5},{10,6},{11,7},{12,8},{13,9},{1... | collective-permute-start | bytes 2408456 | tf_op jit(solution)/shard_map/ppermute | solution.py:403
  22.5 17.1 %collective-permute-start.10 = (bf16[392,1024]{1,0:T(8,128)(2,1)S(1)}, bf16[392,1024]{1,0:T(8,128)(2,1)S(1)}, u32[]{:S(2)}, u32[]{:S(2)}) collective-permute-start(bf16[392,1024]{1,0:T(8,128)(2,1)S(1)} %get-tuple-element.25.refs_2_.refs_7_.refs_3_), channel_id=1, source_target_pairs={{12,0},{13,1},{14,2},{15,3},{0,4},{1,5},{2,6},{3,7},{4,8},{5,9},{6... | collective-permute-start | bytes 2408456 | tf_op jit(solution)/shard_map/ppermute | solution.py:406
  23.3 16.2 %collective-permute-start.7 = (bf16[392,1024]{1,0:T(8,128)(2,1)S(1)}, bf16[392,1024]{1,0:T(8,128)(2,1)S(1)}, u32[]{:S(2)}, u32[]{:S(2)}) collective-permute-start(bf16[392,1024]{1,0:T(8,128)(2,1)S(1)} %get-tuple-element.25.refs_2_.refs_7_.refs_3_), channel_id=1, source_target_pairs={{1,0},{2,1},{3,2},{0,3},{5,4},{6,5},{7,6},{4,7},{9,8},{10,9},{11,1... | collective-permute-start | bytes 2408456 | tf_op jit(solution)/shard_map/ppermute | solution.py:402
  29.1 14.6 %collective-permute-start.16 = (bf16[392,1024]{1,0:T(8,128)(2,1)S(1)}, bf16[392,1024]{1,0:T(8,128)(2,1)S(1)}, u32[]{:S(2)}, u32[]{:S(2)}) collective-permute-start(bf16[392,1024]{1,0:T(8,128)(2,1)S(1)} %get-tuple-element.25.refs_2_.refs_7_.refs_3_), channel_id=1, source_target_pairs={{4,0},{5,1},{6,2},{7,3},{8,4},{9,5},{10,6},{11,7},{12,8},{13,9},{1... | collective-permute-start | bytes 2408456 | tf_op jit(solution)/shard_map/ppermute | solution.py:405
  30.9 18.0 %collective-permute-start.13 = (bf16[392,1024]{1,0:T(8,128)(2,1)S(1)}, bf16[392,1024]{1,0:T(8,128)(2,1)S(1)}, u32[]{:S(2)}, u32[]{:S(2)}) collective-permute-start(bf16[392,1024]{1,0:T(8,128)(2,1)S(1)} %collective-permute-done.12.refs_0_.refs_4_.refs_1_), channel_id=1, source_target_pairs={{1,0},{2,1},{3,2},{0,3},{5,4},{6,5},{7,6},{4,7},{9,8},{10,9},{11,1... | collective-permute-start | bytes 2408456 | tf_op jit(solution)/shard_map/ppermute | solution.py:407
  32.6 16.4 %collective-permute-start.15 = (bf16[392,1024]{1,0:T(8,128)(2,1)S(1)}, bf16[392,1024]{1,0:T(8,128)(2,1)S(1)}, u32[]{:S(2)}, u32[]{:S(2)}) collective-permute-start(bf16[392,1024]{1,0:T(8,128)(2,1)S(1)} %collective-permute-done.14.refs_3_.refs_5_), channel_id=1, source_target_pairs={{4,0},{5,1},{6,2},{7,3},{8,4},{9,5},{10,6},{11,7},{12,8},{13,9},{1... | collective-permute-start | bytes 2408456 | tf_op jit(solution)/shard_map/ppermute | solution.py:409
  39.5 12.5 %collective-permute-start.11 = (bf16[392,1024]{1,0:T(8,128)(2,1)S(1)}, bf16[392,1024]{1,0:T(8,128)(2,1)S(1)}, u32[]{:S(2)}, u32[]{:S(2)}) collective-permute-start(bf16[392,1024]{1,0:T(8,128)(2,1)S(1)} %collective-permute-done.10.refs_7_.refs_5_.refs_2_), channel_id=1, source_target_pairs={{12,0},{13,1},{14,2},{15,3},{0,4},{1,5},{2,6},{3,7},{4,8},{5,9},{6... | collective-permute-start | bytes 2408456 | tf_op jit(solution)/shard_map/ppermute | solution.py:410
  39.5 15.0 %collective-permute-start.8 = (bf16[392,1024]{1,0:T(8,128)(2,1)S(1)}, bf16[392,1024]{1,0:T(8,128)(2,1)S(1)}, u32[]{:S(2)}, u32[]{:S(2)}) collective-permute-start(bf16[392,1024]{1,0:T(8,128)(2,1)S(1)} %collective-permute-done.7.refs_0_.refs_2_), channel_id=1, source_target_pairs={{1,0},{2,1},{3,2},{0,3},{5,4},{6,5},{7,6},{4,7},{9,8},{10,9},{11,1... | collective-permute-start | bytes 2408456 | tf_op jit(solution)/shard_map/ppermute | solution.py:408

commit v6 on v5

--- a/solution.py
+++ b/solution.py
@@ -20,7 +20,7 @@
 LO = 128
 FAR = 1.0e6
 WIDE = 256
-CHUNK = 256
+CHUNK = 768
 VMEM = 12 * 1024 * 1024
 RING_ORDER = (0, 1, 2, 3)
 RING_START = tuple(2 * PIECE * RING_ORDER.index(i) for i in range(4))
@@ -423,8 +423,8 @@
         [
             ((UP, "bottom"), [(OWN, "all")], None),
             ((RIGHT, "bottom"), [(OWN, "all")], None),
+            ((UP, "all"), [(LEFT, "all")], None),
             ((UP, "all"), [(RIGHT, "all")], None),
-            ((UP, "all"), [(LEFT, "all")], None),
             ((RIGHT, "top"), [(LEFT, "bottom")], None),
             ((RIGHT, "bottom"), [(LEFT, "bottom")], ("u", 1)),
         ],

time: 75.9 us -> 75.7 us (level)
  transfers between devices with their start and end apart: 17 -> 17, of which waited for: 7 -> 6; matrix products, arithmetic and copies ran while one was open for 0% -> 0% of each run, Pallas kernels for 17% -> 17%
where the time goes in v6:
time: 75.7 us; the launch traced here: 75.6 us
  starting transfers between devices  24.3 us (32%)
  blocking collectives  18.6 us (25%)
  Pallas kernels  18.5 us (24%)
  waiting for transfers between devices  14.1 us (19%)
    all_to_all x1, blocking collectives, per_device(): got = lax.all_to_all(sent, AXES, split_axis=0, concat_axis=0, tiled=True)  18.6 us
    pallas_call x5, Pallas kernels, meet(): pl.pallas_call(functools.partial(meet_kernel, names, steps, before is not...  13.3 us
    ppermute x7, starting transfers between devices, per_device(): send(pieces[i], perm=packet_pairs(i))  12 us
    ppermute x1, waiting for transfers between devices, per_device(): held[LEFT, 'bottom'] = send(bottom, perm=left)  5.67 us
    ppermute x1, waiting for transfers between devices, per_device(): held[UP, 'top'] = send(top, perm=up)  4.09 us
    pallas_call x1, Pallas kernels, pack(): pl.pallas_call(pack_kernel, out_shape=[jax.ShapeDtypeStruct((1, ROWS), jn...  3.06 us
    ppermute x1, starting transfers between devices, per_device(): held[RIGHT, 'top'] = send(top, perm=right)  1.98 us
    ppermute x1, starting transfers between devices, per_device(): held[UP, 'top'] = send(top, perm=up)  1.77 us
  transfers between devices with their start and end apart: 17, of which 6 were waited for; matrix products, arithmetic and copies ran while one was open for 0% of the time, Pallas kernels for 17%

profile of v6, /device:TPU:1, one launch (start us, length us, event | category | flops | bytes accessed | tf_op | source)
XLA Modules:
  0.0 75.6 jit_solution(17339735372032240193)
XLA Ops:
  0.0 3.1 %shard_map.37 = (s32[1,768]{1,0:T(1,128)S(1)}, bf16[104,1024]{1,0:T(8,128)(2,1)S(1)}, bf16[104,1024]{1,0:T(8,128)(2,1)S(1)}, bf16[104,1024]{1,0:T(8,128)(2,1)S(1...) custom-call(bf16[768,1024]{1,0:T(8,128)(2,1)} %emb_hbm.1, ...), custom_call_target="tpu_custom_call" | custom-call | tf_op jit(solution)/shard_map/pallas_call | solution.py:152
  3.1 1.5 %collective-permute-start = (bf16[104,1024]{1,0:T(8,128)(2,1)S(1)}, bf16[104,1024]{1,0:T(8,128)(2,1)S(1)}, u32[]{:S(2)}, u32[]{:S(2)}) collective-permute-start(bf16[104,1024]{1,0:T(8,128)(2,1)S(1)} %get-tuple-element.18), channel_id=1, source_target_pairs={{0,16},{1,17},{2,18},{3,19},{4,20},{5,21},{6,22},{7,23},{8,24},{9,... | collective-permute-start | bytes 638984 | tf_op jit(solution)/shard_map/ppermute | solution.py:397
  4.6 1.4 %collective-permute-start.1 = (bf16[104,1024]{1,0:T(8,128)(2,1)S(1)}, bf16[104,1024]{1,0:T(8,128)(2,1)S(1)}, u32[]{:S(2)}, u32[]{:S(2)}) collective-permute-start(bf16[104,1024]{1,0:T(8,128)(2,1)S(1)} %get-tuple-element.19), channel_id=1, source_target_pairs={{0,32},{1,33},{2,34},{3,35},{4,36},{5,37},{6,38},{7,39},{8,40},{9,... | collective-permute-start | bytes 638984 | tf_op jit(solution)/shard_map/ppermute | solution.py:397
  5.9 1.4 %collective-permute-start.2 = (bf16[104,1024]{1,0:T(8,128)(2,1)S(1)}, bf16[104,1024]{1,0:T(8,128)(2,1)S(1)}, u32[]{:S(2)}, u32[]{:S(2)}) collective-permute-start(bf16[104,1024]{1,0:T(8,128)(2,1)S(1)} %get-tuple-element.20), channel_id=1, source_target_pairs={{0,20},{1,21},{2,22},{3,23},{4,24},{5,25},{6,26},{7,27},{8,28},{9,... | collective-permute-start | bytes 638984 | tf_op jit(solution)/shard_map/ppermute | solution.py:397
  7.3 2.9 %collective-permute-start.3 = (bf16[104,1024]{1,0:T(8,128)(2,1)S(1)}, bf16[104,1024]{1,0:T(8,128)(2,1)S(1)}, u32[]{:S(2)}, u32[]{:S(2)}) collective-permute-start(bf16[104,1024]{1,0:T(8,128)(2,1)S(1)} %get-tuple-element.21), channel_id=1, source_target_pairs={{0,64},{1,65},{2,66},{3,67},{4,68},{5,69},{6,70},{7,71},{8,72},{9,... | collective-permute-start | bytes 638984 | tf_op jit(solution)/shard_map/ppermute | solution.py:397
  10.2 0.5 collective-permute-start.4
  10.8 1.4 %collective-permute-start.5 = (bf16[104,1024]{1,0:T(8,128)(2,1)S(1)}, bf16[104,1024]{1,0:T(8,128)(2,1)S(1)}, u32[]{:S(2)}, u32[]{:S(2)}) collective-permute-start(bf16[104,1024]{1,0:T(8,128)(2,1)S(1)} %get-tuple-element.23), channel_id=1, source_target_pairs={{0,96},{1,97},{2,98},{3,99},{4,100},{5,101},{6,102},{7,103},{8,104... | collective-permute-start | bytes 638984 | tf_op jit(solution)/shard_map/ppermute | solution.py:397
  12.2 2.9 %collective-permute-start.6 = (bf16[104,1024]{1,0:T(8,128)(2,1)S(1)}, bf16[104,1024]{1,0:T(8,128)(2,1)S(1)}, u32[]{:S(2)}, u32[]{:S(2)}) collective-permute-start(bf16[104,1024]{1,0:T(8,128)(2,1)S(1)} %get-tuple-element.24), channel_id=1, source_target_pairs={{0,28},{1,29},{2,30},{3,31},{4,16},{5,17},{6,18},{7,19},{8,20},{9,... | collective-permute-start | bytes 638984 | tf_op jit(solution)/shard_map/ppermute | solution.py:397
  15.1 0.1 shard_map.38.refs_0_.refs_1_.refs_6_
  15.1 1.8 %collective-permute-start.12 = (bf16[392,1024]{1,0:T(8,128)(2,1)S(1)}, bf16[392,1024]{1,0:T(8,128)(2,1)S(1)}, u32[]{:S(2)}, u32[]{:S(2)}) collective-permute-start(bf16[392,1024]{1,0:T(8,128)(2,1)S(1)} %shard_map.38.refs_0_.refs_1_.refs_6_), channel_id=1, source_target_pairs={{1,0},{2,1},{3,2},{0,3},{5,4},{6,5},{7,6},{4,7},{9,8},{10,9},{11,1... | collective-permute-start | bytes 2408456 | tf_op jit(solution)/shard_map/ppermute | solution.py:401
  16.9 1.3 %collective-permute-done.3.refs_1_ = bf16[104,1024]{1,0:T(8,128)(2,1)S(1)} collective-permute-done((bf16[104,1024]{1,0:T(8,128)(2,1)S(1)}, bf16[104,1024]{1,0:T(8,128)(2,1)S(1)}, u32[]{:S(2)}, u32[]{:S(2)}) %collective-permute-start.3) | collective-permute-done | bytes 213024 | tf_op jit(solution)/shard_map/ppermute | solution.py:397
  18.2 0.9 %collective-permute-start.9 = (bf16[392,1024]{1,0:T(8,128)(2,1)S(1)}, bf16[392,1024]{1,0:T(8,128)(2,1)S(1)}, u32[]{:S(2)}, u32[]{:S(2)}) collective-permute-start(bf16[392,1024]{1,0:T(8,128)(2,1)S(1)} %shard_map.38.refs_0_.refs_1_.refs_6_), channel_id=1, source_target_pairs={{12,0},{13,1},{14,2},{15,3},{0,4},{1,5},{2,6},{3,7},{4,8},{5,9},{6... | collective-permute-start | bytes 2408456 | tf_op jit(solution)/shard_map/ppermute | solution.py:404
  19.1 2.0 %collective-permute-start.14 = (bf16[392,1024]{1,0:T(8,128)(2,1)S(1)}, bf16[392,1024]{1,0:T(8,128)(2,1)S(1)}, u32[]{:S(2)}, u32[]{:S(2)}) collective-permute-start(bf16[392,1024]{1,0:T(8,128)(2,1)S(1)} %shard_map.38.refs_0_.refs_1_.refs_6_), channel_id=1, source_target_pairs={{4,0},{5,1},{6,2},{7,3},{8,4},{9,5},{10,6},{11,7},{12,8},{13,9},{1... | collective-permute-start | bytes 2408456 | tf_op jit(solution)/shard_map/ppermute | solution.py:403
  21.1 1.2 %shard_map.39 = (bf16[392,1024]{1,0:T(8,128)(2,1)S(1)}, f32[6,8,768]{2,1,0:T(8,128)S(1)}) custom-call(bf16[392,1024]{1,0:T(8,128)(2,1)S(1)} %shard_map.38.refs_0_.refs_1_.refs_6_, bf16[104,1024]{1,0:T(8,128)(2,1)S(1)} %collective-permute-done.3.refs_1_, bf16[104,1024]{1,0:T(8,128)(2,1)S(1)} %collective-permute-done.4.refs_2_, ...), custom_call_target="tpu_custom_call" | custom-call | tf_op jit(solution)/shard_map/pallas_call | solution.py:201
  22.3 0.9 %collective-permute-start.10 = (bf16[392,1024]{1,0:T(8,128)(2,1)S(1)}, bf16[392,1024]{1,0:T(8,128)(2,1)S(1)}, u32[]{:S(2)}, u32[]{:S(2)}) collective-permute-start(bf16[392,1024]{1,0:T(8,128)(2,1)S(1)} %get-tuple-element.25.refs_2_.refs_7_.refs_3_), channel_id=1, source_target_pairs={{12,0},{13,1},{14,2},{15,3},{0,4},{1,5},{2,6},{3,7},{4,8},{5,9},{6... | collective-permute-start | bytes 2408456 | tf_op jit(solution)/shard_map/ppermute | solution.py:406
  23.2 1.6 %collective-permute-start.7 = (bf16[392,1024]{1,0:T(8,128)(2,1)S(1)}, bf16[392,1024]{1,0:T(8,128)(2,1)S(1)}, u32[]{:S(2)}, u32[]{:S(2)}) collective-permute-start(bf16[392,1024]{1,0:T(8,128)(2,1)S(1)} %get-tuple-element.25.refs_2_.refs_7_.refs_3_), channel_id=1, source_target_pairs={{1,0},{2,1},{3,2},{0,3},{5,4},{6,5},{7,6},{4,7},{9,8},{10,9},{11,1... | collective-permute-start | bytes 2408456 | tf_op jit(solution)/shard_map/ppermute | solution.py:402
  24.8 4.1 %collective-permute-done.12.refs_0_.refs_4_.refs_1_ = bf16[392,1024]{1,0:T(8,128)(2,1)S(1)} collective-permute-done((bf16[392,1024]{1,0:T(8,128)(2,1)S(1)}, bf16[392,1024]{1,0:T(8,128)(2,1)S(1)}, u32[]{:S(2)}, u32[]{:S(2)}) %collective-permute-start.12) | collective-permute-done | bytes 802848 | tf_op jit(solution)/shard_map/ppermute | solution.py:401
  28.9 0.5 collective-permute-start.16
  29.4 1.3 %collective-permute-done.9.refs_4_.refs_5_.refs_1_ = bf16[392,1024]{1,0:T(8,128)(2,1)S(1)} collective-permute-done((bf16[392,1024]{1,0:T(8,128)(2,1)S(1)}, bf16[392,1024]{1,0:T(8,128)(2,1)S(1)}, u32[]{:S(2)}, u32[]{:S(2)}) %collective-permute-start.9) | collective-permute-done | bytes 802848 | tf_op jit(solution)/shard_map/ppermute | solution.py:404
  30.7 1.7 %collective-permute-start.13 = (bf16[392,1024]{1,0:T(8,128)(2,1)S(1)}, bf16[392,1024]{1,0:T(8,128)(2,1)S(1)}, u32[]{:S(2)}, u32[]{:S(2)}) collective-permute-start(bf16[392,1024]{1,0:T(8,128)(2,1)S(1)} %collective-permute-done.12.refs_0_.refs_4_.refs_1_), channel_id=1, source_target_pairs={{1,0},{2,1},{3,2},{0,3},{5,4},{6,5},{7,6},{4,7},{9,8},{10,9},{11,1... | collective-permute-start | bytes 2408456 | tf_op jit(solution)/shard_map/ppermute | solution.py:407
  32.4 1.3 %collective-permute-start.15 = (bf16[392,1024]{1,0:T(8,128)(2,1)S(1)}, bf16[392,1024]{1,0:T(8,128)(2,1)S(1)}, u32[]{:S(2)}, u32[]{:S(2)}) collective-permute-start(bf16[392,1024]{1,0:T(8,128)(2,1)S(1)} %collective-permute-done.14.refs_3_.refs_7_), channel_id=1, source_target_pairs={{4,0},{5,1},{6,2},{7,3},{8,4},{9,5},{10,6},{11,7},{12,8},{13,9},{1... | collective-permute-start | bytes 2408456 | tf_op jit(solution)/shard_map/ppermute | solution.py:409
  33.7 5.7 %collective-permute-done.10.refs_6_.refs_5_.refs_2_ = bf16[392,1024]{1,0:T(8,128)(2,1)S(1)} collective-permute-done((bf16[392,1024]{1,0:T(8,128)(2,1)S(1)}, bf16[392,1024]{1,0:T(8,128)(2,1)S(1)}, u32[]{:S(2)}, u32[]{:S(2)}) %collective-permute-start.10) | collective-permute-done | bytes 802848 | tf_op jit(solution)/shard_map/ppermute | solution.py:406
  39.3 1.7 %collective-permute-start.8 = (bf16[392,1024]{1,0:T(8,128)(2,1)S(1)}, bf16[392,1024]{1,0:T(8,128)(2,1)S(1)}, u32[]{:S(2)}, u32[]{:S(2)}) collective-permute-start(bf16[392,1024]{1,0:T(8,128)(2,1)S(1)} %collective-permute-done.7.refs_0_.refs_2_), channel_id=1, source_target_pairs={{1,0},{2,1},{3,2},{0,3},{5,4},{6,5},{7,6},{4,7},{9,8},{10,9},{11,1... | collective-permute-start | bytes 2408456 | tf_op jit(solution)/shard_map/ppermute | solution.py:408
  41.0 2.5 %shard_map.40.refs_8_ = f32[6,8,768]{2,1,0:T(8,128)S(1)} custom-call(bf16[392,1024]{1,0:T(8,128)(2,1)S(1)} %collective-permute-done.12.refs_0_.refs_4_.refs_1_, bf16[392,1024]{1,0:T(8,128)(2,1)S(1)} %shard_map.38.refs_0_.refs_1_.refs_6_, bf16[392,1024]{1,0:T(8,128)(2,1)S(1)} %get-tuple-element.25.refs_2_.refs_7_.refs_3_, ...), custom_call_target="tpu_custom_call" | custom-call | flops 10871635968 | bytes 3932160 | tf_op jit(solution)/shard_map/pallas_call | solution.py:340
  43.5 5.2 %shard_map.41.refs_8_ = f32[6,8,768]{2,1,0:T(8,128)S(1)} custom-call(bf16[392,1024]{1,0:T(8,128)(2,1)S(1)} %collective-permute-done.7.refs_0_.refs_2_, bf16[392,1024]{1,0:T(8,128)(2,1)S(1)} %shard_map.38.refs_0_.refs_1_.refs_6_, bf16[392,1024]{1,0:T(8,128)(2,1)S(1)} %get-tuple-element.25.refs_2_.refs_7_.refs_3_, ...), custom_call_target="tpu_custom_call" | custom-call | flops 16911433728 | bytes 6291456 | tf_op jit(solution)/shard_map/pallas_call | solution.py:340
  48.8 2.6 %shard_map.42.refs_4_ = f32[6,8,768]{2,1,0:T(8,128)S(1)} custom-call(bf16[392,1024]{1,0:T(8,128)(2,1)S(1)} %collective-permute-done.15.refs_0_, bf16[392,1024]{1,0:T(8,128)(2,1)S(1)} %collective-permute-done.12.refs_0_.refs_4_.refs_1_, bf16[392,1024]{1,0:T(8,128)(2,1)S(1)} %collective-permute-done.7.refs_0_.refs_2_, ...), custom_call_target="tpu_custom_call" | custom-call | flops 8455716864 | bytes 6291456 | tf_op jit(solution)/shard_map/pallas_call | solution.py:340
  51.4 0.5 collective-permute-done.11.refs_0_.refs_4_
  51.8 1.3 %shard_map.43.refs_5_ = f32[6,8,768]{2,1,0:T(8,128)S(1)} custom-call(bf16[392,1024]{1,0:T(8,128)(2,1)S(1)} %collective-permute-done.11.refs_0_.refs_4_, bf16[392,1024]{1,0:T(8,128)(2,1)S(1)} %collective-permute-done.12.refs_0_.refs_4_.refs_1_, bf16[392,1024]{1,0:T(8,128)(2,1)S(1)} %collective-permute-done.7.refs_0_.refs_2_, ...), custom_call_target="tpu_custom_call" | custom-call | flops 3623878656 | bytes 3145728 | tf_op jit(solution)/shard_map/pallas_call | solution.py:340
  53.2 1.2 %collective-permute-done.8.refs_0_ = bf16[392,1024]{1,0:T(8,128)(2,1)S(1)} collective-permute-done((bf16[392,1024]{1,0:T(8,128)(2,1)S(1)}, bf16[392,1024]{1,0:T(8,128)(2,1)S(1)}, u32[]{:S(2)}, u32[]{:S(2)}) %collective-permute-start.8) | collective-permute-done | bytes 802848 | tf_op jit(solution)/shard_map/ppermute | solution.py:408
  54.4 1.7 %shard_map.44 = f32[128,128]{1,0:T(8,128)S(1)} custom-call(bf16[392,1024]{1,0:T(8,128)(2,1)S(1)} %collective-permute-done.8.refs_0_, bf16[392,1024]{1,0:T(8,128)(2,1)S(1)} %collective-permute-done.9.refs_4_.refs_5_.refs_1_, bf16[392,1024]{1,0:T(8,128)(2,1)S(1)} %collective-permute-done.10.refs_6_.refs_5_.refs_2_, ...), custom_call_target="tpu_custom_call" | custom-call | flops 4831838208 | bytes 3932160 | tf_op jit(solution)/shard_map/pallas_call | solution.py:340
  56.1 18.6 %all_to_all.11 = f32[128,1,128]{2,1,0:T(1,128)S(1)} all-to-all(f32[128,1,128]{2,1,0:T(1,128)S(1)} %bitcast.5), channel_id=1, replica_groups=mesh['clus'=8,'fold'=16] {'clus','fold'}, dimensions={0} | all-to-all | bytes 131072 | tf_op jit(solution)/shard_map/all_to_all | solution.py:459
  74.6 0.9 %shard_map.45 = f32[768]{0:T(1024)} custom-call(s32[1,768]{1,0:T(1,128)S(1)} %get-tuple-element.16.slot_ref, f32[128,128]{1,0:T(8,128)S(1)} %bitcast.4), custom_call_target="tpu_custom_call" | custom-call | tf_op jit(solution)/shard_map/pallas_call | solution.py:379
  (12 shorter events, 0.1 us)
Async XLA Ops:
  3.1 7.7 %collective-permute-start = (bf16[104,1024]{1,0:T(8,128)(2,1)S(1)}, bf16[104,1024]{1,0:T(8,128)(2,1)S(1)}, u32[]{:S(2)}, u32[]{:S(2)}) collective-permute-start(bf16[104,1024]{1,0:T(8,128)(2,1)S(1)} %get-tuple-element.18), channel_id=1, source_target_pairs={{0,16},{1,17},{2,18},{3,19},{4,20},{5,21},{6,22},{7,23},{8,24},{9,... | collective-permute-start | bytes 638984 | tf_op jit(solution)/shard_map/ppermute | solution.py:397
  4.6 7.6 %collective-permute-start.1 = (bf16[104,1024]{1,0:T(8,128)(2,1)S(1)}, bf16[104,1024]{1,0:T(8,128)(2,1)S(1)}, u32[]{:S(2)}, u32[]{:S(2)}) collective-permute-start(bf16[104,1024]{1,0:T(8,128)(2,1)S(1)} %get-tuple-element.19), channel_id=1, source_target_pairs={{0,32},{1,33},{2,34},{3,35},{4,36},{5,37},{6,38},{7,39},{8,40},{9,... | collective-permute-start | bytes 638984 | tf_op jit(solution)/shard_map/ppermute | solution.py:397
  5.9 9.1 %collective-permute-start.2 = (bf16[104,1024]{1,0:T(8,128)(2,1)S(1)}, bf16[104,1024]{1,0:T(8,128)(2,1)S(1)}, u32[]{:S(2)}, u32[]{:S(2)}) collective-permute-start(bf16[104,1024]{1,0:T(8,128)(2,1)S(1)} %get-tuple-element.20), channel_id=1, source_target_pairs={{0,20},{1,21},{2,22},{3,23},{4,24},{5,25},{6,26},{7,27},{8,28},{9,... | collective-permute-start | bytes 638984 | tf_op jit(solution)/shard_map/ppermute | solution.py:397
  7.3 10.9 %collective-permute-start.3 = (bf16[104,1024]{1,0:T(8,128)(2,1)S(1)}, bf16[104,1024]{1,0:T(8,128)(2,1)S(1)}, u32[]{:S(2)}, u32[]{:S(2)}) collective-permute-start(bf16[104,1024]{1,0:T(8,128)(2,1)S(1)} %get-tuple-element.21), channel_id=1, source_target_pairs={{0,64},{1,65},{2,66},{3,67},{4,68},{5,69},{6,70},{7,71},{8,72},{9,... | collective-permute-start | bytes 638984 | tf_op jit(solution)/shard_map/ppermute | solution.py:397
  10.2 8.9 %collective-permute-start.4 = (bf16[104,1024]{1,0:T(8,128)(2,1)S(1)}, bf16[104,1024]{1,0:T(8,128)(2,1)S(1)}, u32[]{:S(2)}, u32[]{:S(2)}) collective-permute-start(bf16[104,1024]{1,0:T(8,128)(2,1)S(1)} %get-tuple-element.22), channel_id=1, source_target_pairs={{0,24},{1,25},{2,26},{3,27},{4,28},{5,29},{6,30},{7,31},{8,16},{9,... | collective-permute-start | bytes 638984 | tf_op jit(solution)/shard_map/ppermute | solution.py:397
  10.8 10.4 %collective-permute-start.5 = (bf16[104,1024]{1,0:T(8,128)(2,1)S(1)}, bf16[104,1024]{1,0:T(8,128)(2,1)S(1)}, u32[]{:S(2)}, u32[]{:S(2)}) collective-permute-start(bf16[104,1024]{1,0:T(8,128)(2,1)S(1)} %get-tuple-element.23), channel_id=1, source_target_pairs={{0,96},{1,97},{2,98},{3,99},{4,100},{5,101},{6,102},{7,103},{8,104... | collective-permute-start | bytes 638984 | tf_op jit(solution)/shard_map/ppermute | solution.py:397
  12.2 9.0 %collective-permute-start.6 = (bf16[104,1024]{1,0:T(8,128)(2,1)S(1)}, bf16[104,1024]{1,0:T(8,128)(2,1)S(1)}, u32[]{:S(2)}, u32[]{:S(2)}) collective-permute-start(bf16[104,1024]{1,0:T(8,128)(2,1)S(1)} %get-tuple-element.24), channel_id=1, source_target_pairs={{0,28},{1,29},{2,30},{3,31},{4,16},{5,17},{6,18},{7,19},{8,20},{9,... | collective-permute-start | bytes 638984 | tf_op jit(solution)/shard_map/ppermute | solution.py:397
  15.1 13.7 %collective-permute-start.12 = (bf16[392,1024]{1,0:T(8,128)(2,1)S(1)}, bf16[392,1024]{1,0:T(8,128)(2,1)S(1)}, u32[]{:S(2)}, u32[]{:S(2)}) collective-permute-start(bf16[392,1024]{1,0:T(8,128)(2,1)S(1)} %shard_map.38.refs_0_.refs_1_.refs_6_), channel_id=1, source_target_pairs={{1,0},{2,1},{3,2},{0,3},{5,4},{6,5},{7,6},{4,7},{9,8},{10,9},{11,1... | collective-permute-start | bytes 2408456 | tf_op jit(solution)/shard_map/ppermute | solution.py:401
  18.2 12.5 %collective-permute-start.9 = (bf16[392,1024]{1,0:T(8,128)(2,1)S(1)}, bf16[392,1024]{1,0:T(8,128)(2,1)S(1)}, u32[]{:S(2)}, u32[]{:S(2)}) collective-permute-start(bf16[392,1024]{1,0:T(8,128)(2,1)S(1)} %shard_map.38.refs_0_.refs_1_.refs_6_), channel_id=1, source_target_pairs={{12,0},{13,1},{14,2},{15,3},{0,4},{1,5},{2,6},{3,7},{4,8},{5,9},{6... | collective-permute-start | bytes 2408456 | tf_op jit(solution)/shard_map/ppermute | solution.py:404
  19.1 13.2 %collective-permute-start.14 = (bf16[392,1024]{1,0:T(8,128)(2,1)S(1)}, bf16[392,1024]{1,0:T(8,128)(2,1)S(1)}, u32[]{:S(2)}, u32[]{:S(2)}) collective-permute-start(bf16[392,1024]{1,0:T(8,128)(2,1)S(1)} %shard_map.38.refs_0_.refs_1_.refs_6_), channel_id=1, source_target_pairs={{4,0},{5,1},{6,2},{7,3},{8,4},{9,5},{10,6},{11,7},{12,8},{13,9},{1... | collective-permute-start | bytes 2408456 | tf_op jit(solution)/shard_map/ppermute | solution.py:403
  22.3 17.0 %collective-permute-start.10 = (bf16[392,1024]{1,0:T(8,128)(2,1)S(1)}, bf16[392,1024]{1,0:T(8,128)(2,1)S(1)}, u32[]{:S(2)}, u32[]{:S(2)}) collective-permute-start(bf16[392,1024]{1,0:T(8,128)(2,1)S(1)} %get-tuple-element.25.refs_2_.refs_7_.refs_3_), channel_id=1, source_target_pairs={{12,0},{13,1},{14,2},{15,3},{0,4},{1,5},{2,6},{3,7},{4,8},{5,9},{6... | collective-permute-start | bytes 2408456 | tf_op jit(solution)/shard_map/ppermute | solution.py:406
  23.2 16.2 %collective-permute-start.7 = (bf16[392,1024]{1,0:T(8,128)(2,1)S(1)}, bf16[392,1024]{1,0:T(8,128)(2,1)S(1)}, u32[]{:S(2)}, u32[]{:S(2)}) collective-permute-start(bf16[392,1024]{1,0:T(8,128)(2,1)S(1)} %get-tuple-element.25.refs_2_.refs_7_.refs_3_), channel_id=1, source_target_pairs={{1,0},{2,1},{3,2},{0,3},{5,4},{6,5},{7,6},{4,7},{9,8},{10,9},{11,1... | collective-permute-start | bytes 2408456 | tf_op jit(solution)/shard_map/ppermute | solution.py:402
  28.9 14.6 %collective-permute-start.16 = (bf16[392,1024]{1,0:T(8,128)(2,1)S(1)}, bf16[392,1024]{1,0:T(8,128)(2,1)S(1)}, u32[]{:S(2)}, u32[]{:S(2)}) collective-permute-start(bf16[392,1024]{1,0:T(8,128)(2,1)S(1)} %get-tuple-element.25.refs_2_.refs_7_.refs_3_), channel_id=1, source_target_pairs={{4,0},{5,1},{6,2},{7,3},{8,4},{9,5},{10,6},{11,7},{12,8},{13,9},{1... | collective-permute-start | bytes 2408456 | tf_op jit(solution)/shard_map/ppermute | solution.py:405
  30.7 18.0 %collective-permute-start.13 = (bf16[392,1024]{1,0:T(8,128)(2,1)S(1)}, bf16[392,1024]{1,0:T(8,128)(2,1)S(1)}, u32[]{:S(2)}, u32[]{:S(2)}) collective-permute-start(bf16[392,1024]{1,0:T(8,128)(2,1)S(1)} %collective-permute-done.12.refs_0_.refs_4_.refs_1_), channel_id=1, source_target_pairs={{1,0},{2,1},{3,2},{0,3},{5,4},{6,5},{7,6},{4,7},{9,8},{10,9},{11,1... | collective-permute-start | bytes 2408456 | tf_op jit(solution)/shard_map/ppermute | solution.py:407
  32.4 16.4 %collective-permute-start.15 = (bf16[392,1024]{1,0:T(8,128)(2,1)S(1)}, bf16[392,1024]{1,0:T(8,128)(2,1)S(1)}, u32[]{:S(2)}, u32[]{:S(2)}) collective-permute-start(bf16[392,1024]{1,0:T(8,128)(2,1)S(1)} %collective-permute-done.14.refs_3_.refs_7_), channel_id=1, source_target_pairs={{4,0},{5,1},{6,2},{7,3},{8,4},{9,5},{10,6},{11,7},{12,8},{13,9},{1... | collective-permute-start | bytes 2408456 | tf_op jit(solution)/shard_map/ppermute | solution.py:409
  39.3 12.5 %collective-permute-start.11 = (bf16[392,1024]{1,0:T(8,128)(2,1)S(1)}, bf16[392,1024]{1,0:T(8,128)(2,1)S(1)}, u32[]{:S(2)}, u32[]{:S(2)}) collective-permute-start(bf16[392,1024]{1,0:T(8,128)(2,1)S(1)} %collective-permute-done.10.refs_6_.refs_5_.refs_2_), channel_id=1, source_target_pairs={{12,0},{13,1},{14,2},{15,3},{0,4},{1,5},{2,6},{3,7},{4,8},{5,9},{6... | collective-permute-start | bytes 2408456 | tf_op jit(solution)/shard_map/ppermute | solution.py:410
  39.3 15.1 %collective-permute-start.8 = (bf16[392,1024]{1,0:T(8,128)(2,1)S(1)}, bf16[392,1024]{1,0:T(8,128)(2,1)S(1)}, u32[]{:S(2)}, u32[]{:S(2)}) collective-permute-start(bf16[392,1024]{1,0:T(8,128)(2,1)S(1)} %collective-permute-done.7.refs_0_.refs_2_), channel_id=1, source_target_pairs={{1,0},{2,1},{3,2},{0,3},{5,4},{6,5},{7,6},{4,7},{9,8},{10,9},{11,1... | collective-permute-start | bytes 2408456 | tf_op jit(solution)/shard_map/ppermute | solution.py:408
